TPU v7x, 128 devices: a whole 4x4x4 slice. The times are simulated.
128 devices in a mesh: leaf: 128 (over y, z, x, core).
Axes of the slice: x: 4, y: 4, z: 4, core: 2. Of those that a mesh axis runs over, the one named last changes fastest.
Arguments:
- points: bfloat16 [64, 131072], P(None, 'leaf'), may hold values from -6 to 6
- weights: bfloat16 [131072, 512], P('leaf'), may hold values from -1.1953125 to 1.1953125
- interp: bfloat16 [131072, 512], P('leaf'), may hold values from -0.1875 to 0.1875
- transfers: bfloat16 [128, 5, 512, 512], P('leaf'), may hold values from -0.25 to 0.25
- near_mask: int32 [128, 4], P('leaf'), may hold values 0 or 1
- skel_index: int32 [128, 512], P('leaf'), may hold values from 0 to 1023, as said below
Outputs:
- product: bfloat16 [131072, 512], P('leaf')
Inputs may be any that keep to these rules, and one draw needn't show every extreme that they name: `skel_index`: each row holds 512 distinct ranks.
All inputs are finite; a program needn't handle non-finite values. No bound on the sum of `near_mask` on one device may be relied on, other than what follows from the above.
Results may differ from a plain program's by a relative error of at most 0.0075.
Values may be sent and summed in bfloat16 or wider, within the bound.
No kernel may reach another device: no remote copies, remote signals or barrier semaphores. Data moves between devices by JAX's collectives and lax.ppermute only.
A program may use at most 128 MiB of HBM per device.

v0:
```python
import jax
import jax.numpy as jnp
from jax import lax
from jax.sharding import PartitionSpec as P


def passed_along(value, axis, steps):
    count = lax.axis_size(axis)
    leading, last = (max(0, -steps), min(count, count - steps))
    return lax.ppermute(value, axis, [(source, source + steps) for source in range(leading, last)])


def from_partner(value, axis, apart):
    mask = 2**apart
    pairs = [(source, source ^ mask) for source in range(lax.axis_size(axis))]
    return lax.ppermute(value, axis, pairs)


def kernel_tile(left, right):
    left_wide = left.astype(jnp.float32)
    right_wide = right.astype(jnp.float32)
    sq_left = jnp.sum(left_wide * left_wide, axis=0)
    sq_right = jnp.sum(right_wide * right_wide, axis=0)
    cross_terms = lax.dot_general(
        left, right, (((0,), (0,)), ((), ())), preferred_element_type=jnp.float32
    )
    distance = sq_left[:, None] + sq_right[None, :] - 2.0 * cross_terms
    return jnp.exp(distance * (-1.0 / left.shape[0])).astype(jnp.bfloat16)


def join_points(own_part, partner_part, upper_half):
    first_part = jnp.where(upper_half == 1, partner_part, own_part)
    second_part = jnp.where(upper_half == 1, own_part, partner_part)
    return jnp.concatenate([first_part, second_part], axis=1)


def coupled_block(own_nodes, sibling_nodes, sibling_sums):
    tile = kernel_tile(own_nodes.astype(jnp.bfloat16), sibling_nodes.astype(jnp.bfloat16))
    return jnp.dot(
        tile, sibling_sums.astype(jnp.bfloat16), preferred_element_type=jnp.float32
    ).astype(jnp.bfloat16)


def couple_level(own_nodes, sibling_nodes, sibling_sums, transfer):
    coupled = coupled_block(own_nodes, sibling_nodes, sibling_sums)
    return jnp.dot(transfer, coupled, preferred_element_type=jnp.float32)


def per_device(points, weights, interp, transfers, near_mask, skel_index):
    leaves = lax.axis_size("leaf")
    leaf_index = lax.axis_index("leaf")
    radius = near_mask.shape[1] // 2
    offsets = list(range(-radius, 0)) + list(range(1, radius + 1))
    near_field = jnp.dot(kernel_tile(points, points), weights, preferred_element_type=jnp.float32)
    blocks_by_offset = {}
    for offset in offsets:
        blocks_by_offset[offset] = passed_along((points, weights), "leaf", -offset)
    for slot_index, offset in enumerate(offsets):
        other_points, other_weights = blocks_by_offset[offset]
        target = leaf_index + offset
        in_range = (target >= 0) & (target < leaves)
        flag_value = jnp.where(in_range, near_mask[0, slot_index], 0).astype(jnp.float32)
        block = jnp.dot(
            kernel_tile(points, other_points), other_weights, preferred_element_type=jnp.float32
        )
        near_field = near_field + flag_value * block
    width = skel_index.shape[1]
    levels = transfers.shape[1]
    skel_points = jnp.take(points, skel_index[0], axis=1).astype(jnp.float32)
    leaf_weights = lax.dot_general(
        interp, weights, (((0,), (0,)), ((), ())), preferred_element_type=jnp.float32
    ).astype(jnp.bfloat16)
    level_terms = jnp.einsum(
        "lab,ac->lbc", transfers[0], leaf_weights, preferred_element_type=jnp.float32
    )
    far_sum = jnp.zeros((width, weights.shape[1]), jnp.float32)
    for level in range(levels):
        node_sum = level_terms[level]
        node_cols = skel_points[:, : width >> level]
        for bit_level in range(level):
            upper_half = leaf_index >> bit_level & 1
            partner_sum, partner_cols = from_partner((node_sum, node_cols), "leaf", bit_level)
            node_sum = node_sum + partner_sum
            node_cols = join_points(node_cols, partner_cols, upper_half)
        sibling_sum, sibling_cols = (
            from_partner(node_sum.astype(jnp.bfloat16), "leaf", level).astype(node_sum.dtype),
            from_partner(node_cols.astype(jnp.bfloat16), "leaf", level).astype(node_cols.dtype),
        )
        far_sum = far_sum + couple_level(node_cols, sibling_cols, sibling_sum, transfers[0, level])
    far_skeleton = far_sum.astype(jnp.bfloat16)
    far_field = jnp.dot(interp, far_skeleton, preferred_element_type=jnp.float32)
    return (near_field + far_field).astype(jnp.bfloat16)


def solution(mesh):
    return jax.shard_map(
        per_device,
        mesh=mesh,
        in_specs=(
            P(None, "leaf"),
            P("leaf", None),
            P("leaf", None),
            P("leaf", None, None, None),
            P("leaf", None),
            P("leaf", None),
        ),
        out_specs=P("leaf", None),
        check_vma=False,
    )
```

profile of v0, /device:TPU:26, one launch (start us, length us, event | category | flops | bytes accessed | tf_op | source)
XLA Modules:
  0.0 293.0 jit_solution(4457440033261373353)
XLA Ops:
  0.0 1.2 copy.9
  2.6 1.3 gather_fusion
  5.2 6.4 %fusion.2 = f32[5,512,512]{1,2,0:T(8,128)} fusion(bf16[1,5,512,512]{3,2,1,0:T(8,128)(2,1)} %param.9, bf16[1024,512]{1,0:T(8,128)(2,1)S(1)} %copy-done, bf16[1024,512]{1,0:T(8,128)(2,1)} %param.7), kind=kOutput, calls=%fused_computation.8 | convolution fusion | flops 1879310336 | bytes 9961472 | tf_op jit(solution)/shard_map/lab,ac->lbc/dot_general | solution.py:73
  11.7 4.3 %slice_bitcast_fusion = (f32[512,512]{0,1:T(8,128)}, f32[512,512]{0,1:T(8,128)}, f32[512,512]{0,1:T(8,128)}, f32[512,512]{0,1:T(8,128)}) fusion(f32[5,512,512]{1,2,0:T(8,128)} %fusion.2), kind=kLoop, calls=%fused_computation.34 | loop fusion | bytes 8388608 | tf_op jit(solution)/shard_map/squeeze | solution.py:78
  16.5 2.1 fusion.14
  18.6 4.6 %fusion.10 = f32[1024,512]{1,0:T(8,128)} fusion(bf16[1024,512]{1,0:T(8,128)(2,1)} %param.7, bf16[64,1024]{1,0:T(8,128)(2,1)S(1)} %copy-done.5, f32[1024]{0:T(1024)S(1)} %multiply_reduce_fusion.14), kind=kOutput, calls=%fused_computation.30 | convolution fusion | flops 1213202432 | bytes 3280896 | tf_op jit(solution)/shard_map/dot_general | solution.py:54
  28.3 3.2 %collective-permute-done.29 = bf16[64,64]{0,1:T(8,128)(2,1)S(1)} collective-permute-done((bf16[64,64]{0,1:T(8,128)(2,1)S(1)}, bf16[64,64]{0,1:T(8,128)(2,1)S(1)}, u32[]{:S(2)}, u32[]{:S(2)}) %collective-permute-start.29) | collective-permute-done | bytes 8224 | tf_op jit(solution)/shard_map/ppermute | solution.py:16
  31.5 1.2 collective-permute-done.14
  33.3 3.3 %collective-permute-done.21 = bf16[64,128]{0,1:T(8,128)(2,1)S(1)} collective-permute-done((bf16[64,128]{0,1:T(8,128)(2,1)S(1)}, bf16[64,128]{0,1:T(8,128)(2,1)S(1)}, u32[]{:S(2)}, u32[]{:S(2)}) %collective-permute-start.21) | collective-permute-done | bytes 16416 | tf_op jit(solution)/shard_map/ppermute | solution.py:16
  36.6 2.1 collective-permute-start.30
  38.8 3.3 %collective-permute-done.30 = bf16[64,128]{0,1:T(8,128)(2,1)S(1)} collective-permute-done((bf16[64,128]{0,1:T(8,128)(2,1)S(1)}, bf16[64,128]{0,1:T(8,128)(2,1)S(1)}, u32[]{:S(2)}, u32[]{:S(2)}) %collective-permute-start.30) | collective-permute-done | bytes 16416 | tf_op jit(solution)/shard_map/ppermute | solution.py:16
  42.1 1.2 collective-permute-done.10
  44.6 3.0 %collective-permute-done.15 = bf16[64,256]{0,1:T(8,128)(2,1)S(1)} collective-permute-done((bf16[64,256]{0,1:T(8,128)(2,1)S(1)}, bf16[64,256]{0,1:T(8,128)(2,1)S(1)}, u32[]{:S(2)}, u32[]{:S(2)}) %collective-permute-start.15) | collective-permute-done | bytes 32800 | tf_op jit(solution)/shard_map/ppermute | solution.py:16
  47.6 2.1 collective-permute-start.22
  50.5 2.9 collective-permute-done.22
  53.3 1.9 collective-permute-start.31
  56.1 1.6 collective-permute-done.31
  59.0 1.3 convolution_multiply_fusion.4
  61.0 3.3 %collective-permute-done.11 = bf16[64,512]{0,1:T(8,128)(2,1)S(1)} collective-permute-done((bf16[64,512]{0,1:T(8,128)(2,1)S(1)}, bf16[64,512]{0,1:T(8,128)(2,1)S(1)}, u32[]{:S(2)}, u32[]{:S(2)}) %collective-permute-start.11) | collective-permute-done | bytes 65568 | tf_op jit(solution)/shard_map/ppermute | solution.py:16
  64.3 2.1 collective-permute-start.16
  66.5 1.3 convolution_multiply_fusion.3
  68.5 2.5 collective-permute-done.16
  71.0 3.4 %collective-permute-start = (bf16[64,1024]{1,0:T(8,128)(2,1)S(1)}, bf16[64,1024]{1,0:T(8,128)(2,1)S(1)}, u32[]{:S(2)}, u32[]{:S(2)}) collective-permute-start(bf16[64,1024]{1,0:T(8,128)(2,1)S(1)} %copy-done.5), channel_id=1, source_target_pairs={{0,2},{1,3},{2,4},{3,5},{4,6},{5,7},{6,8},{7,9},{8,10},{9,11},{10,... | collective-permute-start | bytes 393224 | tf_op jit(solution)/shard_map/ppermute | solution.py:10
  74.4 1.3 convolution_multiply_fusion.2
  75.7 3.2 %collective-permute-start.1 = (bf16[1024,512]{1,0:T(8,128)(2,1)}, bf16[1024,512]{1,0:T(8,128)(2,1)}, u32[]{:S(2)}, u32[]{:S(2)}) collective-permute-start(bf16[1024,512]{1,0:T(8,128)(2,1)} %param.7), channel_id=1, source_target_pairs={{0,2},{1,3},{2,4},{3,5},{4,6},{5,7},{6,8},{7,9},{8,10},{9,11},{10,... | collective-permute-start | bytes 3145736 | tf_op jit(solution)/shard_map/ppermute | solution.py:10
  78.9 1.9 collective-permute-start.2
  80.9 2.2 collective-permute-start.23
  83.0 5.0 %fusion.79 = (f32[512,512]{0,1:T(8,128)S(1)}, f32[512,512]{0,1:T(8,128)S(1)}, f32[512,512]{0,1:T(8,128)}, bf16[512,512]{0,1:T(8,128)(2,1)}) fusion(f32[512,512]{0,1:T(8,128)S(1)} %collective-permute-done.33, f32[5,512,512]{1,2,0:T(8,128)} %fusion.2, f32[512,512]{0,1:T(8,128)} %collective-permute-done.24, f32[512,512]{0,1:T(8,128)} %collective-permute-done.17, ...), kind=kLoop, calls=%fused_computation.145 | loop fusion | flops 1310720 | bytes 12058624 | tf_op jit(solution)/shard_map/add | solution.py:83
  89.6 3.6 %collective-permute-start.32 = (bf16[64,512]{0,1:T(8,128)(2,1)S(1)}, bf16[64,512]{0,1:T(8,128)(2,1)S(1)}, u32[]{:S(2)}, u32[]{:S(2)}) collective-permute-start(bf16[64,512]{0,1:T(8,128)(2,1)S(1)} %pad_maximum_fusion.6), channel_id=1, source_target_pairs={{0,16},{1,17},{2,18},{3,19},{4,20},{5,21},{6,22},{7,23},{8,24},{9,... | collective-permute-start | bytes 196616 | tf_op jit(solution)/shard_map/ppermute | solution.py:16
  93.1 1.3 convolution_multiply_fusion.1
  95.2 2.3 collective-permute-done.32
  97.4 19.0 %collective-permute-start.4 = (bf16[64,1024]{1,0:T(8,128)(2,1)S(1)}, bf16[64,1024]{1,0:T(8,128)(2,1)S(1)}, u32[]{:S(2)}, u32[]{:S(2)}) collective-permute-start(bf16[64,1024]{1,0:T(8,128)(2,1)S(1)} %copy-done.5), channel_id=1, source_target_pairs={{1,0},{2,1},{3,2},{4,3},{5,4},{6,5},{7,6},{8,7},{9,8},{10,9},{11,1... | collective-permute-start | bytes 393224 | tf_op jit(solution)/shard_map/ppermute | solution.py:10
  116.4 2.6 collective-permute-start.6
  120.8 2.2 collective-permute-start.3
  123.3 1.7 collective-permute-start.25
  125.4 2.0 collective-permute-start.5
  127.6 3.6 %collective-permute-start.35 = (f32[512,512]{0,1:T(8,128)S(1)}, f32[512,512]{0,1:T(8,128)}, u32[]{:S(2)}, u32[]{:S(2)}) collective-permute-start(f32[512,512]{0,1:T(8,128)S(1)} %add.266), channel_id=1, source_target_pairs={{0,4},{1,5},{2,6},{3,7},{4,0},{5,1},{6,2},{7,3},{8,12},{9,13},{10,... | collective-permute-start | bytes 3145736 | tf_op jit(solution)/shard_map/ppermute | solution.py:16
  131.2 3.4 %fusion.8 = f32[512,512]{1,0:T(8,128)} fusion(bf16[512,512]{0,1:T(8,128)(2,1)} %copy-done.16, f32[512,512]{1,0:T(8,128)} %convolution_multiply_fusion.4, bf16[1,5,512,512]{3,2,1,0:T(8,128)(2,1)} %param.9, f32[512]{0:T(512)} %multiply_reduce_fusion.8, f32[512]{0:T(512)} %get-tuple-element.5), kind=kOutput, calls=%fused_computation.28 | convolution fusion | flops 538181632 | bytes 3149824 | tf_op jit(solution)/shard_map/dot_general | solution.py:46
  134.6 1.8 collective-permute-start.13
  136.4 4.7 %fusion.11 = f32[1024,512]{1,0:T(8,128)} fusion(bf16[1024,512]{1,0:T(8,128)(2,1)} %collective-permute-done.1, bf16[64,1024]{1,0:T(8,128)(2,1)S(1)} %copy-done.5, bf16[64,1024]{1,0:T(8,128)(2,1)} %copy-done.9, f32[1024]{0:T(1024)} %multiply_reduce_fusion.13, f32[1024]{0:T(1024)S(1)} %multiply_reduce_fusion.14), kind=kOutput, calls=%fused_computation.31 | convolution fusion | flops 1213202432 | bytes 3416064 | tf_op jit(solution)/shard_map/dot_general | solution.py:63
  141.1 8.3 %collective-permute-done.25 = f32[512,512]{0,1:T(8,128)} collective-permute-done((f32[512,512]{0,1:T(8,128)S(1)}, f32[512,512]{0,1:T(8,128)}, u32[]{:S(2)}, u32[]{:S(2)}) %collective-permute-start.25) | collective-permute-done | bytes 1048608 | tf_op jit(solution)/shard_map/ppermute | solution.py:16
  149.4 1.7 collective-permute-start.18
  151.1 2.4 add.259
  153.5 2.0 collective-permute-start.26
  155.4 4.7 %fusion.12 = f32[1024,512]{1,0:T(8,128)} fusion(bf16[1024,512]{1,0:T(8,128)(2,1)} %collective-permute-done.3, bf16[64,1024]{1,0:T(8,128)(2,1)S(1)} %copy-done.5, bf16[64,1024]{1,0:T(8,128)(2,1)} %copy-done.8, f32[1024]{0:T(1024)S(1)} %multiply_reduce_fusion.12, f32[1024]{0:T(1024)S(1)} %multiply_reduce_fusion.14), kind=kOutput, calls=%fused_computation.32 | convolution fusion | flops 1213202432 | bytes 3416064 | tf_op jit(solution)/shard_map/dot_general | solution.py:63
  160.1 35.7 %collective-permute-done.35 = f32[512,512]{0,1:T(8,128)} collective-permute-done((f32[512,512]{0,1:T(8,128)S(1)}, f32[512,512]{0,1:T(8,128)}, u32[]{:S(2)}, u32[]{:S(2)}) %collective-permute-start.35) | collective-permute-done | bytes 1048608 | tf_op jit(solution)/shard_map/ppermute | solution.py:16
  195.8 1.9 collective-permute-start.7
  197.8 2.4 add.267
  200.2 1.4 collective-permute-start.36
  201.6 4.5 %fusion.13 = f32[1024,512]{1,0:T(8,128)} fusion(bf16[1024,512]{1,0:T(8,128)(2,1)} %collective-permute-done.5, bf16[64,1024]{1,0:T(8,128)(2,1)S(1)} %copy-done.5, bf16[64,1024]{1,0:T(8,128)(2,1)S(1)} %copy-done.11, f32[1024]{0:T(1024)S(1)} %multiply_reduce_fusion.11, f32[1024]{0:T(1024)S(1)} %multiply_reduce_fusion.14), kind=kOutput, calls=%fused_computation.33 | convolution fusion | flops 1213202432 | bytes 3416064 | tf_op jit(solution)/shard_map/dot_general | solution.py:63
  206.2 3.5 %convolution_add_fusion.3 = f32[512,512]{1,0:T(8,128)} fusion(f32[512,512]{1,0:T(8,128)} %fusion.8, bf16[512,512]{0,1:T(8,128)(2,1)} %collective-permute-done.13, f32[512,512]{1,0:T(8,128)S(1)} %copy-done.3, bf16[1,5,512,512]{3,2,1,0:T(8,128)(2,1)} %param.9, f32[512]{0:T(512)} %multiply_reduce_fusion.6, f32[512]{0:T(512)S(1)} %copy-done.15), kind=kOutput, calls=%fused_computation.17 | convolution fusion | flops 538443776 | bytes 4198400 | tf_op jit(solution)/shard_map/dot_general | solution.py:46
  209.7 17.6 %collective-permute-done.18 = f32[512,512]{0,1:T(8,128)} collective-permute-done((f32[512,512]{0,1:T(8,128)}, f32[512,512]{0,1:T(8,128)}, u32[]{:S(2)}, u32[]{:S(2)}) %collective-permute-start.18) | collective-permute-done | bytes 1048608 | tf_op jit(solution)/shard_map/ppermute | solution.py:16
  227.2 1.4 add_convert_fusion.2
  228.6 1.9 collective-permute-start.19
  230.6 21.5 %collective-permute-done.26 = f32[512,512]{0,1:T(8,128)} collective-permute-done((f32[512,512]{0,1:T(8,128)}, f32[512,512]{0,1:T(8,128)}, u32[]{:S(2)}, u32[]{:S(2)}) %collective-permute-start.26) | collective-permute-done | bytes 1048608 | tf_op jit(solution)/shard_map/ppermute | solution.py:16
  252.0 2.5 add_convert_fusion.1
  255.6 2.5 add_convert_fusion
  258.1 3.3 %collective-permute-start.37 = (bf16[512,512]{0,1:T(8,128)(2,1)}, bf16[512,512]{0,1:T(8,128)(2,1)}, u32[]{:S(2)}, u32[]{:S(2)}) collective-permute-start(bf16[512,512]{0,1:T(8,128)(2,1)} %add_convert_fusion), channel_id=1, source_target_pairs={{0,16},{1,17},{2,18},{3,19},{4,20},{5,21},{6,22},{7,23},{8,24},{9,... | collective-permute-start | bytes 1572872 | tf_op jit(solution)/shard_map/ppermute | solution.py:16
  261.4 12.4 %collective-permute-done.19 = bf16[512,512]{0,1:T(8,128)(2,1)} collective-permute-done((bf16[512,512]{0,1:T(8,128)(2,1)S(1)}, bf16[512,512]{0,1:T(8,128)(2,1)}, u32[]{:S(2)}, u32[]{:S(2)}) %collective-permute-start.19) | collective-permute-done | bytes 524320 | tf_op jit(solution)/shard_map/ppermute | solution.py:16
  273.8 3.4 %convolution_add_fusion.2 = f32[512,512]{1,0:T(8,128)} fusion(f32[512,512]{1,0:T(8,128)} %convolution_add_fusion.3, bf16[512,512]{0,1:T(8,128)(2,1)} %collective-permute-done.19, f32[512,512]{1,0:T(8,128)S(1)} %copy-done.2, bf16[1,5,512,512]{3,2,1,0:T(8,128)(2,1)} %param.9, f32[512]{0:T(512)} %multiply_reduce_fusion.4, f32[512]{0:T(512)S(1)} %copy-done.13), kind=kOutput, calls=%fused_computation.15 | convolution fusion | flops 538443776 | bytes 4198400 | tf_op jit(solution)/shard_map/dot_general | solution.py:46
  277.3 3.4 %convolution_add_fusion.1 = f32[512,512]{1,0:T(8,128)} fusion(f32[512,512]{1,0:T(8,128)} %convolution_add_fusion.2, bf16[512,512]{0,1:T(8,128)(2,1)} %collective-permute-done.27, f32[512,512]{1,0:T(8,128)S(1)} %copy-done.4, bf16[1,5,512,512]{3,2,1,0:T(8,128)(2,1)} %param.9, f32[512]{0:T(512)} %multiply_reduce_fusion.2, f32[512]{0:T(512)S(1)} %copy-done.14), kind=kOutput, calls=%fused_computation.13 | convolution fusion | flops 538443776 | bytes 4198400 | tf_op jit(solution)/shard_map/dot_general | solution.py:46
  280.7 2.5 convolution_convert_fusion
  283.2 2.7 fusion.9
  285.9 7.1 %fusion.5 = bf16[1024,512]{1,0:T(8,128)(2,1)} fusion(f32[512,1024]{0,1:T(8,128)S(1)} %fusion.9, f32[1024,512]{1,0:T(8,128)} %fusion.13, f32[1024,512]{1,0:T(8,128)} %fusion.12, f32[1024,512]{1,0:T(8,128)} %fusion.10, f32[1024,512]{1,0:T(8,128)} %fusion.11, bf16[1024,512]{1,0:T(8,128)(2,1)} %collective-permute-done.7, bf16[64,1024]{1,0:T(8,128)(2,1)S(1)} %copy-done.5, ...), kind=kOutput, calls=%fused_computation.10 | convolution fusion | flops 1218445312 | bytes 12853264 | tf_op jit(solution)/shard_map/dot_general | solution.py:63
  (116 shorter events, 18.4 us)
Async XLA Ops:
  0.0 5.2 %copy-start = (bf16[1024,512]{1,0:T(8,128)(2,1)S(1)}, bf16[1024,512]{1,0:T(8,128)(2,1)}, u32[]{:S(2)}) copy-start(bf16[1024,512]{1,0:T(8,128)(2,1)} %param.8) | copy-start | bytes 3145732
  4.7 53.7 %collective-permute-start.8 = (bf16[64,512]{0,1:T(8,128)(2,1)S(1)}, bf16[64,512]{0,1:T(8,128)(2,1)S(1)}, u32[]{:S(2)}, u32[]{:S(2)}) collective-permute-start(bf16[64,512]{0,1:T(8,128)(2,1)S(1)} %get-tuple-element.6), channel_id=1, source_target_pairs={{0,1},{1,0},{2,3},{3,2},{4,5},{5,4},{6,7},{7,6},{8,9},{9,8},{10,11... | collective-permute-start | bytes 196616 | tf_op jit(solution)/shard_map/ppermute | solution.py:16
  4.7 21.6 %collective-permute-start.28 = (bf16[64,32]{0,1:T(8,128)(2,1)S(1)}, bf16[64,32]{0,1:T(8,128)(2,1)S(1)}, u32[]{:S(2)}, u32[]{:S(2)}) collective-permute-start(bf16[64,32]{0,1:T(8,128)(2,1)S(1)} %slice.82), channel_id=1, source_target_pairs={{0,1},{1,0},{2,3},{3,2},{4,5},{5,4},{6,7},{7,6},{8,9},{9,8},{10,11... | collective-permute-start | bytes 12296 | tf_op jit(solution)/shard_map/ppermute | solution.py:16
  11.7 6.9 %copy-start.5 = (bf16[64,1024]{1,0:T(8,128)(2,1)S(1)}, bf16[64,1024]{1,0:T(8,128)(2,1)}, u32[]{:S(2)}) copy-start(bf16[64,1024]{1,0:T(8,128)(2,1)} %param.6) | copy-start | bytes 393220
  16.0 59.7 %collective-permute-start.12 = (f32[512,512]{0,1:T(8,128)}, f32[512,512]{0,1:T(8,128)S(1)}, u32[]{:S(2)}, u32[]{:S(2)}) collective-permute-start(f32[512,512]{0,1:T(8,128)} %get-tuple-element.14), channel_id=1, source_target_pairs={{0,1},{1,0},{2,3},{3,2},{4,5},{5,4},{6,7},{7,6},{8,9},{9,8},{10,11... | collective-permute-start | bytes 3145736 | tf_op jit(solution)/shard_map/ppermute | solution.py:16
  16.0 63.0 %collective-permute-start.17 = (f32[512,512]{0,1:T(8,128)}, f32[512,512]{0,1:T(8,128)}, u32[]{:S(2)}, u32[]{:S(2)}) collective-permute-start(f32[512,512]{0,1:T(8,128)} %get-tuple-element.13), channel_id=1, source_target_pairs={{0,1},{1,0},{2,3},{3,2},{4,5},{5,4},{6,7},{7,6},{8,9},{9,8},{10,11... | collective-permute-start | bytes 3145736 | tf_op jit(solution)/shard_map/ppermute | solution.py:16
  16.5 64.4 %collective-permute-start.24 = (f32[512,512]{0,1:T(8,128)}, f32[512,512]{0,1:T(8,128)}, u32[]{:S(2)}, u32[]{:S(2)}) collective-permute-start(f32[512,512]{0,1:T(8,128)} %get-tuple-element.12), channel_id=1, source_target_pairs={{0,1},{1,0},{2,3},{3,2},{4,5},{5,4},{6,7},{7,6},{8,9},{9,8},{10,11... | collective-permute-start | bytes 3145736 | tf_op jit(solution)/shard_map/ppermute | solution.py:16
  18.6 4.6 %copy-start.12 = (s32[1,4]{1,0:T(1,128)S(1)}, s32[1,4]{1,0:T(1,128)}, u32[]{:S(2)}) copy-start(s32[1,4]{1,0:T(1,128)} %param.10) | copy-start | bytes 52
  26.3 1.4 collective-permute-start.20
  27.8 3.7 %collective-permute-start.29 = (bf16[64,64]{0,1:T(8,128)(2,1)S(1)}, bf16[64,64]{0,1:T(8,128)(2,1)S(1)}, u32[]{:S(2)}, u32[]{:S(2)}) collective-permute-start(bf16[64,64]{0,1:T(8,128)(2,1)S(1)} %pad_maximum_fusion.9), channel_id=1, source_target_pairs={{0,2},{1,3},{2,0},{3,1},{4,6},{5,7},{6,4},{7,5},{8,10},{9,11},{10,... | collective-permute-start | bytes 24584 | tf_op jit(solution)/shard_map/ppermute | solution.py:16
  31.5 1.2 collective-permute-start.14
  32.7 3.9 %collective-permute-start.21 = (bf16[64,128]{0,1:T(8,128)(2,1)S(1)}, bf16[64,128]{0,1:T(8,128)(2,1)S(1)}, u32[]{:S(2)}, u32[]{:S(2)}) collective-permute-start(bf16[64,128]{0,1:T(8,128)(2,1)S(1)} %pad_maximum_fusion.7), channel_id=1, source_target_pairs={{0,2},{1,3},{2,0},{3,1},{4,6},{5,7},{6,4},{7,5},{8,10},{9,11},{10,... | collective-permute-start | bytes 49160 | tf_op jit(solution)/shard_map/ppermute | solution.py:16
  36.6 5.4 %collective-permute-start.30 = (bf16[64,128]{0,1:T(8,128)(2,1)S(1)}, bf16[64,128]{0,1:T(8,128)(2,1)S(1)}, u32[]{:S(2)}, u32[]{:S(2)}) collective-permute-start(bf16[64,128]{0,1:T(8,128)(2,1)S(1)} %pad_maximum_fusion.8), channel_id=1, source_target_pairs={{0,4},{1,5},{2,6},{3,7},{4,0},{5,1},{6,2},{7,3},{8,12},{9,13},{10,... | collective-permute-start | bytes 49160 | tf_op jit(solution)/shard_map/ppermute | solution.py:16
  42.1 1.3 collective-permute-start.10
  43.3 4.3 %collective-permute-start.15 = (bf16[64,256]{0,1:T(8,128)(2,1)S(1)}, bf16[64,256]{0,1:T(8,128)(2,1)S(1)}, u32[]{:S(2)}, u32[]{:S(2)}) collective-permute-start(bf16[64,256]{0,1:T(8,128)(2,1)S(1)} %pad_maximum_fusion.1), channel_id=1, source_target_pairs={{0,2},{1,3},{2,0},{3,1},{4,6},{5,7},{6,4},{7,5},{8,10},{9,11},{10,... | collective-permute-start | bytes 98312 | tf_op jit(solution)/shard_map/ppermute | solution.py:16
  47.6 5.8 %collective-permute-start.22 = (bf16[64,256]{0,1:T(8,128)(2,1)S(1)}, bf16[64,256]{0,1:T(8,128)(2,1)S(1)}, u32[]{:S(2)}, u32[]{:S(2)}) collective-permute-start(bf16[64,256]{0,1:T(8,128)(2,1)S(1)} %pad_maximum_fusion.3), channel_id=1, source_target_pairs={{0,4},{1,5},{2,6},{3,7},{4,0},{5,1},{6,2},{7,3},{8,12},{9,13},{10,... | collective-permute-start | bytes 98312 | tf_op jit(solution)/shard_map/ppermute | solution.py:16
  53.3 4.3 %collective-permute-start.31 = (bf16[64,256]{0,1:T(8,128)(2,1)S(1)}, bf16[64,256]{0,1:T(8,128)(2,1)S(1)}, u32[]{:S(2)}, u32[]{:S(2)}) collective-permute-start(bf16[64,256]{0,1:T(8,128)(2,1)S(1)} %pad_maximum_fusion.5), channel_id=1, source_target_pairs={{0,8},{1,9},{2,10},{3,11},{4,12},{5,13},{6,14},{7,15},{8,0},{9,1},... | collective-permute-start | bytes 98312 | tf_op jit(solution)/shard_map/ppermute | solution.py:16
  57.6 25.4 %collective-permute-start.33 = (f32[512,512]{0,1:T(8,128)}, f32[512,512]{0,1:T(8,128)S(1)}, u32[]{:S(2)}, u32[]{:S(2)}) collective-permute-start(f32[512,512]{0,1:T(8,128)} %get-tuple-element.11), channel_id=1, source_target_pairs={{0,1},{1,0},{2,3},{3,2},{4,5},{5,4},{6,7},{7,6},{8,9},{9,8},{10,11... | collective-permute-start | bytes 3145736 | tf_op jit(solution)/shard_map/ppermute | solution.py:16
  58.4 5.9 %collective-permute-start.11 = (bf16[64,512]{0,1:T(8,128)(2,1)S(1)}, bf16[64,512]{0,1:T(8,128)(2,1)S(1)}, u32[]{:S(2)}, u32[]{:S(2)}) collective-permute-start(bf16[64,512]{0,1:T(8,128)(2,1)S(1)} %pad_maximum_fusion), channel_id=1, source_target_pairs={{0,2},{1,3},{2,0},{3,1},{4,6},{5,7},{6,4},{7,5},{8,10},{9,11},{10,... | collective-permute-start | bytes 196616 | tf_op jit(solution)/shard_map/ppermute | solution.py:16
  64.3 6.6 %collective-permute-start.16 = (bf16[64,512]{0,1:T(8,128)(2,1)S(1)}, bf16[64,512]{0,1:T(8,128)(2,1)S(1)}, u32[]{:S(2)}, u32[]{:S(2)}) collective-permute-start(bf16[64,512]{0,1:T(8,128)(2,1)S(1)} %pad_maximum_fusion.2), channel_id=1, source_target_pairs={{0,4},{1,5},{2,6},{3,7},{4,0},{5,1},{6,2},{7,3},{8,12},{9,13},{10,... | collective-permute-start | bytes 196616 | tf_op jit(solution)/shard_map/ppermute | solution.py:16
  71.0 45.4 %collective-permute-start = (bf16[64,1024]{1,0:T(8,128)(2,1)S(1)}, bf16[64,1024]{1,0:T(8,128)(2,1)S(1)}, u32[]{:S(2)}, u32[]{:S(2)}) collective-permute-start(bf16[64,1024]{1,0:T(8,128)(2,1)S(1)} %copy-done.5), channel_id=1, source_target_pairs={{0,2},{1,3},{2,4},{3,5},{4,6},{5,7},{6,8},{7,9},{8,10},{9,11},{10,... | collective-permute-start | bytes 393224 | tf_op jit(solution)/shard_map/ppermute | solution.py:10
  75.7 43.4 %copy-start.6 = (bf16[512,512]{0,1:T(8,128)(2,1)S(1)}, bf16[512,512]{0,1:T(8,128)(2,1)}, u32[]{:S(2)}) copy-start(bf16[512,512]{0,1:T(8,128)(2,1)} %fusion.14) | copy-start | bytes 1572868
  75.7 58.9 %collective-permute-start.1 = (bf16[1024,512]{1,0:T(8,128)(2,1)}, bf16[1024,512]{1,0:T(8,128)(2,1)}, u32[]{:S(2)}, u32[]{:S(2)}) collective-permute-start(bf16[1024,512]{1,0:T(8,128)(2,1)} %param.7), channel_id=1, source_target_pairs={{0,2},{1,3},{2,4},{3,5},{4,6},{5,7},{6,8},{7,9},{8,10},{9,11},{10,... | collective-permute-start | bytes 3145736 | tf_op jit(solution)/shard_map/ppermute | solution.py:10
  78.9 40.1 %collective-permute-start.2 = (bf16[64,1024]{1,0:T(8,128)(2,1)S(1)}, bf16[64,1024]{1,0:T(8,128)(2,1)S(1)}, u32[]{:S(2)}, u32[]{:S(2)}) collective-permute-start(bf16[64,1024]{1,0:T(8,128)(2,1)S(1)} %copy-done.5), channel_id=1, source_target_pairs={{0,1},{1,2},{2,3},{3,4},{4,5},{5,6},{6,7},{7,8},{8,9},{9,10},{10,1... | collective-permute-start | bytes 393224 | tf_op jit(solution)/shard_map/ppermute | solution.py:10
  80.9 8.7 %collective-permute-start.23 = (bf16[64,512]{0,1:T(8,128)(2,1)S(1)}, bf16[64,512]{0,1:T(8,128)(2,1)S(1)}, u32[]{:S(2)}, u32[]{:S(2)}) collective-permute-start(bf16[64,512]{0,1:T(8,128)(2,1)S(1)} %pad_maximum_fusion.4), channel_id=1, source_target_pairs={{0,8},{1,9},{2,10},{3,11},{4,12},{5,13},{6,14},{7,15},{8,0},{9,1},... | collective-permute-start | bytes 196616 | tf_op jit(solution)/shard_map/ppermute | solution.py:16
  88.0 37.4 %collective-permute-start.34 = (f32[512,512]{0,1:T(8,128)S(1)}, f32[512,512]{0,1:T(8,128)S(1)}, u32[]{:S(2)}, u32[]{:S(2)}) collective-permute-start(f32[512,512]{0,1:T(8,128)S(1)} %get-tuple-element.7), channel_id=1, source_target_pairs={{0,2},{1,3},{2,0},{3,1},{4,6},{5,7},{6,4},{7,5},{8,10},{9,11},{10,... | collective-permute-start | bytes 3145736 | tf_op jit(solution)/shard_map/ppermute | solution.py:16
  89.6 7.9 %collective-permute-start.32 = (bf16[64,512]{0,1:T(8,128)(2,1)S(1)}, bf16[64,512]{0,1:T(8,128)(2,1)S(1)}, u32[]{:S(2)}, u32[]{:S(2)}) collective-permute-start(bf16[64,512]{0,1:T(8,128)(2,1)S(1)} %pad_maximum_fusion.6), channel_id=1, source_target_pairs={{0,16},{1,17},{2,18},{3,19},{4,20},{5,21},{6,22},{7,23},{8,24},{9,... | collective-permute-start | bytes 196616 | tf_op jit(solution)/shard_map/ppermute | solution.py:16
  97.4 23.3 %collective-permute-start.4 = (bf16[64,1024]{1,0:T(8,128)(2,1)S(1)}, bf16[64,1024]{1,0:T(8,128)(2,1)S(1)}, u32[]{:S(2)}, u32[]{:S(2)}) collective-permute-start(bf16[64,1024]{1,0:T(8,128)(2,1)S(1)} %copy-done.5), channel_id=1, source_target_pairs={{1,0},{2,1},{3,2},{4,3},{5,4},{6,5},{7,6},{8,7},{9,8},{10,9},{11,1... | collective-permute-start | bytes 393224 | tf_op jit(solution)/shard_map/ppermute | solution.py:10
  116.4 14.8 %copy-start.9 = (bf16[64,1024]{1,0:T(8,128)(2,1)}, bf16[64,1024]{1,0:T(8,128)(2,1)S(1)}, u32[]{:S(2)}) copy-start(bf16[64,1024]{1,0:T(8,128)(2,1)S(1)} %collective-permute-done) | copy-start | bytes 393220
  116.4 6.9 %collective-permute-start.6 = (bf16[64,1024]{1,0:T(8,128)(2,1)S(1)}, bf16[64,1024]{1,0:T(8,128)(2,1)S(1)}, u32[]{:S(2)}, u32[]{:S(2)}) collective-permute-start(bf16[64,1024]{1,0:T(8,128)(2,1)S(1)} %copy-done.5), channel_id=1, source_target_pairs={{2,0},{3,1},{4,2},{5,3},{6,4},{7,5},{8,6},{9,7},{10,8},{11,9},{12,... | collective-permute-start | bytes 393224 | tf_op jit(solution)/shard_map/ppermute | solution.py:10
  119.1 8.5 %copy-start.8 = (bf16[64,1024]{1,0:T(8,128)(2,1)}, bf16[64,1024]{1,0:T(8,128)(2,1)S(1)}, u32[]{:S(2)}) copy-start(bf16[64,1024]{1,0:T(8,128)(2,1)S(1)} %collective-permute-done.2) | copy-start | bytes 393220
  119.1 8.5 %collective-permute-start.9 = (bf16[512,512]{0,1:T(8,128)(2,1)S(1)}, bf16[512,512]{0,1:T(8,128)(2,1)S(1)}, u32[]{:S(2)}, u32[]{:S(2)}) collective-permute-start(bf16[512,512]{0,1:T(8,128)(2,1)S(1)} %copy-done.6), channel_id=1, source_target_pairs={{0,1},{1,0},{2,3},{3,2},{4,5},{5,4},{6,7},{7,6},{8,9},{9,8},{10,11... | collective-permute-start | bytes 1572872 | tf_op jit(solution)/shard_map/ppermute | solution.py:16
  120.7 4.7 %copy-start.10 = (bf16[64,1024]{1,0:T(8,128)(2,1)}, bf16[64,1024]{1,0:T(8,128)(2,1)S(1)}, u32[]{:S(2)}) copy-start(bf16[64,1024]{1,0:T(8,128)(2,1)S(1)} %collective-permute-done.4) | copy-start | bytes 393220
  120.8 32.7 %collective-permute-start.3 = (bf16[1024,512]{1,0:T(8,128)(2,1)}, bf16[1024,512]{1,0:T(8,128)(2,1)}, u32[]{:S(2)}, u32[]{:S(2)}) collective-permute-start(bf16[1024,512]{1,0:T(8,128)(2,1)} %param.7), channel_id=1, source_target_pairs={{0,1},{1,2},{2,3},{3,4},{4,5},{5,6},{6,7},{7,8},{8,9},{9,10},{10,1... | collective-permute-start | bytes 3145736 | tf_op jit(solution)/shard_map/ppermute | solution.py:10
  123.3 2.1 copy-start.7
  123.3 26.1 %collective-permute-start.25 = (f32[512,512]{0,1:T(8,128)S(1)}, f32[512,512]{0,1:T(8,128)}, u32[]{:S(2)}, u32[]{:S(2)}) collective-permute-start(f32[512,512]{0,1:T(8,128)S(1)} %get-tuple-element.8), channel_id=1, source_target_pairs={{0,2},{1,3},{2,0},{3,1},{4,6},{5,7},{6,4},{7,5},{8,10},{9,11},{10,... | collective-permute-start | bytes 3145736 | tf_op jit(solution)/shard_map/ppermute | solution.py:16
  125.4 74.8 %collective-permute-start.5 = (bf16[1024,512]{1,0:T(8,128)(2,1)}, bf16[1024,512]{1,0:T(8,128)(2,1)}, u32[]{:S(2)}, u32[]{:S(2)}) collective-permute-start(bf16[1024,512]{1,0:T(8,128)(2,1)} %param.7), channel_id=1, source_target_pairs={{1,0},{2,1},{3,2},{4,3},{5,4},{6,5},{7,6},{8,7},{9,8},{10,9},{11,1... | collective-permute-start | bytes 3145736 | tf_op jit(solution)/shard_map/ppermute | solution.py:10
  127.6 3.6 %copy-start.16 = (bf16[512,512]{0,1:T(8,128)(2,1)}, bf16[512,512]{0,1:T(8,128)(2,1)S(1)}, u32[]{:S(2)}) copy-start(bf16[512,512]{0,1:T(8,128)(2,1)S(1)} %collective-permute-done.9) | copy-start | bytes 1572868
  127.6 68.2 %collective-permute-start.35 = (f32[512,512]{0,1:T(8,128)S(1)}, f32[512,512]{0,1:T(8,128)}, u32[]{:S(2)}, u32[]{:S(2)}) collective-permute-start(f32[512,512]{0,1:T(8,128)S(1)} %add.266), channel_id=1, source_target_pairs={{0,4},{1,5},{2,6},{3,7},{4,0},{5,1},{6,2},{7,3},{8,12},{9,13},{10,... | collective-permute-start | bytes 3145736 | tf_op jit(solution)/shard_map/ppermute | solution.py:16
  134.6 71.5 %collective-permute-start.13 = (bf16[512,512]{0,1:T(8,128)(2,1)}, bf16[512,512]{0,1:T(8,128)(2,1)}, u32[]{:S(2)}, u32[]{:S(2)}) collective-permute-start(bf16[512,512]{0,1:T(8,128)(2,1)} %get-tuple-element.10), channel_id=1, source_target_pairs={{0,2},{1,3},{2,0},{3,1},{4,6},{5,7},{6,4},{7,5},{8,10},{9,11},{10,... | collective-permute-start | bytes 1572872 | tf_op jit(solution)/shard_map/ppermute | solution.py:16
  149.4 77.8 %collective-permute-start.18 = (f32[512,512]{0,1:T(8,128)}, f32[512,512]{0,1:T(8,128)}, u32[]{:S(2)}, u32[]{:S(2)}) collective-permute-start(f32[512,512]{0,1:T(8,128)} %get-tuple-element.9), channel_id=1, source_target_pairs={{0,2},{1,3},{2,0},{3,1},{4,6},{5,7},{6,4},{7,5},{8,10},{9,11},{10,... | collective-permute-start | bytes 3145736 | tf_op jit(solution)/shard_map/ppermute | solution.py:16
  153.5 48.1 %copy-start.11 = (bf16[64,1024]{1,0:T(8,128)(2,1)S(1)}, bf16[64,1024]{1,0:T(8,128)(2,1)}, u32[]{:S(2)}) copy-start(bf16[64,1024]{1,0:T(8,128)(2,1)} %copy-done.10) | copy-start | bytes 393220
  153.5 98.5 %collective-permute-start.26 = (f32[512,512]{0,1:T(8,128)}, f32[512,512]{0,1:T(8,128)}, u32[]{:S(2)}, u32[]{:S(2)}) collective-permute-start(f32[512,512]{0,1:T(8,128)} %add.259), channel_id=1, source_target_pairs={{0,4},{1,5},{2,6},{3,7},{4,0},{5,1},{6,2},{7,3},{8,12},{9,13},{10,... | collective-permute-start | bytes 3145736 | tf_op jit(solution)/shard_map/ppermute | solution.py:16
  195.8 90.0 %collective-permute-start.7 = (bf16[1024,512]{1,0:T(8,128)(2,1)}, bf16[1024,512]{1,0:T(8,128)(2,1)}, u32[]{:S(2)}, u32[]{:S(2)}) collective-permute-start(bf16[1024,512]{1,0:T(8,128)(2,1)} %param.7), channel_id=1, source_target_pairs={{2,0},{3,1},{4,2},{5,3},{6,4},{7,5},{8,6},{9,7},{10,8},{11,9},{12,... | collective-permute-start | bytes 3145736 | tf_op jit(solution)/shard_map/ppermute | solution.py:10
  200.2 6.0 %copy-start.3 = (f32[512,512]{1,0:T(8,128)S(1)}, f32[512,512]{1,0:T(8,128)}, u32[]{:S(2)}) copy-start(f32[512,512]{1,0:T(8,128)} %convolution_multiply_fusion.3) | copy-start | bytes 3145732
  200.2 6.0 %copy-start.15 = (f32[512]{0:T(512)S(1)}, f32[512]{0:T(512)}, u32[]{:S(2)}) copy-start(f32[512]{0:T(512)} %multiply_reduce_fusion.7) | copy-start | bytes 6148
  200.2 55.4 %collective-permute-start.36 = (f32[512,512]{0,1:T(8,128)}, f32[512,512]{0,1:T(8,128)}, u32[]{:S(2)}, u32[]{:S(2)}) collective-permute-start(f32[512,512]{0,1:T(8,128)} %add.267), channel_id=1, source_target_pairs={{0,8},{1,9},{2,10},{3,11},{4,12},{5,13},{6,14},{7,15},{8,0},{9,1},... | collective-permute-start | bytes 3145736 | tf_op jit(solution)/shard_map/ppermute | solution.py:16
  206.2 21.1 %copy-start.1 = (f32[512,512]{0,1:T(8,128)S(1)}, f32[512,512]{0,1:T(8,128)}, u32[]{:S(2)}) copy-start(f32[512,512]{0,1:T(8,128)} %get-tuple-element.9) | copy-start | bytes 3145732
  209.7 64.1 %copy-start.2 = (f32[512,512]{1,0:T(8,128)S(1)}, f32[512,512]{1,0:T(8,128)}, u32[]{:S(2)}) copy-start(f32[512,512]{1,0:T(8,128)} %convolution_multiply_fusion.2) | copy-start | bytes 3145732
  209.7 64.1 %copy-start.13 = (f32[512]{0:T(512)S(1)}, f32[512]{0:T(512)}, u32[]{:S(2)}) copy-start(f32[512]{0:T(512)} %multiply_reduce_fusion.5) | copy-start | bytes 6148
  228.6 45.2 %collective-permute-start.19 = (bf16[512,512]{0,1:T(8,128)(2,1)S(1)}, bf16[512,512]{0,1:T(8,128)(2,1)}, u32[]{:S(2)}, u32[]{:S(2)}) collective-permute-start(bf16[512,512]{0,1:T(8,128)(2,1)S(1)} %add_convert_fusion.2), channel_id=1, source_target_pairs={{0,4},{1,5},{2,6},{3,7},{4,0},{5,1},{6,2},{7,3},{8,12},{9,13},{10,... | collective-permute-start | bytes 1572872 | tf_op jit(solution)/shard_map/ppermute | solution.py:16
  254.6 22.7 %copy-start.4 = (f32[512,512]{1,0:T(8,128)S(1)}, f32[512,512]{1,0:T(8,128)}, u32[]{:S(2)}) copy-start(f32[512,512]{1,0:T(8,128)} %convolution_multiply_fusion.1) | copy-start | bytes 3145732
  254.6 22.7 %copy-start.14 = (f32[512]{0:T(512)S(1)}, f32[512]{0:T(512)}, u32[]{:S(2)}) copy-start(f32[512]{0:T(512)} %multiply_reduce_fusion.3) | copy-start | bytes 6148
  254.6 22.7 %collective-permute-start.27 = (bf16[512,512]{0,1:T(8,128)(2,1)}, bf16[512,512]{0,1:T(8,128)(2,1)}, u32[]{:S(2)}, u32[]{:S(2)}) collective-permute-start(bf16[512,512]{0,1:T(8,128)(2,1)} %add_convert_fusion.1), channel_id=1, source_target_pairs={{0,8},{1,9},{2,10},{3,11},{4,12},{5,13},{6,14},{7,15},{8,0},{9,1},... | collective-permute-start | bytes 1572872 | tf_op jit(solution)/shard_map/ppermute | solution.py:16
  258.1 22.6 %collective-permute-start.37 = (bf16[512,512]{0,1:T(8,128)(2,1)}, bf16[512,512]{0,1:T(8,128)(2,1)}, u32[]{:S(2)}, u32[]{:S(2)}) collective-permute-start(bf16[512,512]{0,1:T(8,128)(2,1)} %add_convert_fusion), channel_id=1, source_target_pairs={{0,16},{1,17},{2,18},{3,19},{4,20},{5,21},{6,22},{7,23},{8,24},{9,... | collective-permute-start | bytes 1572872 | tf_op jit(solution)/shard_map/ppermute | solution.py:16
where the time goes:
time: 294 us; the launch traced here: 293 us
  waiting for transfers between devices  125 us (43%)
  starting transfers between devices  73.5 us (25%)
  matrix products  56.1 us (19%)
  other arithmetic  26.3 us (9%)
  local copies, waits for them, and re-layouts  9.58 us (3%)
    ppermute x30, waiting for transfers between devices, from_partner(): return lax.ppermute(value, axis, pairs)  124 us
    ppermute x30, starting transfers between devices, from_partner(): return lax.ppermute(value, axis, pairs)  37.3 us
    ppermute x8, starting transfers between devices, passed_along(): lax.ppermute(value, axis, [(source, source + steps) for source in range(l...  36.2 us
    dot_general x4, matrix products, per_device(): jnp.dot(kernel_tile(points, other_points), other_weights, preferred_eleme...  21 us
    dot_general x4, matrix products, couple_level(): return jnp.dot(transfer, coupled, preferred_element_type=jnp.float32)  13.8 us
    add x4, other arithmetic, per_device(): node_sum = node_sum + partner_sum  10 us
    dot_general x1, matrix products, per_device(): jnp.einsum('lab,ac->lbc', transfers[0], leaf_weights, preferred_element_t...  6.44 us
    convert_element_type x3, other arithmetic, per_device(): node_sum.astype(jnp.bfloat16)  6.39 us
  transfers between devices with their start and end apart: 38, of which 19 were waited for; matrix products, arithmetic and copies ran while one was open for 27% of the time, Pallas kernels for 0%

commit v1 on v0

v1 whole, which is shorter than its diff:
```python
import math

import jax
import jax.numpy as jnp
from jax import lax
from jax.experimental import pallas as pl
from jax.experimental.pallas import tpu as pltpu
from jax.sharding import PartitionSpec as P

F32 = jnp.float32
BF16 = jnp.bfloat16
AXIS = "leaf"
VMEM_BYTES = 48 * 1024 * 1024
ROWS = 256


def dot(a, b, over=((1,), (0,))):
    return lax.dot_general(a, b, (over, ((), ())), preferred_element_type=F32)


def place():
    leaf = lax.axis_index(AXIS)
    return leaf & 1, (leaf >> 1) & 3, (leaf >> 3) & 3


def split_norm(wide, scale):
    norm = jnp.sum(wide * wide, axis=0, keepdims=True) * scale
    high = norm.astype(BF16).astype(F32)
    rest = norm - high
    middle = rest.astype(BF16).astype(F32)
    return high, middle, rest - middle


def lifted(points, left):
    dim, count = points.shape
    scale = math.log2(math.e) / dim
    wide = points.astype(F32)
    high, middle, low = split_norm(wide, -scale)
    row = lax.broadcasted_iota(jnp.int32, (16, count), 0)
    at = 0 if left else 3
    ones = 3 - at
    extra = jnp.where(row == at, high, jnp.where(row == at + 1, middle, jnp.where(row == at + 2, low, 0.0)))
    extra = jnp.where((row >= ones) & (row < ones + 3), 1.0, extra).astype(BF16)
    if left:
        scaled = wide * (2.0 * scale)
        first = scaled.astype(BF16)
        second = (scaled - first.astype(F32)).astype(BF16)
    else:
        first = second = points
    return jnp.concatenate([first, second, extra], axis=0)


def gaussian(left, right):
    return jnp.exp2(dot(left, right, ((0,), (0,)))).astype(BF16)


def call(body, name, outs, args, flops, smem=(), scratch=(), grid=None, in_specs=None):
    specs = in_specs or [pl.BlockSpec(memory_space=pltpu.SMEM if k in smem else pltpu.VMEM) for k in range(len(args))]
    moved = sum(a.size * a.dtype.itemsize for a in args) + sum(math.prod(s) * jnp.dtype(t).itemsize for s, t in outs)
    return pl.pallas_call(
        body,
        name=name,
        grid=grid or (),
        in_specs=specs,
        out_specs=[pl.BlockSpec(memory_space=pltpu.VMEM) for _ in outs],
        out_shape=[jax.ShapeDtypeStruct(s, t) for s, t in outs],
        scratch_shapes=list(scratch),
        compiler_params=pltpu.CompilerParams(vmem_limit_bytes=VMEM_BYTES),
        cost_estimate=pl.CostEstimate(flops=int(flops), bytes_accessed=int(moved), transcendentals=0),
    )(*args)


def pack(half):
    return jnp.concatenate([half[:32], half[32:]], axis=1)


def unpack(packed):
    return jnp.concatenate([packed[:, :256], packed[:, 256:]], axis=0)


def picked(columns, count, wide, kept):
    source = lax.broadcasted_iota(jnp.int32, (columns.shape[1], count), 0)
    target = lax.broadcasted_iota(jnp.int32, (columns.shape[1], count), 1)
    choice = (source == (target // kept) * wide + target % kept).astype(F32).astype(BF16)
    return dot(columns, choice).astype(BF16)


def terms_kernel(w, p, t, pts, index, term0, send, keep, skel, lifted_weights):
    step = pl.program_id(0)
    core, _, _ = place()

    @pl.when(step == 0)
    def _():
        lifted_weights[...] = dot(w[...], p[...], ((0,), (0,))).astype(BF16)
        rank = lax.broadcasted_iota(jnp.int32, (pts.shape[1], index.shape[1]), 0)
        choice = (rank == index[...]).astype(F32).astype(BF16)
        chosen = dot(pts[...], choice).astype(BF16)
        skel[...] = chosen
        send[1024:1088, :] = chosen

    @pl.when(step < 4)
    def _():
        row = pl.multiple_of(step * 256, 256)
        theirs = pl.multiple_of((1 - core) * 256, 256)
        mine = pl.multiple_of(core * 256, 256)
        send[pl.ds(row, 256), :] = dot(lifted_weights[pl.ds(theirs, 256), :], t[0, 0]).astype(BF16)
        keep[pl.ds(row, 256), :] = dot(lifted_weights[pl.ds(mine, 256), :], t[0, 0])

    @pl.when(step == 4)
    def _():
        term0[...] = dot(lifted_weights[...], t[0, 0]).astype(BF16)


def chip_kernel(keep, came, skel, to2, to4, to6, kept, pair, total):
    core, x, _ = place()
    mine, theirs = skel[...], came[1024:1088, :]
    first = jnp.where(core == 0, mine, theirs)
    second = jnp.where(core == 0, theirs, mine)
    pair[0:64, :] = first
    pair[64:128, :] = second
    total[...] = keep[...] + came[0:1024, :].astype(F32)
    to2[0:256, :] = total[0:256, :].astype(BF16)
    to2[384:448, :] = jnp.concatenate([first[:, :256], second[:, :256]], axis=1)
    for level, at in ((3, 0), (4, 64)):
        for out, row, other in ((to2, 256, x ^ 1), (to4, 128, x ^ 2), (to6, 128, x ^ 3)):
            rows = pl.ds(pl.multiple_of((level - 1) * 256 + other * 64, 64), 64)
            out[row + at : row + at + 64, :] = total[rows, :].astype(BF16)
        kept[at : at + 64, :] = total[pl.ds(pl.multiple_of((level - 1) * 256 + x * 64, 64), 64), :]
    packed = pack(jnp.concatenate([first[:, :128], second[:, :128]], axis=1))
    for out, part in ((to4, x & 1), (to6, (x & 1) ^ 1)):
        out[0:128, :] = total[pl.ds(pl.multiple_of(256 + part * 128, 128), 128), :].astype(BF16)
        out[256:288, :] = packed


def row_kernel(from2, from4, from6, kept, pair, to8, to16, ring):
    _, x, _ = place()
    near = from2[384:448, :]
    ring[x] = jnp.concatenate([pair[0:64, 0:128], pair[64:128, 0:128]], axis=1)
    ring[x ^ 1] = jnp.concatenate([near[:, 0:128], near[:, 256:384]], axis=1)
    ring[x ^ 2] = unpack(from4[256:288, :])
    ring[x ^ 3] = unpack(from6[256:288, :])
    points3 = picked(jnp.concatenate([ring[k] for k in range(4)], axis=1), 512, 128, 64)
    for out, at in ((to8, 0), (to16, 64)):
        total = kept[at : at + 64, :] + from2[256 + at : 320 + at, :].astype(F32)
        total = total + from4[128 + at : 192 + at, :].astype(F32) + from6[128 + at : 192 + at, :].astype(F32)
        out[0:64, :] = total.astype(BF16)
    to8[64:128, :] = points3
    to16[64:96, :] = pack(picked(points3, 256, 64, 32))


def couple(sums, own, sibling):
    return dot(sums, gaussian(lifted(sibling, True), lifted(own, False))).astype(BF16)


def couple_low_kernel(term0, from2, from4, from6, pair, ring, out0, out1, out2):
    core, x, _ = place()
    first, second = pair[0:64, :], pair[64:128, :]
    out0[...] = couple(term0[...], jnp.where(core == 0, first, second), jnp.where(core == 0, second, first))
    own = jnp.concatenate([first[:, :256], second[:, :256]], axis=1)
    out1[...] = couple(from2[0:256, :], own, from2[384:448, :])
    low = x & 2
    own = jnp.concatenate([ring[low], ring[low | 1]], axis=1)
    sibling = jnp.concatenate([ring[low ^ 2], ring[(low ^ 2) | 1]], axis=1)
    sums = (from4[0:128, :].astype(F32) + from6[0:128, :].astype(F32)).astype(BF16)
    out2[...] = couple(sums, own, sibling)


def couple_high_kernel(from8, from16, from24, to8, to16, coupled2, out2, out4):
    _, _, z = place()
    points3 = from8[64:128, :]
    level3 = couple(from8[0:64, :], to8[64:128, :], points3)
    mine, beside = unpack(to16[64:96, :]), picked(points3, 256, 64, 32)
    even = (z & 1) == 0
    own = jnp.concatenate([jnp.where(even, mine, beside), jnp.where(even, beside, mine)], axis=1)
    across, past = unpack(from16[64:96, :]), unpack(from24[64:96, :])
    sibling = jnp.concatenate([jnp.where(even, across, past), jnp.where(even, past, across)], axis=1)
    sums = (from16[0:64, :].astype(F32) + from24[0:64, :].astype(F32)).astype(BF16)
    level4 = couple(sums, own, sibling)
    out2[0:64, :] = level3
    out2[64:128, :] = level4
    out2[128:256, :] = coupled2[...]
    out4[0:64, :] = level3
    out4[64:128, :] = level4


def half_kernel(coupled1, own, from2, from4, from6, out):
    _, x, _ = place()
    out[0:256, :] = coupled1[...]
    out[pl.ds(pl.multiple_of(256 + (x & 1) * 128, 128), 128), :] = own[128:256, :]
    out[pl.ds(pl.multiple_of(256 + ((x & 1) ^ 1) * 128, 128), 128), :] = from2[128:256, :]
    for base, at in ((512, 0), (768, 64)):
        for part, block in ((x, own), (x ^ 1, from2), (x ^ 2, from4), (x ^ 3, from6)):
            out[pl.ds(pl.multiple_of(base + part * 64, 64), 64), :] = block[at : at + 64, :]


def near_kernel(count, slots, with_total, *refs):
    mask, own = refs[0], refs[1]
    blocks = refs[2 : 2 + count]
    total = refs[2 + count] if with_total else None
    out = refs[-1]
    core, _, _ = place()
    size = own.shape[1]
    left = lifted(own[...], True)
    result = [None] * (size // ROWS)
    for block, slot in zip(blocks, slots):
        if slot is None:
            right = lifted(own[...], False)
        else:
            columns = jnp.concatenate([block[size : size + 64, :], block[size + 64 : size + 128, :]], axis=1)
            right = lifted(columns, False)
            flag = jnp.where(core == 0, mask[0, slot[0]], mask[0, slot[1]]).astype(F32)
        values = block[0:size, :]
        for k in range(size // ROWS):
            tile = gaussian(left[:, k * ROWS : (k + 1) * ROWS], right)
            part = dot(tile, values)
            if slot is not None:
                part = part * flag
            result[k] = part if result[k] is None else result[k] + part
    for k in range(size // ROWS):
        rows = slice(k * ROWS, (k + 1) * ROWS)
        out[rows, :] = result[k] + total[rows, :] if with_total else result[k]


def near(mask, points, blocks, slots, total, name):
    args = [mask, points, *blocks] + ([] if total is None else [total])
    size, width = points.shape[1], blocks[0].shape[1]

    def body(*refs):
        near_kernel(len(blocks), slots, total is not None, *refs)

    flops = 2 * len(blocks) * size * size * (width + 256)
    return call(body, name, [((size, width), F32)], args, flops, smem=(0,))[0]


def product_kernel(total, interp, transfers, coupled0, mine, theirs, out, far):
    core, _, _ = place()
    base = dot(transfers[0, 0], coupled0[...], ((1,), (1,)))
    far[...] = base
    for part, half in ((core, mine), (1 - core, theirs)):
        columns = pl.ds(pl.multiple_of(part * 256, 256), 256)
        value = far[:, columns]
        for level in range(1, 5):
            value = value + dot(transfers[0, level], half[(level - 1) * 256 : level * 256, :], ((1,), (1,)))
        far[:, columns] = value
    skeleton = far[...].astype(BF16)
    for k in range(total.shape[0] // ROWS):
        rows = slice(k * ROWS, (k + 1) * ROWS)
        out[rows, :] = (total[rows, :] + dot(interp[rows, :], skeleton)).astype(BF16)


def per_device(points, weights, interp, transfers, near_mask, skel_index):
    leaves = lax.axis_size(AXIS)
    size, width = weights.shape

    def swap(value, mask):
        return lax.ppermute(value, AXIS, [(leaf, leaf ^ mask) for leaf in range(leaves)])

    def moved(value, even, odd):
        pairs = [(leaf, leaf + (odd if leaf & 1 else even)) for leaf in range(leaves)]
        return lax.ppermute(value, AXIS, [(a, b) for a, b in pairs if 0 <= b < leaves])

    payload = jnp.concatenate([weights, points[:, : size // 2], points[:, size // 2 :]], axis=0)
    outer = moved(payload, -1, 1)
    partner = swap(payload, 1)

    whole = lambda *shape: pl.BlockSpec(shape, lambda g: (0,) * len(shape))
    term0, send, keep, skel = call(
        terms_kernel,
        "terms",
        [((512, 512), BF16), ((1088, 512), BF16), ((1024, 512), F32), ((64, 512), BF16)],
        [weights, interp, transfers, points, skel_index],
        2 * 512 * 512 * (1024 + 5 * 512),
        scratch=[pltpu.VMEM((512, 512), BF16)],
        grid=(5,),
        in_specs=[
            whole(size, width),
            whole(size, 512),
            pl.BlockSpec((1, 1, 512, 512), lambda g: (0, lax.rem(g + 1, 5), 0, 0)),
            whole(64, size),
            whole(1, 512),
        ],
    )
    came = swap(send, 1)
    term0 = swap(term0, 1)
    total = near(near_mask, points, [weights, partner], [None, (2, 1)], None, "near_own")

    to2, to4, to6, kept, pair = call(
        chip_kernel,
        "chip",
        [((448, 512), BF16), ((288, 512), BF16), ((288, 512), BF16), ((128, 512), F32), ((128, 512), BF16)],
        [keep, came, skel],
        1e6,
        scratch=[pltpu.VMEM((1024, 512), F32)],
    )
    from2, from4, from6 = swap(to2, 2), swap(to4, 4), swap(to6, 6)
    past = swap(outer, 1)
    second = moved(payload, 2, -2)

    to8, to16, ring = call(
        row_kernel,
        "row",
        [((128, 512), BF16), ((96, 512), BF16), ((4, 64, 256), BF16)],
        [from2, from4, from6, kept, pair],
        1e8,
    )
    from8, from16, from24 = swap(to8, 8), swap(to16, 16), swap(to16, 24)
    coupled0, coupled1, coupled2 = call(
        couple_low_kernel,
        "couple_low",
        [((512, 512), BF16), ((256, 512), BF16), ((128, 512), BF16)],
        [term0, from2, from4, from6, pair, ring],
        2 * 512 * 512 * (3 * 256 + 896),
    )
    total = near(near_mask, points, [outer, past], [(1, 2), (3, 0)], total, "near_outer")
    part2, part4 = call(
        couple_high_kernel,
        "couple_high",
        [((256, 512), BF16), ((128, 512), BF16)],
        [from8, from16, from24, to8, to16, coupled2],
        2 * 512 * 512 * (2 * 256 + 128),
    )
    back2, back4, back6 = swap(part2, 2), swap(part4, 4), swap(part4, 6)
    (mine,) = call(half_kernel, "half", [((1024, 512), BF16)], [coupled1, part2, back2, back4, back6], 1e6)
    theirs = swap(mine, 1)
    total = near(near_mask, points, [second], [(0, 3)], total, "near_second")
    return call(
        product_kernel,
        "product",
        [((size, width), BF16)],
        [total, interp, transfers, coupled0, mine, theirs],
        2 * 512 * 512 * (5 * 512 + 1024),
        scratch=[pltpu.VMEM((512, 512), F32)],
    )[0]


def solution(mesh):
    return jax.shard_map(
        per_device,
        mesh=mesh,
        in_specs=(
            P(None, AXIS),
            P(AXIS, None),
            P(AXIS, None),
            P(AXIS, None, None, None),
            P(AXIS, None),
            P(AXIS, None),
        ),
        out_specs=P(AXIS, None),
        check_vma=False,
    )
```

time: 294 us -> 109 us (0.37)
  the two profiles are of different devices: /device:TPU:26 before, /device:TPU:25 now
where the time goes in v1:
time: 109 us; the launch traced here: 106 us
  waiting for transfers between devices  48.4 us (44%)
  starting transfers between devices  26.9 us (25%)
  Pallas kernels  25.5 us (23%)
  local copies, waits for them, and re-layouts  5.41 us (5%)
    ppermute x14, waiting for transfers between devices, swap(): lax.ppermute(value, AXIS, [(leaf, leaf ^ mask) for leaf in range(leaves)])  33.8 us
    pallas_call x10, Pallas kernels, call(): pl.pallas_call(body, name=name, grid=grid or (), in_specs=specs, out_spec...  25.5 us
    ppermute x14, starting transfers between devices, swap(): lax.ppermute(value, AXIS, [(leaf, leaf ^ mask) for leaf in range(leaves)])  20.6 us
    ppermute x2, waiting for transfers between devices, moved(): lax.ppermute(value, AXIS, [(a, b) for a, b in pairs if 0 <= b < leaves])  14.6 us
    ppermute x2, starting transfers between devices, moved(): lax.ppermute(value, AXIS, [(a, b) for a, b in pairs if 0 <= b < leaves])  6.32 us
    unnamed x18, local copies, waits for them, and re-layouts  5.4 us
  transfers between devices with their start and end apart: 16, of which 5 were waited for; matrix products, arithmetic and copies ran while one was open for 0% of the time, Pallas kernels for 14%

profile of v1, /device:TPU:25, one launch (start us, length us, event | category | flops | bytes accessed | tf_op | source)
XLA Modules:
  0.0 106.5 jit_solution(12391951959212515167)
XLA Ops:
  0.0 0.0 copy-start
  0.0 1.2 %copy-done = bf16[1024,512]{1,0:T(8,128)(2,1)S(1)} copy-done((bf16[1024,512]{1,0:T(8,128)(2,1)S(1)}, bf16[1024,512]{1,0:T(8,128)(2,1)}, u32[]{:S(2)}) %copy-start) | copy-done | bytes 1048600
  1.2 0.0 copy-start.2
  1.2 1.2 %copy-done.2 = bf16[1024,512]{1,0:T(8,128)(2,1)S(1)} copy-done((bf16[1024,512]{1,0:T(8,128)(2,1)S(1)}, bf16[1024,512]{1,0:T(8,128)(2,1)}, u32[]{:S(2)}) %copy-start.2) | copy-done | bytes 1048600
  2.5 0.0 copy-start.4
  2.5 0.9 copy-done.4
  3.4 0.0 copy-start.6
  3.4 0.7 copy-done.6
  4.0 5.4 %terms.1 = (bf16[512,512]{1,0:T(8,128)(2,1)S(1)}, bf16[1088,512]{1,0:T(8,128)(2,1)S(1)}, f32[1024,512]{1,0:T(8,128)S(1)}, bf16[64,512]{1,0:T(8,128)(2,1)S(1)}) custom-call(bf16[1024,512]{1,0:T(8,128)(2,1)S(1)} %copy-done.2, bf16[1024,512]{1,0:T(8,128)(2,1)S(1)} %copy-done, bf16[1,5,512,512]{3,2,1,0:T(8,128)(2,1)} %transfers.1, ...), custom_call_target="tpu_custom_call" | custom-call | flops 1879048192 | bytes 8652800 | tf_op jit(solution)/shard_map/terms/pallas_call | solution.py:60
  9.5 0.8 collective-permute-start.5
  10.2 0.1 pad_maximum_fusion
  10.3 3.0 %collective-permute-start.1 = (bf16[1152,512]{1,0:T(8,128)(2,1)S(1)}, bf16[1152,512]{1,0:T(8,128)(2,1)S(1)}, u32[]{:S(2)}, u32[]{:S(2)}) collective-permute-start(bf16[1152,512]{1,0:T(8,128)(2,1)S(1)} %pad_maximum_fusion), channel_id=1, source_target_pairs={{1,2},{2,1},{3,4},{4,3},{5,6},{6,5},{7,8},{8,7},{9,10},{10,9},{11,... | collective-permute-start | bytes 3538952 | tf_op jit(solution)/shard_map/ppermute | solution.py:260
  13.3 5.5 %collective-permute-start.4 = (bf16[512,512]{1,0:T(8,128)(2,1)S(1)}, bf16[512,512]{1,0:T(8,128)(2,1)S(1)}, u32[]{:S(2)}, u32[]{:S(2)}) collective-permute-start(bf16[512,512]{1,0:T(8,128)(2,1)S(1)} %get-tuple-element.22), channel_id=1, source_target_pairs={{0,1},{1,0},{2,3},{3,2},{4,5},{5,4},{6,7},{7,6},{8,9},{9,8},{10,11... | collective-permute-start | bytes 1572872 | tf_op jit(solution)/shard_map/ppermute | solution.py:256
  18.8 0.0 collective-permute-done.5.came
  18.8 0.4 chip.1
  19.2 0.1 collective-permute-start.6
  19.3 0.1 collective-permute-start.3
  19.4 0.1 collective-permute-start.7
  19.5 14.6 %collective-permute-done.1.refs_2_ = bf16[1152,512]{1,0:T(8,128)(2,1)S(1)} collective-permute-done((bf16[1152,512]{1,0:T(8,128)(2,1)S(1)}, bf16[1152,512]{1,0:T(8,128)(2,1)S(1)}, u32[]{:S(2)}, u32[]{:S(2)}) %collective-permute-start.1) | collective-permute-done | bytes 1179680 | tf_op jit(solution)/shard_map/ppermute | solution.py:260
  34.2 0.0 collective-permute-start.8
  34.2 11.4 %collective-permute-done.7.from4 = bf16[288,512]{1,0:T(8,128)(2,1)S(1)} collective-permute-done((bf16[288,512]{1,0:T(8,128)(2,1)S(1)}, bf16[288,512]{1,0:T(8,128)(2,1)S(1)}, u32[]{:S(2)}, u32[]{:S(2)}) %collective-permute-start.7) | collective-permute-done | bytes 294944 | tf_op jit(solution)/shard_map/ppermute | solution.py:256
  45.6 0.0 collective-permute-start.2
  45.6 0.0 collective-permute-done.8.from6
  45.6 0.0 collective-permute-done.6.from2
  45.6 0.5 row.1
  46.1 5.1 %collective-permute-start.9 = (bf16[128,512]{1,0:T(8,128)(2,1)S(1)}, bf16[128,512]{1,0:T(8,128)(2,1)S(1)}, u32[]{:S(2)}, u32[]{:S(2)}) collective-permute-start(bf16[128,512]{1,0:T(8,128)(2,1)S(1)} %get-tuple-element.34.to8), channel_id=1, source_target_pairs={{0,8},{1,9},{2,10},{3,11},{4,12},{5,13},{6,14},{7,15},{8,0},{9,1},... | collective-permute-start | bytes 393224 | tf_op jit(solution)/shard_map/ppermute | solution.py:256
  51.2 2.5 %collective-permute-start.11 = (bf16[96,512]{1,0:T(8,128)(2,1)S(1)}, bf16[96,512]{1,0:T(8,128)(2,1)S(1)}, u32[]{:S(2)}, u32[]{:S(2)}) collective-permute-start(bf16[96,512]{1,0:T(8,128)(2,1)S(1)} %get-tuple-element.35.to16), channel_id=1, source_target_pairs={{0,24},{1,25},{2,26},{3,27},{4,28},{5,29},{6,30},{7,31},{8,16},{9,... | collective-permute-start | bytes 294920 | tf_op jit(solution)/shard_map/ppermute | solution.py:256
  53.7 0.0 collective-permute-done.4.term0
  53.7 1.1 %collective-permute-start.10 = (bf16[96,512]{1,0:T(8,128)(2,1)S(1)}, bf16[96,512]{1,0:T(8,128)(2,1)S(1)}, u32[]{:S(2)}, u32[]{:S(2)}) collective-permute-start(bf16[96,512]{1,0:T(8,128)(2,1)S(1)} %get-tuple-element.35.to16), channel_id=1, source_target_pairs={{0,16},{1,17},{2,18},{3,19},{4,20},{5,21},{6,22},{7,23},{8,24},{9,... | collective-permute-start | bytes 294920 | tf_op jit(solution)/shard_map/ppermute | solution.py:256
  54.8 1.4 %couple_low.1 = (bf16[512,512]{1,0:T(8,128)(2,1)S(1)}, bf16[256,512]{1,0:T(8,128)(2,1)S(1)}, bf16[128,512]{1,0:T(8,128)(2,1)S(1)}) custom-call(bf16[512,512]{1,0:T(8,128)(2,1)S(1)} %collective-permute-done.4.term0, bf16[448,512]{1,0:T(8,128)(2,1)S(1)} %collective-permute-done.6.from2, bf16[288,512]{1,0:T(8,128)(2,1)S(1)} %collective-permute-done.7.from4, ...), custom_call_target="tpu_custom_call" | custom-call | flops 872415232 | bytes 2752512 | tf_op jit(solution)/shard_map/couple_low/pallas_call | solution.py:60
  56.2 1.5 %collective-permute-done.11.from24 = bf16[96,512]{1,0:T(8,128)(2,1)S(1)} collective-permute-done((bf16[96,512]{1,0:T(8,128)(2,1)S(1)}, bf16[96,512]{1,0:T(8,128)(2,1)S(1)}, u32[]{:S(2)}, u32[]{:S(2)}) %collective-permute-start.11) | collective-permute-done | bytes 98336 | tf_op jit(solution)/shard_map/ppermute | solution.py:256
  57.7 3.3 %collective-permute-start = (bf16[1152,512]{1,0:T(8,128)(2,1)S(1)}, bf16[1152,512]{1,0:T(8,128)(2,1)S(1)}, u32[]{:S(2)}, u32[]{:S(2)}) collective-permute-start(bf16[1152,512]{1,0:T(8,128)(2,1)S(1)} %pad_maximum_fusion), channel_id=1, source_target_pairs={{0,2},{2,4},{3,1},{4,6},{5,3},{6,8},{7,5},{8,10},{9,7},{10,12},{11... | collective-permute-start | bytes 3538952 | tf_op jit(solution)/shard_map/ppermute | solution.py:260
  61.0 0.0 collective-permute-done.10.from16
  61.0 0.0 collective-permute-done.9.from8
  61.0 1.0 couple_high.1
  62.0 0.0 copy-start.3
  62.0 0.0 copy-start.5
  62.1 0.0 copy-start.7
  62.1 0.1 collective-permute-start.14
  62.2 0.1 collective-permute-start.12
  62.3 14.6 %collective-permute-done.14.from6 = bf16[128,512]{1,0:T(8,128)(2,1)S(1)} collective-permute-done((bf16[128,512]{1,0:T(8,128)(2,1)S(1)}, bf16[128,512]{1,0:T(8,128)(2,1)S(1)}, u32[]{:S(2)}, u32[]{:S(2)}) %collective-permute-start.14) | collective-permute-done | bytes 131104 | tf_op jit(solution)/shard_map/ppermute | solution.py:256
  76.9 0.0 collective-permute-start.13
  77.0 6.2 %collective-permute-done.13.from4 = bf16[128,512]{1,0:T(8,128)(2,1)S(1)} collective-permute-done((bf16[128,512]{1,0:T(8,128)(2,1)S(1)}, bf16[128,512]{1,0:T(8,128)(2,1)S(1)}, u32[]{:S(2)}, u32[]{:S(2)}) %collective-permute-start.13) | collective-permute-done | bytes 131104 | tf_op jit(solution)/shard_map/ppermute | solution.py:256
  83.2 0.0 collective-permute-done.12.from2
  83.2 0.1 half.1.mine
  83.3 5.1 %collective-permute-start.15 = (bf16[1024,512]{1,0:T(8,128)(2,1)S(1)}, bf16[1024,512]{1,0:T(8,128)(2,1)S(1)}, u32[]{:S(2)}, u32[]{:S(2)}) collective-permute-start(bf16[1024,512]{1,0:T(8,128)(2,1)S(1)} %half.1.mine), channel_id=1, source_target_pairs={{0,1},{1,0},{2,3},{3,2},{4,5},{5,4},{6,7},{7,6},{8,9},{9,8},{10,11... | collective-permute-start | bytes 3145736 | tf_op jit(solution)/shard_map/ppermute | solution.py:256
  88.4 0.0 collective-permute-done.3.refs_3_
  88.4 0.0 copy-done.3
  88.4 0.0 copy-done.5
  88.4 0.0 copy-done.7
  88.4 4.1 %near_own.1.refs_4_ = f32[1024,512]{1,0:T(8,128)S(1)} custom-call(s32[1,4]{1,0:T(1,128)S(1)} %copy-done.7, bf16[64,1024]{1,0:T(8,128)(2,1)S(1)} %copy-done.5, bf16[1024,512]{1,0:T(8,128)(2,1)S(1)} %copy-done.3, bf16[1152,512]{1,0:T(8,128)(2,1)S(1)} %collective-permute-done.3.refs_3_), custom_call_target="tpu_custom_call" | custom-call | flops 3221225472 | bytes 4456464 | tf_op jit(solution)/shard_map/near_own/pallas_call | solution.py:60
  92.5 0.0 copy-start.8
  92.5 1.3 %copy-done.8 = f32[1024,512]{1,0:T(8,128)} copy-done((f32[1024,512]{1,0:T(8,128)}, f32[1024,512]{1,0:T(8,128)S(1)}, u32[]{:S(2)}) %copy-start.8) | copy-done | bytes 2097176
  93.8 0.0 collective-permute-done.2.refs_3_
  93.8 5.1 %near_outer.1.refs_3_ = f32[1024,512]{1,0:T(8,128)S(1)} custom-call(s32[1,4]{1,0:T(1,128)S(1)} %copy-done.7, bf16[64,1024]{1,0:T(8,128)(2,1)S(1)} %copy-done.5, bf16[1152,512]{1,0:T(8,128)(2,1)S(1)} %collective-permute-done.1.refs_2_, bf16[1152,512]{1,0:T(8,128)(2,1)S(1)} %collective-permute-done.2.refs_3_, f32[1024,512]{1,0:T(8,128)} %copy-done.8), custom_call_target="tpu_custom_call" | custom-call | flops 3221225472 | bytes 6684688 | tf_op jit(solution)/shard_map/near_outer/pallas_call | solution.py:60
  98.9 0.0 copy-start.1
  98.9 0.0 collective-permute-done.refs_2_
  99.0 2.4 %near_second.1.total = f32[1024,512]{1,0:T(8,128)S(1)} custom-call(s32[1,4]{1,0:T(1,128)S(1)} %copy-done.7, bf16[64,1024]{1,0:T(8,128)(2,1)S(1)} %copy-done.5, bf16[1152,512]{1,0:T(8,128)(2,1)S(1)} %collective-permute-done.refs_2_, f32[1024,512]{1,0:T(8,128)S(1)} %near_outer.1.refs_3_), custom_call_target="tpu_custom_call" | custom-call | flops 1610612736 | bytes 5505040 | tf_op jit(solution)/shard_map/near_second/pallas_call | solution.py:60
  101.4 0.0 collective-permute-done.15.theirs
  101.4 0.0 copy-done.1
  101.4 5.1 %product.1 = bf16[1024,512]{1,0:T(8,128)(2,1)} custom-call(f32[1024,512]{1,0:T(8,128)S(1)} %near_second.1.total, bf16[1024,512]{1,0:T(8,128)(2,1)S(1)} %copy-done.1, bf16[1,5,512,512]{3,2,1,0:T(8,128)(2,1)} %transfers.1, bf16[512,512]{1,0:T(8,128)(2,1)S(1)} %get-tuple-element.32.coupled0, bf16[1024,512]{1,0:T(8,128)(2,1)S(1)} %half.1.mine, ...), custom_call_target="tpu_custom_call" | custom-call | flops 1879048192 | bytes 9437184 | tf_op jit(solution)/shard_map/product/pallas_call | solution.py:60
  (1 shorter events, 0.0 us)
Async XLA Ops:
  0.0 1.2 %copy-start = (bf16[1024,512]{1,0:T(8,128)(2,1)S(1)}, bf16[1024,512]{1,0:T(8,128)(2,1)}, u32[]{:S(2)}) copy-start(bf16[1024,512]{1,0:T(8,128)(2,1)} %interp.1) | copy-start | bytes 3145732
  1.2 1.2 %copy-start.2 = (bf16[1024,512]{1,0:T(8,128)(2,1)S(1)}, bf16[1024,512]{1,0:T(8,128)(2,1)}, u32[]{:S(2)}) copy-start(bf16[1024,512]{1,0:T(8,128)(2,1)} %w.1) | copy-start | bytes 3145732
  2.5 0.9 copy-start.4
  3.4 0.7 copy-start.6
  9.5 9.4 %collective-permute-start.5 = (bf16[1088,512]{1,0:T(8,128)(2,1)S(1)}, bf16[1088,512]{1,0:T(8,128)(2,1)S(1)}, u32[]{:S(2)}, u32[]{:S(2)}) collective-permute-start(bf16[1088,512]{1,0:T(8,128)(2,1)S(1)} %get-tuple-element.24), channel_id=1, source_target_pairs={{0,1},{1,0},{2,3},{3,2},{4,5},{5,4},{6,7},{7,6},{8,9},{9,8},{10,11... | collective-permute-start | bytes 3342344 | tf_op jit(solution)/shard_map/ppermute | solution.py:256
  10.3 23.8 %collective-permute-start.1 = (bf16[1152,512]{1,0:T(8,128)(2,1)S(1)}, bf16[1152,512]{1,0:T(8,128)(2,1)S(1)}, u32[]{:S(2)}, u32[]{:S(2)}) collective-permute-start(bf16[1152,512]{1,0:T(8,128)(2,1)S(1)} %pad_maximum_fusion), channel_id=1, source_target_pairs={{1,2},{2,1},{3,4},{4,3},{5,6},{6,5},{7,8},{8,7},{9,10},{10,9},{11,... | collective-permute-start | bytes 3538952 | tf_op jit(solution)/shard_map/ppermute | solution.py:260
  13.3 40.4 %collective-permute-start.4 = (bf16[512,512]{1,0:T(8,128)(2,1)S(1)}, bf16[512,512]{1,0:T(8,128)(2,1)S(1)}, u32[]{:S(2)}, u32[]{:S(2)}) collective-permute-start(bf16[512,512]{1,0:T(8,128)(2,1)S(1)} %get-tuple-element.22), channel_id=1, source_target_pairs={{0,1},{1,0},{2,3},{3,2},{4,5},{5,4},{6,7},{7,6},{8,9},{9,8},{10,11... | collective-permute-start | bytes 1572872 | tf_op jit(solution)/shard_map/ppermute | solution.py:256
  19.2 26.4 %collective-permute-start.6 = (bf16[448,512]{1,0:T(8,128)(2,1)S(1)}, bf16[448,512]{1,0:T(8,128)(2,1)S(1)}, u32[]{:S(2)}, u32[]{:S(2)}) collective-permute-start(bf16[448,512]{1,0:T(8,128)(2,1)S(1)} %get-tuple-element.26), channel_id=1, source_target_pairs={{0,2},{1,3},{2,0},{3,1},{4,6},{5,7},{6,4},{7,5},{8,10},{9,11},{10,... | collective-permute-start | bytes 1376264 | tf_op jit(solution)/shard_map/ppermute | solution.py:256
  19.3 69.0 %collective-permute-start.3 = (bf16[1152,512]{1,0:T(8,128)(2,1)S(1)}, bf16[1152,512]{1,0:T(8,128)(2,1)S(1)}, u32[]{:S(2)}, u32[]{:S(2)}) collective-permute-start(bf16[1152,512]{1,0:T(8,128)(2,1)S(1)} %pad_maximum_fusion), channel_id=1, source_target_pairs={{0,1},{1,0},{2,3},{3,2},{4,5},{5,4},{6,7},{7,6},{8,9},{9,8},{10,11... | collective-permute-start | bytes 3538952 | tf_op jit(solution)/shard_map/ppermute | solution.py:256
  19.4 26.2 %collective-permute-start.7 = (bf16[288,512]{1,0:T(8,128)(2,1)S(1)}, bf16[288,512]{1,0:T(8,128)(2,1)S(1)}, u32[]{:S(2)}, u32[]{:S(2)}) collective-permute-start(bf16[288,512]{1,0:T(8,128)(2,1)S(1)} %get-tuple-element.27), channel_id=1, source_target_pairs={{0,4},{1,5},{2,6},{3,7},{4,0},{5,1},{6,2},{7,3},{8,12},{9,13},{10,... | collective-permute-start | bytes 884744 | tf_op jit(solution)/shard_map/ppermute | solution.py:256
  34.2 11.5 %collective-permute-start.8 = (bf16[288,512]{1,0:T(8,128)(2,1)S(1)}, bf16[288,512]{1,0:T(8,128)(2,1)S(1)}, u32[]{:S(2)}, u32[]{:S(2)}) collective-permute-start(bf16[288,512]{1,0:T(8,128)(2,1)S(1)} %get-tuple-element.28), channel_id=1, source_target_pairs={{0,6},{1,7},{2,4},{3,5},{4,2},{5,3},{6,0},{7,1},{8,14},{9,15},{10,... | collective-permute-start | bytes 884744 | tf_op jit(solution)/shard_map/ppermute | solution.py:256
  45.6 48.2 %collective-permute-start.2 = (bf16[1152,512]{1,0:T(8,128)(2,1)S(1)}, bf16[1152,512]{1,0:T(8,128)(2,1)S(1)}, u32[]{:S(2)}, u32[]{:S(2)}) collective-permute-start(bf16[1152,512]{1,0:T(8,128)(2,1)S(1)} %collective-permute-done.1.refs_2_), channel_id=1, source_target_pairs={{0,1},{1,0},{2,3},{3,2},{4,5},{5,4},{6,7},{7,6},{8,9},{9,8},{10,11... | collective-permute-start | bytes 3538952 | tf_op jit(solution)/shard_map/ppermute | solution.py:256
  46.1 14.9 %collective-permute-start.9 = (bf16[128,512]{1,0:T(8,128)(2,1)S(1)}, bf16[128,512]{1,0:T(8,128)(2,1)S(1)}, u32[]{:S(2)}, u32[]{:S(2)}) collective-permute-start(bf16[128,512]{1,0:T(8,128)(2,1)S(1)} %get-tuple-element.34.to8), channel_id=1, source_target_pairs={{0,8},{1,9},{2,10},{3,11},{4,12},{5,13},{6,14},{7,15},{8,0},{9,1},... | collective-permute-start | bytes 393224 | tf_op jit(solution)/shard_map/ppermute | solution.py:256
  51.2 6.5 %collective-permute-start.11 = (bf16[96,512]{1,0:T(8,128)(2,1)S(1)}, bf16[96,512]{1,0:T(8,128)(2,1)S(1)}, u32[]{:S(2)}, u32[]{:S(2)}) collective-permute-start(bf16[96,512]{1,0:T(8,128)(2,1)S(1)} %get-tuple-element.35.to16), channel_id=1, source_target_pairs={{0,24},{1,25},{2,26},{3,27},{4,28},{5,29},{6,30},{7,31},{8,16},{9,... | collective-permute-start | bytes 294920 | tf_op jit(solution)/shard_map/ppermute | solution.py:256
  53.7 7.3 %collective-permute-start.10 = (bf16[96,512]{1,0:T(8,128)(2,1)S(1)}, bf16[96,512]{1,0:T(8,128)(2,1)S(1)}, u32[]{:S(2)}, u32[]{:S(2)}) collective-permute-start(bf16[96,512]{1,0:T(8,128)(2,1)S(1)} %get-tuple-element.35.to16), channel_id=1, source_target_pairs={{0,16},{1,17},{2,18},{3,19},{4,20},{5,21},{6,22},{7,23},{8,24},{9,... | collective-permute-start | bytes 294920 | tf_op jit(solution)/shard_map/ppermute | solution.py:256
  57.7 41.2 %collective-permute-start = (bf16[1152,512]{1,0:T(8,128)(2,1)S(1)}, bf16[1152,512]{1,0:T(8,128)(2,1)S(1)}, u32[]{:S(2)}, u32[]{:S(2)}) collective-permute-start(bf16[1152,512]{1,0:T(8,128)(2,1)S(1)} %pad_maximum_fusion), channel_id=1, source_target_pairs={{0,2},{2,4},{3,1},{4,6},{5,3},{6,8},{7,5},{8,10},{9,7},{10,12},{11... | collective-permute-start | bytes 3538952 | tf_op jit(solution)/shard_map/ppermute | solution.py:260
  62.0 26.3 %copy-start.3 = (bf16[1024,512]{1,0:T(8,128)(2,1)S(1)}, bf16[1024,512]{1,0:T(8,128)(2,1)}, u32[]{:S(2)}) copy-start(bf16[1024,512]{1,0:T(8,128)(2,1)} %w.1) | copy-start | bytes 3145732
  62.0 26.3 %copy-start.5 = (bf16[64,1024]{1,0:T(8,128)(2,1)S(1)}, bf16[64,1024]{1,0:T(8,128)(2,1)}, u32[]{:S(2)}) copy-start(bf16[64,1024]{1,0:T(8,128)(2,1)} %pts.1) | copy-start | bytes 393220
  62.1 26.3 %copy-start.7 = (s32[1,4]{1,0:T(1,128)S(1)}, s32[1,4]{1,0:T(1,128)}, u32[]{:S(2)}) copy-start(s32[1,4]{1,0:T(1,128)} %refs_0_.5) | copy-start | bytes 52
  62.1 14.9 %collective-permute-start.14 = (bf16[128,512]{1,0:T(8,128)(2,1)S(1)}, bf16[128,512]{1,0:T(8,128)(2,1)S(1)}, u32[]{:S(2)}, u32[]{:S(2)}) collective-permute-start(bf16[128,512]{1,0:T(8,128)(2,1)S(1)} %get-tuple-element.38), channel_id=1, source_target_pairs={{0,6},{1,7},{2,4},{3,5},{4,2},{5,3},{6,0},{7,1},{8,14},{9,15},{10,... | collective-permute-start | bytes 393224 | tf_op jit(solution)/shard_map/ppermute | solution.py:256
  62.2 21.0 %collective-permute-start.12 = (bf16[256,512]{1,0:T(8,128)(2,1)S(1)}, bf16[256,512]{1,0:T(8,128)(2,1)S(1)}, u32[]{:S(2)}, u32[]{:S(2)}) collective-permute-start(bf16[256,512]{1,0:T(8,128)(2,1)S(1)} %get-tuple-element.37.own), channel_id=1, source_target_pairs={{0,2},{1,3},{2,0},{3,1},{4,6},{5,7},{6,4},{7,5},{8,10},{9,11},{10,... | collective-permute-start | bytes 786440 | tf_op jit(solution)/shard_map/ppermute | solution.py:256
  76.9 6.2 %collective-permute-start.13 = (bf16[128,512]{1,0:T(8,128)(2,1)S(1)}, bf16[128,512]{1,0:T(8,128)(2,1)S(1)}, u32[]{:S(2)}, u32[]{:S(2)}) collective-permute-start(bf16[128,512]{1,0:T(8,128)(2,1)S(1)} %get-tuple-element.38), channel_id=1, source_target_pairs={{0,4},{1,5},{2,6},{3,7},{4,0},{5,1},{6,2},{7,3},{8,12},{9,13},{10,... | collective-permute-start | bytes 393224 | tf_op jit(solution)/shard_map/ppermute | solution.py:256
  83.3 18.1 %collective-permute-start.15 = (bf16[1024,512]{1,0:T(8,128)(2,1)S(1)}, bf16[1024,512]{1,0:T(8,128)(2,1)S(1)}, u32[]{:S(2)}, u32[]{:S(2)}) collective-permute-start(bf16[1024,512]{1,0:T(8,128)(2,1)S(1)} %half.1.mine), channel_id=1, source_target_pairs={{0,1},{1,0},{2,3},{3,2},{4,5},{5,4},{6,7},{7,6},{8,9},{9,8},{10,11... | collective-permute-start | bytes 3145736 | tf_op jit(solution)/shard_map/ppermute | solution.py:256
  92.5 1.4 %copy-start.8 = (f32[1024,512]{1,0:T(8,128)}, f32[1024,512]{1,0:T(8,128)S(1)}, u32[]{:S(2)}) copy-start(f32[1024,512]{1,0:T(8,128)S(1)} %near_own.1.refs_4_) | copy-start | bytes 6291460
  98.9 2.4 %copy-start.1 = (bf16[1024,512]{1,0:T(8,128)(2,1)S(1)}, bf16[1024,512]{1,0:T(8,128)(2,1)}, u32[]{:S(2)}) copy-start(bf16[1024,512]{1,0:T(8,128)(2,1)} %interp.1) | copy-start | bytes 3145732

commit v2 on v1

--- a/solution.py
+++ b/solution.py
@@ -10,8 +10,9 @@
 F32 = jnp.float32
 BF16 = jnp.bfloat16
 AXIS = "leaf"
-VMEM_BYTES = 48 * 1024 * 1024
+VMEM_BYTES = 24 * 1024 * 1024
 ROWS = 256
+WORK = 1.0
 
 
 def dot(a, b, over=((1,), (0,))):
@@ -54,11 +55,17 @@
     return jnp.exp2(dot(left, right, ((0,), (0,)))).astype(BF16)
 
 
-def call(body, name, outs, args, flops, smem=(), scratch=(), grid=None, in_specs=None):
+def call(body, name, outs, args, flops, smem=(), scratch=(), grid=None, in_specs=None, after=()):
     specs = in_specs or [pl.BlockSpec(memory_space=pltpu.SMEM if k in smem else pltpu.VMEM) for k in range(len(args))]
+    specs = specs + [pl.BlockSpec(memory_space=pl.ANY) for _ in after]
+    taken = len(args)
+
+    def reading(*refs):
+        body(*refs[:taken], *refs[taken + len(after) :])
+
     moved = sum(a.size * a.dtype.itemsize for a in args) + sum(math.prod(s) * jnp.dtype(t).itemsize for s, t in outs)
     return pl.pallas_call(
-        body,
+        reading,
         name=name,
         grid=grid or (),
         in_specs=specs,
@@ -66,8 +73,8 @@
         out_shape=[jax.ShapeDtypeStruct(s, t) for s, t in outs],
         scratch_shapes=list(scratch),
         compiler_params=pltpu.CompilerParams(vmem_limit_bytes=VMEM_BYTES),
-        cost_estimate=pl.CostEstimate(flops=int(flops), bytes_accessed=int(moved), transcendentals=0),
-    )(*args)
+        cost_estimate=pl.CostEstimate(flops=int(flops * WORK), bytes_accessed=int(moved * WORK), transcendentals=0),
+    )(*args, *after)
 
 
 def pack(half):
@@ -85,44 +92,56 @@
     return dot(columns, choice).astype(BF16)
 
 
-def terms_kernel(w, p, t, pts, index, term0, send, keep, skel, lifted_weights):
+def pack_kernel(points, weights, out, done):
+    half = points.shape[1] // 2
+    rows = weights.shape[0]
+    copies = [
+        pltpu.make_async_copy(weights, out.at[0:rows, :], done.at[0]),
+        pltpu.make_async_copy(points.at[:, 0:half], out.at[rows : rows + 64, :], done.at[1]),
+        pltpu.make_async_copy(points.at[:, half : 2 * half], out.at[rows + 64 : rows + 128, :], done.at[2]),
+    ]
+    for copy in copies:
+        copy.start()
+    for copy in copies:
+        copy.wait()
+
+
+def terms_kernel(w, p, t, send, keep, lifted_weights):
     step = pl.program_id(0)
     core, _, _ = place()
 
     @pl.when(step == 0)
     def _():
-        lifted_weights[...] = dot(w[...], p[...], ((0,), (0,))).astype(BF16)
-        rank = lax.broadcasted_iota(jnp.int32, (pts.shape[1], index.shape[1]), 0)
-        choice = (rank == index[...]).astype(F32).astype(BF16)
-        chosen = dot(pts[...], choice).astype(BF16)
-        skel[...] = chosen
-        send[1024:1088, :] = chosen
-
-    @pl.when(step < 4)
-    def _():
-        row = pl.multiple_of(step * 256, 256)
-        theirs = pl.multiple_of((1 - core) * 256, 256)
-        mine = pl.multiple_of(core * 256, 256)
-        send[pl.ds(row, 256), :] = dot(lifted_weights[pl.ds(theirs, 256), :], t[0, 0]).astype(BF16)
-        keep[pl.ds(row, 256), :] = dot(lifted_weights[pl.ds(mine, 256), :], t[0, 0])
-
-    @pl.when(step == 4)
-    def _():
-        term0[...] = dot(lifted_weights[...], t[0, 0]).astype(BF16)
-
-
-def chip_kernel(keep, came, skel, to2, to4, to6, kept, pair, total):
+        lifted_weights[...] = dot(w[0:1024, :], p[...], ((0,), (0,))).astype(BF16)
+
+    row = pl.multiple_of(step * 256, 256)
+    theirs = pl.multiple_of((1 - core) * 256, 256)
+    mine = pl.multiple_of(core * 256, 256)
+    send[pl.ds(row, 256), :] = dot(lifted_weights[pl.ds(theirs, 256), :], t[0, 0]).astype(BF16)
+    keep[pl.ds(row, 256), :] = dot(lifted_weights[pl.ds(mine, 256), :], t[0, 0])
+
+
+def leaf_kernel(lifted_weights, t, payload, index, out):
+    size = payload.shape[0] - 128
+    out[0:512, :] = dot(lifted_weights[...], t[0, 0]).astype(BF16)
+    rank = lax.broadcasted_iota(jnp.int32, (size // 2, index.shape[1]), 0)
+    chosen = dot(payload[size : size + 64, :], (rank == index[...]).astype(F32).astype(BF16))
+    chosen = chosen + dot(payload[size + 64 : size + 128, :], (rank + size // 2 == index[...]).astype(F32).astype(BF16))
+    out[512:576, :] = chosen.astype(BF16)
+
+
+def chip_kernel(keep, came, mine, theirs, to1, to2, to4, to6, kept, pair, total):
     core, x, _ = place()
-    mine, theirs = skel[...], came[1024:1088, :]
+    mine, theirs = mine[512:576, :], theirs[512:576, :]
     first = jnp.where(core == 0, mine, theirs)
     second = jnp.where(core == 0, theirs, mine)
     pair[0:64, :] = first
     pair[64:128, :] = second
-    total[...] = keep[...] + came[0:1024, :].astype(F32)
-    to2[0:256, :] = total[0:256, :].astype(BF16)
-    to2[384:448, :] = jnp.concatenate([first[:, :256], second[:, :256]], axis=1)
+    total[...] = keep[...] + came[...].astype(F32)
+    to1[...] = total[0:256, :].astype(BF16)
+    to2[128:192, :] = jnp.concatenate([first[:, :256], second[:, :256]], axis=1)
     for level, at in ((3, 0), (4, 64)):
-        for out, row, other in ((to2, 256, x ^ 1), (to4, 128, x ^ 2), (to6, 128, x ^ 3)):
+        for out, row, other in ((to2, 0, x ^ 1), (to4, 128, x ^ 2), (to6, 128, x ^ 3)):
             rows = pl.ds(pl.multiple_of((level - 1) * 256 + other * 64, 64), 64)
             out[row + at : row + at + 64, :] = total[rows, :].astype(BF16)
         kept[at : at + 64, :] = total[pl.ds(pl.multiple_of((level - 1) * 256 + x * 64, 64), 64), :]
@@ -134,14 +153,14 @@
 
 def row_kernel(from2, from4, from6, kept, pair, to8, to16, ring):
     _, x, _ = place()
-    near = from2[384:448, :]
+    near = from2[128:192, :]
     ring[x] = jnp.concatenate([pair[0:64, 0:128], pair[64:128, 0:128]], axis=1)
     ring[x ^ 1] = jnp.concatenate([near[:, 0:128], near[:, 256:384]], axis=1)
     ring[x ^ 2] = unpack(from4[256:288, :])
     ring[x ^ 3] = unpack(from6[256:288, :])
     points3 = picked(jnp.concatenate([ring[k] for k in range(4)], axis=1), 512, 128, 64)
     for out, at in ((to8, 0), (to16, 64)):
-        total = kept[at : at + 64, :] + from2[256 + at : 320 + at, :].astype(F32)
+        total = kept[at : at + 64, :] + from2[at : 64 + at, :].astype(F32)
         total = total + from4[128 + at : 192 + at, :].astype(F32) + from6[128 + at : 192 + at, :].astype(F32)
         out[0:64, :] = total.astype(BF16)
     to8[64:128, :] = points3
@@ -152,17 +171,20 @@
     return dot(sums, gaussian(lifted(sibling, True), lifted(own, False))).astype(BF16)
 
 
-def couple_low_kernel(term0, from2, from4, from6, pair, ring, out0, out1, out2):
+def couple_low_kernel(term0, from4, from6, pair, ring, out0, out2):
     core, x, _ = place()
     first, second = pair[0:64, :], pair[64:128, :]
-    out0[...] = couple(term0[...], jnp.where(core == 0, first, second), jnp.where(core == 0, second, first))
-    own = jnp.concatenate([first[:, :256], second[:, :256]], axis=1)
-    out1[...] = couple(from2[0:256, :], own, from2[384:448, :])
+    out0[...] = couple(term0[0:512, :], jnp.where(core == 0, first, second), jnp.where(core == 0, second, first))
     low = x & 2
     own = jnp.concatenate([ring[low], ring[low | 1]], axis=1)
     sibling = jnp.concatenate([ring[low ^ 2], ring[(low ^ 2) | 1]], axis=1)
     sums = (from4[0:128, :].astype(F32) + from6[0:128, :].astype(F32)).astype(BF16)
     out2[...] = couple(sums, own, sibling)
+
+
+def couple_chip_kernel(sums, from2, pair, out1):
+    own = jnp.concatenate([pair[0:64, 0:256], pair[64:128, 0:256]], axis=1)
+    out1[...] = couple(sums[...], own, from2[128:192, :])
 
 
 def couple_high_kernel(from8, from16, from24, to8, to16, coupled2, out2, out4):
@@ -197,7 +219,8 @@
     mask, own = refs[0], refs[1]
     blocks = refs[2 : 2 + count]
     total = refs[2 + count] if with_total else None
-    out = refs[-1]
+    out, token = refs[-2], refs[-1]
+    token[...] = jnp.zeros_like(token)
     core, _, _ = place()
     size = own.shape[1]
     left = lifted(own[...], True)
@@ -221,7 +244,7 @@
         out[rows, :] = result[k] + total[rows, :] if with_total else result[k]
 
 
-def near(mask, points, blocks, slots, total, name):
+def near(mask, points, blocks, slots, total, name, after):
     args = [mask, points, *blocks] + ([] if total is None else [total])
     size, width = points.shape[1], blocks[0].shape[1]
 
@@ -229,19 +252,27 @@
         near_kernel(len(blocks), slots, total is not None, *refs)
 
     flops = 2 * len(blocks) * size * size * (width + 256)
-    return call(body, name, [((size, width), F32)], args, flops, smem=(0,))[0]
-
-
-def product_kernel(total, interp, transfers, coupled0, mine, theirs, out, far):
+    return call(body, name, [((size, width), F32), ((8, 128), F32)], args, flops, smem=(0,), after=after)
+
+
+def add_levels(far, transfers, half, part):
+    columns = pl.ds(pl.multiple_of(part * 256, 256), 256)
+    value = far[:, columns]
+    for level in range(1, 5):
+        value = value + dot(transfers[0, level], half[(level - 1) * 256 : level * 256, :], ((1,), (1,)))
+    far[:, columns] = value
+
+
+def far_kernel(transfers, coupled0, mine, far):
     core, _, _ = place()
-    base = dot(transfers[0, 0], coupled0[...], ((1,), (1,)))
-    far[...] = base
-    for part, half in ((core, mine), (1 - core, theirs)):
-        columns = pl.ds(pl.multiple_of(part * 256, 256), 256)
-        value = far[:, columns]
-        for level in range(1, 5):
-            value = value + dot(transfers[0, level], half[(level - 1) * 256 : level * 256, :], ((1,), (1,)))
-        far[:, columns] = value
+    far[...] = dot(transfers[0, 0], coupled0[...], ((1,), (1,)))
+    add_levels(far, transfers, mine, core)
+
+
+def product_kernel(total, interp, transfers, begun, theirs, out, far):
+    core, _, _ = place()
+    far[...] = begun[...]
+    add_levels(far, transfers, theirs, 1 - core)
     skeleton = far[...].astype(BF16)
     for k in range(total.shape[0] // ROWS):
         rows = slice(k * ROWS, (k + 1) * ROWS)
@@ -259,76 +290,113 @@
         pairs = [(leaf, leaf + (odd if leaf & 1 else even)) for leaf in range(leaves)]
         return lax.ppermute(value, AXIS, [(a, b) for a, b in pairs if 0 <= b < leaves])
 
-    payload = jnp.concatenate([weights, points[:, : size // 2], points[:, size // 2 :]], axis=0)
+    def rows(count, dtype=BF16):
+        return (count, 512), dtype
+
+    def whole(*shape):
+        return pl.BlockSpec(shape, lambda g: (0,) * len(shape))
+
+    def near_of(blocks, slots, total, name, after):
+        return near(near_mask, points, blocks, slots, total, name, after)
+
+    (payload,) = call(
+        pack_kernel,
+        "pack",
+        [rows(size + 128)],
+        [points, weights],
+        0,
+        scratch=[pltpu.SemaphoreType.DMA((3,))],
+        in_specs=[pl.BlockSpec(memory_space=pl.ANY)] * 2,
+    )
     outer = moved(payload, -1, 1)
+    second = moved(payload, 2, -2)
     partner = swap(payload, 1)
-
-    whole = lambda *shape: pl.BlockSpec(shape, lambda g: (0,) * len(shape))
-    term0, send, keep, skel = call(
+    send, keep, lifted_weights = call(
         terms_kernel,
         "terms",
-        [((512, 512), BF16), ((1088, 512), BF16), ((1024, 512), F32), ((64, 512), BF16)],
-        [weights, interp, transfers, points, skel_index],
-        2 * 512 * 512 * (1024 + 5 * 512),
-        scratch=[pltpu.VMEM((512, 512), BF16)],
-        grid=(5,),
+        [rows(1024), rows(1024, F32), rows(512)],
+        [payload, interp, transfers],
+        2 * 512 * 512 * (1024 + 4 * 512),
+        grid=(4,),
         in_specs=[
-            whole(size, width),
+            whole(size + 128, width),
             whole(size, 512),
-            pl.BlockSpec((1, 1, 512, 512), lambda g: (0, lax.rem(g + 1, 5), 0, 0)),
-            whole(64, size),
+            pl.BlockSpec((1, 1, 512, 512), lambda g: (0, g + 1, 0, 0)),
+        ],
+    )
+    came = swap(send, 1)
+    (term0,) = call(
+        leaf_kernel,
+        "leaf",
+        [rows(576)],
+        [lifted_weights, transfers, payload, skel_index],
+        2 * 512 * 512 * 768,
+        grid=(1,),
+        in_specs=[
+            whole(512, 512),
+            pl.BlockSpec((1, 1, 512, 512), lambda g: (0, 0, 0, 0)),
+            whole(size + 128, width),
             whole(1, 512),
         ],
     )
-    came = swap(send, 1)
-    term0 = swap(term0, 1)
-    total = near(near_mask, points, [weights, partner], [None, (2, 1)], None, "near_own")
-
-    to2, to4, to6, kept, pair = call(
+    other0 = swap(term0, 1)
+    total, token = near_of([payload, partner], [None, (2, 1)], None, "near_own", (term0,))
+
+    to1, to2, to4, to6, kept, pair = call(
         chip_kernel,
         "chip",
-        [((448, 512), BF16), ((288, 512), BF16), ((288, 512), BF16), ((128, 512), F32), ((128, 512), BF16)],
-        [keep, came, skel],
+        [rows(256), rows(192), rows(288), rows(288), rows(128, F32), rows(128)],
+        [keep, came, term0, other0],
         1e6,
+        after=(token,),
         scratch=[pltpu.VMEM((1024, 512), F32)],
     )
     from2, from4, from6 = swap(to2, 2), swap(to4, 4), swap(to6, 6)
-    past = swap(outer, 1)
-    second = moved(payload, 2, -2)
-
+    total, token = near_of([outer], [(1, 2)], total, "near_outer", (pair,))
+
+    total, token = near_of([second], [(0, 3)], total, "near_second", (token,))
     to8, to16, ring = call(
         row_kernel,
         "row",
-        [((128, 512), BF16), ((96, 512), BF16), ((4, 64, 256), BF16)],
+        [rows(128), rows(96), ((4, 64, 256), BF16)],
         [from2, from4, from6, kept, pair],
         1e8,
+        after=(token,),
     )
     from8, from16, from24 = swap(to8, 8), swap(to16, 16), swap(to16, 24)
-    coupled0, coupled1, coupled2 = call(
+    to1, outer, ring = lax.optimization_barrier((to1, outer, ring))
+    from1 = swap(to1, 2)
+    past = swap(outer, 1)
+    coupled0, coupled2 = call(
         couple_low_kernel,
         "couple_low",
-        [((512, 512), BF16), ((256, 512), BF16), ((128, 512), BF16)],
-        [term0, from2, from4, from6, pair, ring],
-        2 * 512 * 512 * (3 * 256 + 896),
-    )
-    total = near(near_mask, points, [outer, past], [(1, 2), (3, 0)], total, "near_outer")
+        [rows(512), rows(128)],
+        [other0, from4, from6, pair, ring],
+        40 * 512 * 512 * (2 * 256 + 640),
+    )
     part2, part4 = call(
         couple_high_kernel,
         "couple_high",
-        [((256, 512), BF16), ((128, 512), BF16)],
+        [rows(256), rows(128)],
         [from8, from16, from24, to8, to16, coupled2],
         2 * 512 * 512 * (2 * 256 + 128),
     )
     back2, back4, back6 = swap(part2, 2), swap(part4, 4), swap(part4, 6)
-    (mine,) = call(half_kernel, "half", [((1024, 512), BF16)], [coupled1, part2, back2, back4, back6], 1e6)
+    (coupled1,) = call(
+        couple_chip_kernel, "couple_chip", [rows(256)], [from1, from2, pair], 2 * 512 * 512 * 512, after=(part4,)
+    )
+    total, token = near_of([past], [(3, 0)], total, "near_past", (coupled1,))
+    (mine,) = call(
+        half_kernel, "half", [rows(1024)], [coupled1, part2, back2, back4, back6], 1e6, after=(token,)
+    )
     theirs = swap(mine, 1)
-    total = near(near_mask, points, [second], [(0, 3)], total, "near_second")
+    (far,) = call(far_kernel, "far", [rows(512, F32)], [transfers, coupled0, mine], 2 * 512 * 512 * 5 * 400)
     return call(
         product_kernel,
         "product",
         [((size, width), BF16)],
-        [total, interp, transfers, coupled0, mine, theirs],
-        2 * 512 * 512 * (5 * 512 + 1024),
+        [total, interp, transfers, far, theirs],
+        2 * 512 * 512 * (4 * 256 + 1024),
         scratch=[pltpu.VMEM((512, 512), F32)],
     )[0]
 

time: 109 us -> 78.3 us (0.72); the launches traced: 106 us -> 78.1 us
  waiting for transfers between devices: 48.4 us -> 27.8 us
  starting transfers between devices: 26.9 us -> 23.3 us
  Pallas kernels: 25.5 us -> 22.6 us
  local copies, waits for them, and re-layouts: 5.41 us -> 4.13 us
    ppermute x14 -> x15, waiting for transfers between devices: 33.8 us -> 10.4 us  [swap(): lax.ppermute(value, AXIS, [(leaf, leaf ^ mask) for leaf in range(leaves)])]
    pallas_call x10 -> x15, Pallas kernels: 25.5 us -> 22.6 us  [call(): pl.pallas_call(reading, name=name, grid=grid or (), in_specs=specs, out_s...]
    ppermute x2, waiting for transfers between devices: 14.6 us -> 17.4 us  [moved(): lax.ppermute(value, AXIS, [(a, b) for a, b in pairs if 0 <= b < leaves])]
    ppermute x14 -> x15, starting transfers between devices: 20.6 us -> 17.8 us  [swap(): lax.ppermute(value, AXIS, [(leaf, leaf ^ mask) for leaf in range(leaves)])]
    unnamed x18 -> x16, local copies, waits for them, and re-layouts: 5.4 us -> 4.13 us
  transfers between devices with their start and end apart: 16 -> 17, of which waited for: 5 -> 7; matrix products, arithmetic and copies ran while one was open for 0% -> 0% of each run, Pallas kernels for 14% -> 24%
where the time goes in v2:
time: 78.3 us; the launch traced here: 78.1 us
  waiting for transfers between devices  27.8 us (36%)
  starting transfers between devices  23.3 us (30%)
  Pallas kernels  22.6 us (29%)
  local copies, waits for them, and re-layouts  4.13 us (5%)
    pallas_call x15, Pallas kernels, call(): pl.pallas_call(reading, name=name, grid=grid or (), in_specs=specs, out_s...  22.6 us
    ppermute x15, starting transfers between devices, swap(): lax.ppermute(value, AXIS, [(leaf, leaf ^ mask) for leaf in range(leaves)])  17.8 us
    ppermute x2, waiting for transfers between devices, moved(): lax.ppermute(value, AXIS, [(a, b) for a, b in pairs if 0 <= b < leaves])  17.4 us
    ppermute x15, waiting for transfers between devices, swap(): lax.ppermute(value, AXIS, [(leaf, leaf ^ mask) for leaf in range(leaves)])  10.4 us
    ppermute x2, starting transfers between devices, moved(): lax.ppermute(value, AXIS, [(a, b) for a, b in pairs if 0 <= b < leaves])  5.46 us
    unnamed x16, local copies, waits for them, and re-layouts  4.13 us
  transfers between devices with their start and end apart: 17, of which 7 were waited for; matrix products, arithmetic and copies ran while one was open for 0% of the time, Pallas kernels for 24%

profile of v2, /device:TPU:25, one launch (start us, length us, event | category | flops | bytes accessed | tf_op | source)
XLA Modules:
  0.0 78.1 jit_solution(1624598887789658026)
XLA Ops:
  0.0 0.0 copy-start.2
  0.0 0.0 copy-start.3
  0.0 1.3 %copy-done.3 = bf16[1024,512]{1,0:T(8,128)(2,1)S(1)} copy-done((bf16[1024,512]{1,0:T(8,128)(2,1)S(1)}, bf16[1024,512]{1,0:T(8,128)(2,1)}, u32[]{:S(2)}) %copy-start.3) | copy-done | bytes 1048600
  1.3 0.0 copy-start.4
  1.3 0.9 %copy-done.4 = bf16[64,1024]{1,0:T(8,128)(2,1)S(1)} copy-done((bf16[64,1024]{1,0:T(8,128)(2,1)S(1)}, bf16[64,1024]{1,0:T(8,128)(2,1)}, u32[]{:S(2)}) %copy-start.4) | copy-done | bytes 131096
  2.2 0.0 copy-start.6
  2.2 0.1 pack.1.refs_0_.refs_2_
  2.4 0.8 collective-permute-start.2
  3.1 3.0 %collective-permute-start.3 = (bf16[1152,512]{1,0:T(8,128)(2,1)S(1)}, bf16[1152,512]{1,0:T(8,128)(2,1)S(1)}, u32[]{:S(2)}, u32[]{:S(2)}) collective-permute-start(bf16[1152,512]{1,0:T(8,128)(2,1)S(1)} %pack.1.refs_0_.refs_2_), channel_id=1, source_target_pairs={{1,2},{2,1},{3,4},{4,3},{5,6},{6,5},{7,8},{8,7},{9,10},{10,9},{11,... | collective-permute-start | bytes 3538952 | tf_op jit(solution)/shard_map/ppermute | solution.py:291
  6.1 0.0 copy-done.2
  6.1 0.0 copy-start
  6.2 1.7 %copy-done = bf16[1,5,512,512]{3,2,1,0:T(8,128)(2,1)S(1)} copy-done((bf16[1,5,512,512]{3,2,1,0:T(8,128)(2,1)S(1)}, bf16[1,5,512,512]{3,2,1,0:T(8,128)(2,1)}, u32[]{:S(2)}) %copy-start) | copy-done | bytes 2621464
  7.9 2.5 %terms.1 = (bf16[1024,512]{1,0:T(8,128)(2,1)S(1)}, f32[1024,512]{1,0:T(8,128)S(1)}, bf16[512,512]{1,0:T(8,128)(2,1)S(1)}) custom-call(bf16[1152,512]{1,0:T(8,128)(2,1)S(1)} %pack.1.refs_0_.refs_2_, bf16[1024,512]{1,0:T(8,128)(2,1)S(1)} %copy-done.2, bf16[1,5,512,512]{3,2,1,0:T(8,128)(2,1)S(1)} %copy-done), custom_call_target="tpu_custom_call" | custom-call | flops 1610612736 | bytes 8519680 | tf_op jit(solution)/shard_map/terms/pallas_call | solution.py:67
  10.4 5.5 %collective-permute-start = (bf16[1024,512]{1,0:T(8,128)(2,1)S(1)}, bf16[1024,512]{1,0:T(8,128)(2,1)S(1)}, u32[]{:S(2)}, u32[]{:S(2)}) collective-permute-start(bf16[1024,512]{1,0:T(8,128)(2,1)S(1)} %get-tuple-element.33), channel_id=1, source_target_pairs={{0,1},{1,0},{2,3},{3,2},{4,5},{5,4},{6,7},{7,6},{8,9},{9,8},{10,11... | collective-permute-start | bytes 3145736 | tf_op jit(solution)/shard_map/ppermute | solution.py:287
  15.9 2.4 %collective-permute-start.7 = (bf16[1152,512]{1,0:T(8,128)(2,1)S(1)}, bf16[1152,512]{1,0:T(8,128)(2,1)S(1)}, u32[]{:S(2)}, u32[]{:S(2)}) collective-permute-start(bf16[1152,512]{1,0:T(8,128)(2,1)S(1)} %pack.1.refs_0_.refs_2_), channel_id=1, source_target_pairs={{0,2},{2,4},{3,1},{4,6},{5,3},{6,8},{7,5},{8,10},{9,7},{10,12},{11... | collective-permute-start | bytes 3538952 | tf_op jit(solution)/shard_map/ppermute | solution.py:291
  18.3 0.0 copy-done.6
  18.4 0.0 copy-done.1
  18.4 0.0 copy-start.5
  18.4 0.0 copy-start.7
  18.4 0.6 leaf.1.refs_4_.refs_2_
  19.0 0.1 collective-permute-start.1
  19.1 0.0 collective-permute-done.2.refs_3_
  19.1 0.2 copy-done.5
  19.3 0.0 copy-done.7
  19.3 4.0 %near_own.1 = (f32[1024,512]{1,0:T(8,128)S(1)}, f32[8,128]{1,0:T(8,128)S(1)}) custom-call(s32[1,4]{1,0:T(1,128)S(1)} %copy-done.7, bf16[64,1024]{1,0:T(8,128)(2,1)S(1)} %copy-done.5, bf16[1152,512]{1,0:T(8,128)(2,1)S(1)} %pack.1.refs_0_.refs_2_, bf16[1152,512]{1,0:T(8,128)(2,1)S(1)} %collective-permute-done.2.refs_3_, bf16[576,512]{1,0:T(8,128)(2,1)S(1)} %leaf.1.refs_4_.refs_2_), custom_call_target="tpu_custom_call" | custom-call | flops 3221225472 | bytes 4591632 | tf_op jit(solution)/shard_map/near_own/pallas_call | solution.py:67
  23.3 0.0 collective-permute-done.1.refs_3_.refs_0_
  23.3 0.0 collective-permute-done.refs_1_
  23.3 0.4 chip.1
  23.7 0.1 collective-permute-start.5
  23.8 3.3 %collective-permute-start.6 = (bf16[288,512]{1,0:T(8,128)(2,1)S(1)}, bf16[288,512]{1,0:T(8,128)(2,1)S(1)}, u32[]{:S(2)}, u32[]{:S(2)}) collective-permute-start(bf16[288,512]{1,0:T(8,128)(2,1)S(1)} %get-tuple-element.39), channel_id=1, source_target_pairs={{0,6},{1,7},{2,4},{3,5},{4,2},{5,3},{6,0},{7,1},{8,14},{9,15},{10,... | collective-permute-start | bytes 884744 | tf_op jit(solution)/shard_map/ppermute | solution.py:287
  27.1 0.0 collective-permute-start.4
  27.1 0.0 collective-permute-done.3.refs_2_
  27.1 2.4 %near_outer.1 = (f32[1024,512]{1,0:T(8,128)S(1)}, f32[8,128]{1,0:T(8,128)S(1)}) custom-call(s32[1,4]{1,0:T(1,128)S(1)} %copy-done.7, bf16[64,1024]{1,0:T(8,128)(2,1)S(1)} %copy-done.5, bf16[1152,512]{1,0:T(8,128)(2,1)S(1)} %collective-permute-done.3.refs_2_, f32[1024,512]{1,0:T(8,128)S(1)} %get-tuple-element.42.refs_3_, ...), custom_call_target="tpu_custom_call" | custom-call | flops 1610612736 | bytes 5509136 | tf_op jit(solution)/shard_map/near_outer/pallas_call | solution.py:67
  29.5 17.4 %collective-permute-done.7.refs_2_ = bf16[1152,512]{1,0:T(8,128)(2,1)S(1)} collective-permute-done((bf16[1152,512]{1,0:T(8,128)(2,1)S(1)}, bf16[1152,512]{1,0:T(8,128)(2,1)S(1)}, u32[]{:S(2)}, u32[]{:S(2)}) %collective-permute-start.7) | collective-permute-done | bytes 1179680 | tf_op jit(solution)/shard_map/ppermute | solution.py:291
  47.0 2.4 %near_second.1 = (f32[1024,512]{1,0:T(8,128)S(1)}, f32[8,128]{1,0:T(8,128)S(1)}) custom-call(s32[1,4]{1,0:T(1,128)S(1)} %copy-done.7, bf16[64,1024]{1,0:T(8,128)(2,1)S(1)} %copy-done.5, bf16[1152,512]{1,0:T(8,128)(2,1)S(1)} %collective-permute-done.7.refs_2_, f32[1024,512]{1,0:T(8,128)S(1)} %get-tuple-element.43.refs_3_, f32[8,128]{1,0:T(8,128)S(1)} %get-tuple-element.44.refs_4_), custom_call_target="tpu_custom_call" | custom-call | flops 1610612736 | bytes 5509136 | tf_op jit(solution)/shard_map/near_second/pallas_call | solution.py:67
  49.4 0.0 collective-permute-done.4.refs_0_.refs_1_
  49.4 0.0 collective-permute-done.5.refs_1_
  49.4 0.7 collective-permute-done.6.refs_2_
  50.1 0.5 row.1
  50.6 0.1 collective-permute-start.11
  50.7 0.1 collective-permute-start.12
  50.8 2.5 %collective-permute-start.10 = (bf16[128,512]{1,0:T(8,128)(2,1)S(1)}, bf16[128,512]{1,0:T(8,128)(2,1)S(1)}, u32[]{:S(2)}, u32[]{:S(2)}) collective-permute-start(bf16[128,512]{1,0:T(8,128)(2,1)S(1)} %get-tuple-element.50.refs_3_), channel_id=1, source_target_pairs={{0,8},{1,9},{2,10},{3,11},{4,12},{5,13},{6,14},{7,15},{8,0},{9,1},... | collective-permute-start | bytes 393224 | tf_op jit(solution)/shard_map/ppermute | solution.py:287
  53.4 0.0 collective-permute-start.9
  53.4 0.9 %collective-permute-start.8 = (bf16[1152,512]{1,0:T(8,128)(2,1)S(1)}, bf16[1152,512]{1,0:T(8,128)(2,1)S(1)}, u32[]{:S(2)}, u32[]{:S(2)}) collective-permute-start(bf16[1152,512]{1,0:T(8,128)(2,1)S(1)} %collective-permute-done.3.refs_2_), channel_id=1, source_target_pairs={{0,1},{1,0},{2,3},{3,2},{4,5},{5,4},{6,7},{7,6},{8,9},{9,8},{10,11... | collective-permute-start | bytes 3538952 | tf_op jit(solution)/shard_map/ppermute | solution.py:287
  54.2 1.0 %couple_low.1 = (bf16[512,512]{1,0:T(8,128)(2,1)S(1)}, bf16[128,512]{1,0:T(8,128)(2,1)S(1)}) custom-call(bf16[576,512]{1,0:T(8,128)(2,1)S(1)} %collective-permute-done.1.refs_3_.refs_0_, bf16[288,512]{1,0:T(8,128)(2,1)S(1)} %collective-permute-done.5.refs_1_, bf16[288,512]{1,0:T(8,128)(2,1)S(1)} %collective-permute-done.6.refs_2_, ...), custom_call_target="tpu_custom_call" | custom-call | flops 12079595520 | bytes 2097152 | tf_op jit(solution)/shard_map/couple_low/pallas_call | solution.py:67
  55.3 1.4 %collective-permute-done.11.refs_1_ = bf16[96,512]{1,0:T(8,128)(2,1)S(1)} collective-permute-done((bf16[96,512]{1,0:T(8,128)(2,1)S(1)}, bf16[96,512]{1,0:T(8,128)(2,1)S(1)}, u32[]{:S(2)}, u32[]{:S(2)}) %collective-permute-start.11) | collective-permute-done | bytes 98336 | tf_op jit(solution)/shard_map/ppermute | solution.py:287
  56.7 1.8 %collective-permute-done.12.refs_2_ = bf16[96,512]{1,0:T(8,128)(2,1)S(1)} collective-permute-done((bf16[96,512]{1,0:T(8,128)(2,1)S(1)}, bf16[96,512]{1,0:T(8,128)(2,1)S(1)}, u32[]{:S(2)}, u32[]{:S(2)}) %collective-permute-start.12) | collective-permute-done | bytes 98336 | tf_op jit(solution)/shard_map/ppermute | solution.py:287
  58.4 0.0 collective-permute-done.10.refs_0_
  58.4 1.0 %couple_high.1 = (bf16[256,512]{1,0:T(8,128)(2,1)S(1)}, bf16[128,512]{1,0:T(8,128)(2,1)S(1)}) custom-call(bf16[128,512]{1,0:T(8,128)(2,1)S(1)} %collective-permute-done.10.refs_0_, bf16[96,512]{1,0:T(8,128)(2,1)S(1)} %collective-permute-done.11.refs_1_, bf16[96,512]{1,0:T(8,128)(2,1)S(1)} %collective-permute-done.12.refs_2_, ...), custom_call_target="tpu_custom_call" | custom-call | flops 335544320 | bytes 1081344 | tf_op jit(solution)/shard_map/couple_high/pallas_call | solution.py:67
  59.4 0.1 collective-permute-start.13
  59.5 2.7 %collective-permute-start.14 = (bf16[128,512]{1,0:T(8,128)(2,1)S(1)}, bf16[128,512]{1,0:T(8,128)(2,1)S(1)}, u32[]{:S(2)}, u32[]{:S(2)}) collective-permute-start(bf16[128,512]{1,0:T(8,128)(2,1)S(1)} %get-tuple-element.54.refs_3_), channel_id=1, source_target_pairs={{0,4},{1,5},{2,6},{3,7},{4,0},{5,1},{6,2},{7,3},{8,12},{9,13},{10,... | collective-permute-start | bytes 393224 | tf_op jit(solution)/shard_map/ppermute | solution.py:287
  62.2 1.2 %collective-permute-start.15 = (bf16[128,512]{1,0:T(8,128)(2,1)S(1)}, bf16[128,512]{1,0:T(8,128)(2,1)S(1)}, u32[]{:S(2)}, u32[]{:S(2)}) collective-permute-start(bf16[128,512]{1,0:T(8,128)(2,1)S(1)} %get-tuple-element.54.refs_3_), channel_id=1, source_target_pairs={{0,6},{1,7},{2,4},{3,5},{4,2},{5,3},{6,0},{7,1},{8,14},{9,15},{10,... | collective-permute-start | bytes 393224 | tf_op jit(solution)/shard_map/ppermute | solution.py:287
  63.4 0.0 collective-permute-done.9.refs_0_
  63.4 0.6 couple_chip.1.refs_4_.refs_0_
  64.0 0.0 collective-permute-done.8.refs_2_
  64.0 2.5 %near_past.1 = (f32[1024,512]{1,0:T(8,128)S(1)}, f32[8,128]{1,0:T(8,128)S(1)}) custom-call(s32[1,4]{1,0:T(1,128)S(1)} %copy-done.7, bf16[64,1024]{1,0:T(8,128)(2,1)S(1)} %copy-done.5, bf16[1152,512]{1,0:T(8,128)(2,1)S(1)} %collective-permute-done.8.refs_2_, f32[1024,512]{1,0:T(8,128)S(1)} %get-tuple-element.48.refs_3_, ...), custom_call_target="tpu_custom_call" | custom-call | flops 1610612736 | bytes 5509136 | tf_op jit(solution)/shard_map/near_past/pallas_call | solution.py:67
  66.4 4.2 %collective-permute-done.14.refs_3_ = bf16[128,512]{1,0:T(8,128)(2,1)S(1)} collective-permute-done((bf16[128,512]{1,0:T(8,128)(2,1)S(1)}, bf16[128,512]{1,0:T(8,128)(2,1)S(1)}, u32[]{:S(2)}, u32[]{:S(2)}) %collective-permute-start.14) | collective-permute-done | bytes 131104 | tf_op jit(solution)/shard_map/ppermute | solution.py:287
  70.6 1.0 %collective-permute-done.15.refs_4_ = bf16[128,512]{1,0:T(8,128)(2,1)S(1)} collective-permute-done((bf16[128,512]{1,0:T(8,128)(2,1)S(1)}, bf16[128,512]{1,0:T(8,128)(2,1)S(1)}, u32[]{:S(2)}, u32[]{:S(2)}) %collective-permute-start.15) | collective-permute-done | bytes 131104 | tf_op jit(solution)/shard_map/ppermute | solution.py:287
  71.6 0.0 collective-permute-done.13.refs_2_
  71.6 0.1 half.1.refs_2_
  71.7 0.6 collective-permute-start.16
  72.3 1.0 %far.1.refs_3_ = f32[512,512]{1,0:T(8,128)S(1)} custom-call(bf16[1,5,512,512]{3,2,1,0:T(8,128)(2,1)S(1)} %copy-done.1, bf16[512,512]{1,0:T(8,128)(2,1)S(1)} %get-tuple-element.56.refs_1_, bf16[1024,512]{1,0:T(8,128)(2,1)S(1)} %half.1.refs_2_), custom_call_target="tpu_custom_call" | custom-call | flops 1048576000 | bytes 5242880 | tf_op jit(solution)/shard_map/far/pallas_call | solution.py:67
  73.3 1.3 %collective-permute-done.16.refs_4_ = bf16[1024,512]{1,0:T(8,128)(2,1)S(1)} collective-permute-done((bf16[1024,512]{1,0:T(8,128)(2,1)S(1)}, bf16[1024,512]{1,0:T(8,128)(2,1)S(1)}, u32[]{:S(2)}, u32[]{:S(2)}) %collective-permute-start.16) | collective-permute-done | bytes 1048608 | tf_op jit(solution)/shard_map/ppermute | solution.py:287
  74.6 3.5 %product.1 = bf16[1024,512]{1,0:T(8,128)(2,1)} custom-call(f32[1024,512]{1,0:T(8,128)S(1)} %get-tuple-element.55.refs_0_, bf16[1024,512]{1,0:T(8,128)(2,1)S(1)} %copy-done.2, bf16[1,5,512,512]{3,2,1,0:T(8,128)(2,1)S(1)} %copy-done.1, f32[512,512]{1,0:T(8,128)S(1)} %far.1.refs_3_, bf16[1024,512]{1,0:T(8,128)(2,1)S(1)} %collective-permute-done.16.refs_4_), custom_call_target="tpu_custom_call" | custom-call | flops 1073741824 | bytes 8912896 | tf_op jit(solution)/shard_map/product/pallas_call | solution.py:67
  (1 shorter events, 0.0 us)
Async XLA Ops:
  0.0 6.1 %copy-start.2 = (bf16[1024,512]{1,0:T(8,128)(2,1)S(1)}, bf16[1024,512]{1,0:T(8,128)(2,1)}, u32[]{:S(2)}) copy-start(bf16[1024,512]{1,0:T(8,128)(2,1)} %refs_1_.15) | copy-start | bytes 3145732
  0.0 1.3 %copy-start.3 = (bf16[1024,512]{1,0:T(8,128)(2,1)S(1)}, bf16[1024,512]{1,0:T(8,128)(2,1)}, u32[]{:S(2)}) copy-start(bf16[1024,512]{1,0:T(8,128)(2,1)} %refs_1_.8) | copy-start | bytes 3145732
  1.3 0.9 %copy-start.4 = (bf16[64,1024]{1,0:T(8,128)(2,1)S(1)}, bf16[64,1024]{1,0:T(8,128)(2,1)}, u32[]{:S(2)}) copy-start(bf16[64,1024]{1,0:T(8,128)(2,1)} %refs_1_.14) | copy-start | bytes 393220
  2.2 16.1 %copy-start.6 = (s32[1,512]{1,0:T(1,128)S(1)}, s32[1,512]{1,0:T(1,128)}, u32[]{:S(2)}) copy-start(s32[1,512]{1,0:T(1,128)} %refs_3_.1) | copy-start | bytes 6148
  2.4 16.8 %collective-permute-start.2 = (bf16[1152,512]{1,0:T(8,128)(2,1)S(1)}, bf16[1152,512]{1,0:T(8,128)(2,1)S(1)}, u32[]{:S(2)}, u32[]{:S(2)}) collective-permute-start(bf16[1152,512]{1,0:T(8,128)(2,1)S(1)} %pack.1.refs_0_.refs_2_), channel_id=1, source_target_pairs={{0,1},{1,0},{2,3},{3,2},{4,5},{5,4},{6,7},{7,6},{8,9},{9,8},{10,11... | collective-permute-start | bytes 3538952 | tf_op jit(solution)/shard_map/ppermute | solution.py:287
  3.1 24.0 %collective-permute-start.3 = (bf16[1152,512]{1,0:T(8,128)(2,1)S(1)}, bf16[1152,512]{1,0:T(8,128)(2,1)S(1)}, u32[]{:S(2)}, u32[]{:S(2)}) collective-permute-start(bf16[1152,512]{1,0:T(8,128)(2,1)S(1)} %pack.1.refs_0_.refs_2_), channel_id=1, source_target_pairs={{1,2},{2,1},{3,4},{4,3},{5,6},{6,5},{7,8},{8,7},{9,10},{10,9},{11,... | collective-permute-start | bytes 3538952 | tf_op jit(solution)/shard_map/ppermute | solution.py:291
  6.1 1.7 %copy-start = (bf16[1,5,512,512]{3,2,1,0:T(8,128)(2,1)S(1)}, bf16[1,5,512,512]{3,2,1,0:T(8,128)(2,1)}, u32[]{:S(2)}) copy-start(bf16[1,5,512,512]{3,2,1,0:T(8,128)(2,1)} %refs_2_.3) | copy-start | bytes 7864324
  7.9 10.5 %copy-start.1 = (bf16[1,5,512,512]{3,2,1,0:T(8,128)(2,1)S(1)}, bf16[1,5,512,512]{3,2,1,0:T(8,128)(2,1)}, u32[]{:S(2)}) copy-start(bf16[1,5,512,512]{3,2,1,0:T(8,128)(2,1)} %refs_2_.3) | copy-start | bytes 7864324
  10.4 12.9 %collective-permute-start = (bf16[1024,512]{1,0:T(8,128)(2,1)S(1)}, bf16[1024,512]{1,0:T(8,128)(2,1)S(1)}, u32[]{:S(2)}, u32[]{:S(2)}) collective-permute-start(bf16[1024,512]{1,0:T(8,128)(2,1)S(1)} %get-tuple-element.33), channel_id=1, source_target_pairs={{0,1},{1,0},{2,3},{3,2},{4,5},{5,4},{6,7},{7,6},{8,9},{9,8},{10,11... | collective-permute-start | bytes 3145736 | tf_op jit(solution)/shard_map/ppermute | solution.py:287
  15.9 31.1 %collective-permute-start.7 = (bf16[1152,512]{1,0:T(8,128)(2,1)S(1)}, bf16[1152,512]{1,0:T(8,128)(2,1)S(1)}, u32[]{:S(2)}, u32[]{:S(2)}) collective-permute-start(bf16[1152,512]{1,0:T(8,128)(2,1)S(1)} %pack.1.refs_0_.refs_2_), channel_id=1, source_target_pairs={{0,2},{2,4},{3,1},{4,6},{5,3},{6,8},{7,5},{8,10},{9,7},{10,12},{11... | collective-permute-start | bytes 3538952 | tf_op jit(solution)/shard_map/ppermute | solution.py:291
  18.4 0.9 %copy-start.5 = (bf16[64,1024]{1,0:T(8,128)(2,1)S(1)}, bf16[64,1024]{1,0:T(8,128)(2,1)}, u32[]{:S(2)}) copy-start(bf16[64,1024]{1,0:T(8,128)(2,1)} %refs_1_.14) | copy-start | bytes 393220
  18.4 0.9 %copy-start.7 = (s32[1,4]{1,0:T(1,128)S(1)}, s32[1,4]{1,0:T(1,128)}, u32[]{:S(2)}) copy-start(s32[1,4]{1,0:T(1,128)} %refs_0_.10) | copy-start | bytes 52
  19.0 4.3 %collective-permute-start.1 = (bf16[576,512]{1,0:T(8,128)(2,1)S(1)}, bf16[576,512]{1,0:T(8,128)(2,1)S(1)}, u32[]{:S(2)}, u32[]{:S(2)}) collective-permute-start(bf16[576,512]{1,0:T(8,128)(2,1)S(1)} %leaf.1.refs_4_.refs_2_), channel_id=1, source_target_pairs={{0,1},{1,0},{2,3},{3,2},{4,5},{5,4},{6,7},{7,6},{8,9},{9,8},{10,11... | collective-permute-start | bytes 1769480 | tf_op jit(solution)/shard_map/ppermute | solution.py:287
  23.7 25.7 %collective-permute-start.5 = (bf16[288,512]{1,0:T(8,128)(2,1)S(1)}, bf16[288,512]{1,0:T(8,128)(2,1)S(1)}, u32[]{:S(2)}, u32[]{:S(2)}) collective-permute-start(bf16[288,512]{1,0:T(8,128)(2,1)S(1)} %get-tuple-element.38), channel_id=1, source_target_pairs={{0,4},{1,5},{2,6},{3,7},{4,0},{5,1},{6,2},{7,3},{8,12},{9,13},{10,... | collective-permute-start | bytes 884744 | tf_op jit(solution)/shard_map/ppermute | solution.py:287
  23.8 26.3 %collective-permute-start.6 = (bf16[288,512]{1,0:T(8,128)(2,1)S(1)}, bf16[288,512]{1,0:T(8,128)(2,1)S(1)}, u32[]{:S(2)}, u32[]{:S(2)}) collective-permute-start(bf16[288,512]{1,0:T(8,128)(2,1)S(1)} %get-tuple-element.39), channel_id=1, source_target_pairs={{0,6},{1,7},{2,4},{3,5},{4,2},{5,3},{6,0},{7,1},{8,14},{9,15},{10,... | collective-permute-start | bytes 884744 | tf_op jit(solution)/shard_map/ppermute | solution.py:287
  27.1 22.2 %collective-permute-start.4 = (bf16[192,512]{1,0:T(8,128)(2,1)S(1)}, bf16[192,512]{1,0:T(8,128)(2,1)S(1)}, u32[]{:S(2)}, u32[]{:S(2)}) collective-permute-start(bf16[192,512]{1,0:T(8,128)(2,1)S(1)} %get-tuple-element.37), channel_id=1, source_target_pairs={{0,2},{1,3},{2,0},{3,1},{4,6},{5,7},{6,4},{7,5},{8,10},{9,11},{10,... | collective-permute-start | bytes 589832 | tf_op jit(solution)/shard_map/ppermute | solution.py:287
  50.6 6.0 %collective-permute-start.11 = (bf16[96,512]{1,0:T(8,128)(2,1)S(1)}, bf16[96,512]{1,0:T(8,128)(2,1)S(1)}, u32[]{:S(2)}, u32[]{:S(2)}) collective-permute-start(bf16[96,512]{1,0:T(8,128)(2,1)S(1)} %get-tuple-element.51.refs_4_), channel_id=1, source_target_pairs={{0,16},{1,17},{2,18},{3,19},{4,20},{5,21},{6,22},{7,23},{8,24},{9,... | collective-permute-start | bytes 294920 | tf_op jit(solution)/shard_map/ppermute | solution.py:287
  50.7 7.7 %collective-permute-start.12 = (bf16[96,512]{1,0:T(8,128)(2,1)S(1)}, bf16[96,512]{1,0:T(8,128)(2,1)S(1)}, u32[]{:S(2)}, u32[]{:S(2)}) collective-permute-start(bf16[96,512]{1,0:T(8,128)(2,1)S(1)} %get-tuple-element.51.refs_4_), channel_id=1, source_target_pairs={{0,24},{1,25},{2,26},{3,27},{4,28},{5,29},{6,30},{7,31},{8,16},{9,... | collective-permute-start | bytes 294920 | tf_op jit(solution)/shard_map/ppermute | solution.py:287
  50.8 7.6 %collective-permute-start.10 = (bf16[128,512]{1,0:T(8,128)(2,1)S(1)}, bf16[128,512]{1,0:T(8,128)(2,1)S(1)}, u32[]{:S(2)}, u32[]{:S(2)}) collective-permute-start(bf16[128,512]{1,0:T(8,128)(2,1)S(1)} %get-tuple-element.50.refs_3_), channel_id=1, source_target_pairs={{0,8},{1,9},{2,10},{3,11},{4,12},{5,13},{6,14},{7,15},{8,0},{9,1},... | collective-permute-start | bytes 393224 | tf_op jit(solution)/shard_map/ppermute | solution.py:287
  53.4 10.0 %collective-permute-start.9 = (bf16[256,512]{1,0:T(8,128)(2,1)S(1)}, bf16[256,512]{1,0:T(8,128)(2,1)S(1)}, u32[]{:S(2)}, u32[]{:S(2)}) collective-permute-start(bf16[256,512]{1,0:T(8,128)(2,1)S(1)} %get-tuple-element.49), channel_id=1, source_target_pairs={{0,2},{1,3},{2,0},{3,1},{4,6},{5,7},{6,4},{7,5},{8,10},{9,11},{10,... | collective-permute-start | bytes 786440 | tf_op jit(solution)/shard_map/ppermute | solution.py:287
  53.4 10.6 %collective-permute-start.8 = (bf16[1152,512]{1,0:T(8,128)(2,1)S(1)}, bf16[1152,512]{1,0:T(8,128)(2,1)S(1)}, u32[]{:S(2)}, u32[]{:S(2)}) collective-permute-start(bf16[1152,512]{1,0:T(8,128)(2,1)S(1)} %collective-permute-done.3.refs_2_), channel_id=1, source_target_pairs={{0,1},{1,0},{2,3},{3,2},{4,5},{5,4},{6,7},{7,6},{8,9},{9,8},{10,11... | collective-permute-start | bytes 3538952 | tf_op jit(solution)/shard_map/ppermute | solution.py:287
  59.4 12.2 %collective-permute-start.13 = (bf16[256,512]{1,0:T(8,128)(2,1)S(1)}, bf16[256,512]{1,0:T(8,128)(2,1)S(1)}, u32[]{:S(2)}, u32[]{:S(2)}) collective-permute-start(bf16[256,512]{1,0:T(8,128)(2,1)S(1)} %get-tuple-element.57.refs_1_), channel_id=1, source_target_pairs={{0,2},{1,3},{2,0},{3,1},{4,6},{5,7},{6,4},{7,5},{8,10},{9,11},{10,... | collective-permute-start | bytes 786440 | tf_op jit(solution)/shard_map/ppermute | solution.py:287
  59.5 11.1 %collective-permute-start.14 = (bf16[128,512]{1,0:T(8,128)(2,1)S(1)}, bf16[128,512]{1,0:T(8,128)(2,1)S(1)}, u32[]{:S(2)}, u32[]{:S(2)}) collective-permute-start(bf16[128,512]{1,0:T(8,128)(2,1)S(1)} %get-tuple-element.54.refs_3_), channel_id=1, source_target_pairs={{0,4},{1,5},{2,6},{3,7},{4,0},{5,1},{6,2},{7,3},{8,12},{9,13},{10,... | collective-permute-start | bytes 393224 | tf_op jit(solution)/shard_map/ppermute | solution.py:287
  62.2 9.4 %collective-permute-start.15 = (bf16[128,512]{1,0:T(8,128)(2,1)S(1)}, bf16[128,512]{1,0:T(8,128)(2,1)S(1)}, u32[]{:S(2)}, u32[]{:S(2)}) collective-permute-start(bf16[128,512]{1,0:T(8,128)(2,1)S(1)} %get-tuple-element.54.refs_3_), channel_id=1, source_target_pairs={{0,6},{1,7},{2,4},{3,5},{4,2},{5,3},{6,0},{7,1},{8,14},{9,15},{10,... | collective-permute-start | bytes 393224 | tf_op jit(solution)/shard_map/ppermute | solution.py:287
  71.7 2.9 %collective-permute-start.16 = (bf16[1024,512]{1,0:T(8,128)(2,1)S(1)}, bf16[1024,512]{1,0:T(8,128)(2,1)S(1)}, u32[]{:S(2)}, u32[]{:S(2)}) collective-permute-start(bf16[1024,512]{1,0:T(8,128)(2,1)S(1)} %half.1.refs_2_), channel_id=1, source_target_pairs={{0,1},{1,0},{2,3},{3,2},{4,5},{5,4},{6,7},{7,6},{8,9},{9,8},{10,11... | collective-permute-start | bytes 3145736 | tf_op jit(solution)/shard_map/ppermute | solution.py:287

commit v3 on v2

--- a/solution.py
+++ b/solution.py
@@ -13,6 +13,7 @@
 VMEM_BYTES = 24 * 1024 * 1024
 ROWS = 256
 WORK = 1.0
+LOW = 1.0
 
 
 def dot(a, b, over=((1,), (0,))):
@@ -55,7 +56,7 @@
     return jnp.exp2(dot(left, right, ((0,), (0,)))).astype(BF16)
 
 
-def call(body, name, outs, args, flops, smem=(), scratch=(), grid=None, in_specs=None, after=()):
+def call(body, name, outs, args, flops, smem=(), scratch=(), in_specs=None, after=(), out_space=pltpu.VMEM):
     specs = in_specs or [pl.BlockSpec(memory_space=pltpu.SMEM if k in smem else pltpu.VMEM) for k in range(len(args))]
     specs = specs + [pl.BlockSpec(memory_space=pl.ANY) for _ in after]
     taken = len(args)
@@ -67,9 +68,8 @@
     return pl.pallas_call(
         reading,
         name=name,
-        grid=grid or (),
         in_specs=specs,
-        out_specs=[pl.BlockSpec(memory_space=pltpu.VMEM) for _ in outs],
+        out_specs=[pl.BlockSpec(memory_space=out_space) for _ in outs],
         out_shape=[jax.ShapeDtypeStruct(s, t) for s, t in outs],
         scratch_shapes=list(scratch),
         compiler_params=pltpu.CompilerParams(vmem_limit_bytes=VMEM_BYTES),
@@ -92,45 +92,58 @@
     return dot(columns, choice).astype(BF16)
 
 
+def start_all(copies):
+    for copy in copies:
+        copy.start()
+    return copies
+
+
+def wait_all(copies):
+    for copy in copies:
+        copy.wait()
+
+
 def pack_kernel(points, weights, out, done):
     half = points.shape[1] // 2
     rows = weights.shape[0]
-    copies = [
-        pltpu.make_async_copy(weights, out.at[0:rows, :], done.at[0]),
-        pltpu.make_async_copy(points.at[:, 0:half], out.at[rows : rows + 64, :], done.at[1]),
-        pltpu.make_async_copy(points.at[:, half : 2 * half], out.at[rows + 64 : rows + 128, :], done.at[2]),
-    ]
-    for copy in copies:
-        copy.start()
-    for copy in copies:
-        copy.wait()
-
-
-def terms_kernel(w, p, t, send, keep, lifted_weights):
-    step = pl.program_id(0)
+    quarter = rows // 4
+    parts = [(weights.at[k * quarter : (k + 1) * quarter, :], out.at[k * quarter : (k + 1) * quarter, :]) for k in range(4)]
+    parts += [(points.at[:, k * half : (k + 1) * half], out.at[rows + k * 64 : rows + k * 64 + 64, :]) for k in range(2)]
+    wait_all(start_all([pltpu.make_async_copy(a, b, done.at[k]) for k, (a, b) in enumerate(parts)]))
+
+
+def terms_kernel(w, interp, transfers, send, keep, lifted_weights, transfer0, p, t, done):
     core, _, _ = place()
-
-    @pl.when(step == 0)
-    def _():
-        lifted_weights[...] = dot(w[0:1024, :], p[...], ((0,), (0,))).astype(BF16)
-
-    row = pl.multiple_of(step * 256, 256)
+    half = p.shape[0] // 2
+    first = start_all(
+        [
+            pltpu.make_async_copy(interp.at[k * half : (k + 1) * half, :], p.at[k * half : (k + 1) * half, :], done.at[k])
+            for k in range(2)
+        ]
+    )
+    levels = start_all([pltpu.make_async_copy(transfers.at[0, k + 1], t.at[k], done.at[2 + k]) for k in range(4)])
+    last = start_all([pltpu.make_async_copy(transfers.at[0, 0], transfer0, done.at[6])])
+    wait_all(first)
+    lifted_weights[...] = dot(w[0 : 2 * half, :], p[...], ((0,), (0,))).astype(BF16)
     theirs = pl.multiple_of((1 - core) * 256, 256)
     mine = pl.multiple_of(core * 256, 256)
-    send[pl.ds(row, 256), :] = dot(lifted_weights[pl.ds(theirs, 256), :], t[0, 0]).astype(BF16)
-    keep[pl.ds(row, 256), :] = dot(lifted_weights[pl.ds(mine, 256), :], t[0, 0])
+    for k in range(4):
+        levels[k].wait()
+        send[k * 256 : (k + 1) * 256, :] = dot(lifted_weights[pl.ds(theirs, 256), :], t[k]).astype(BF16)
+        keep[k * 256 : (k + 1) * 256, :] = dot(lifted_weights[pl.ds(mine, 256), :], t[k])
+    wait_all(last)
 
 
 def leaf_kernel(lifted_weights, t, payload, index, out):
     size = payload.shape[0] - 128
-    out[0:512, :] = dot(lifted_weights[...], t[0, 0]).astype(BF16)
+    out[0:512, :] = dot(lifted_weights[...], t[...]).astype(BF16)
     rank = lax.broadcasted_iota(jnp.int32, (size // 2, index.shape[1]), 0)
     chosen = dot(payload[size : size + 64, :], (rank == index[...]).astype(F32).astype(BF16))
     chosen = chosen + dot(payload[size + 64 : size + 128, :], (rank + size // 2 == index[...]).astype(F32).astype(BF16))
     out[512:576, :] = chosen.astype(BF16)
 
 
-def chip_kernel(keep, came, mine, theirs, to1, to2, to4, to6, kept, pair, total):
+def chip_kernel(keep, came, mine, theirs, to2, to4, to6, kept, pair, total):
     core, x, _ = place()
     mine, theirs = mine[512:576, :], theirs[512:576, :]
     first = jnp.where(core == 0, mine, theirs)
@@ -138,7 +151,7 @@
     pair[0:64, :] = first
     pair[64:128, :] = second
     total[...] = keep[...] + came[...].astype(F32)
-    to1[...] = total[0:256, :].astype(BF16)
+    to2[192:448, :] = total[0:256, :].astype(BF16)
     to2[128:192, :] = jnp.concatenate([first[:, :256], second[:, :256]], axis=1)
     for level, at in ((3, 0), (4, 64)):
         for out, row, other in ((to2, 0, x ^ 1), (to4, 128, x ^ 2), (to6, 128, x ^ 3)):
@@ -171,20 +184,17 @@
     return dot(sums, gaussian(lifted(sibling, True), lifted(own, False))).astype(BF16)
 
 
-def couple_low_kernel(term0, from4, from6, pair, ring, out0, out2):
+def couple_low_kernel(term0, from2, from4, from6, pair, ring, out0, out1, out2):
     core, x, _ = place()
     first, second = pair[0:64, :], pair[64:128, :]
     out0[...] = couple(term0[0:512, :], jnp.where(core == 0, first, second), jnp.where(core == 0, second, first))
+    own = jnp.concatenate([first[:, 0:256], second[:, 0:256]], axis=1)
+    out1[...] = couple(from2[192:448, :], own, from2[128:192, :])
     low = x & 2
     own = jnp.concatenate([ring[low], ring[low | 1]], axis=1)
     sibling = jnp.concatenate([ring[low ^ 2], ring[(low ^ 2) | 1]], axis=1)
     sums = (from4[0:128, :].astype(F32) + from6[0:128, :].astype(F32)).astype(BF16)
     out2[...] = couple(sums, own, sibling)
-
-
-def couple_chip_kernel(sums, from2, pair, out1):
-    own = jnp.concatenate([pair[0:64, 0:256], pair[64:128, 0:256]], axis=1)
-    out1[...] = couple(sums[...], own, from2[128:192, :])
 
 
 def couple_high_kernel(from8, from16, from24, to8, to16, coupled2, out2, out4):
@@ -244,14 +254,14 @@
         out[rows, :] = result[k] + total[rows, :] if with_total else result[k]
 
 
-def near(mask, points, blocks, slots, total, name, after):
+def near(mask, points, blocks, slots, total, name, after, cover=1):
     args = [mask, points, *blocks] + ([] if total is None else [total])
     size, width = points.shape[1], blocks[0].shape[1]
 
     def body(*refs):
         near_kernel(len(blocks), slots, total is not None, *refs)
 
-    flops = 2 * len(blocks) * size * size * (width + 256)
+    flops = cover * 2 * len(blocks) * size * size * (width + 256)
     return call(body, name, [((size, width), F32), ((8, 128), F32)], args, flops, smem=(0,), after=after)
 
 
@@ -269,14 +279,17 @@
     add_levels(far, transfers, mine, core)
 
 
-def product_kernel(total, interp, transfers, begun, theirs, out, far):
+def product_kernel(total, interp, transfers, begun, theirs, product, far, out, done):
     core, _, _ = place()
     far[...] = begun[...]
     add_levels(far, transfers, theirs, 1 - core)
     skeleton = far[...].astype(BF16)
-    for k in range(total.shape[0] // ROWS):
-        rows = slice(k * ROWS, (k + 1) * ROWS)
+    copies = []
+    for k in range(total.shape[0] // 128):
+        rows = slice(k * 128, (k + 1) * 128)
         out[rows, :] = (total[rows, :] + dot(interp[rows, :], skeleton)).astype(BF16)
+        copies += start_all([pltpu.make_async_copy(out.at[rows, :], product.at[rows, :], done.at[k])])
+    wait_all(copies)
 
 
 def per_device(points, weights, interp, transfers, near_mask, skel_index):
@@ -290,71 +303,76 @@
         pairs = [(leaf, leaf + (odd if leaf & 1 else even)) for leaf in range(leaves)]
         return lax.ppermute(value, AXIS, [(a, b) for a, b in pairs if 0 <= b < leaves])
 
+    def staged_across_rows(value):
+        end = {leaf: leaf + (-8 if leaf & 1 else 8) for leaf in range(leaves) if (leaf & 7) in (1, 6)}
+        pairs = [(leaf, end.get(leaf, leaf)) for leaf in range(leaves)]
+        return lax.ppermute(value, AXIS, [(a, b) for a, b in pairs if 0 <= b < leaves])
+
+    def turned(value):
+        pairs = [(leaf, (leaf & ~7) | ((leaf + (-2 if leaf & 1 else 2)) & 7)) for leaf in range(leaves)]
+        return lax.ppermute(value, AXIS, pairs)
+
     def rows(count, dtype=BF16):
         return (count, 512), dtype
 
-    def whole(*shape):
-        return pl.BlockSpec(shape, lambda g: (0,) * len(shape))
-
-    def near_of(blocks, slots, total, name, after):
-        return near(near_mask, points, blocks, slots, total, name, after)
-
+    def near_of(blocks, slots, total, name, after, cover=1):
+        return near(near_mask, points, blocks, slots, total, name, after, cover)
+
+    in_hbm = pl.BlockSpec(memory_space=pltpu.HBM)
+
+    def kept_in_hbm(value):
+        return pltpu.with_memory_space_constraint(value, pltpu.HBM)
+
+    in_vmem = pl.BlockSpec(memory_space=pltpu.VMEM)
     (payload,) = call(
         pack_kernel,
         "pack",
         [rows(size + 128)],
-        [points, weights],
+        [kept_in_hbm(points), kept_in_hbm(weights)],
         0,
-        scratch=[pltpu.SemaphoreType.DMA((3,))],
-        in_specs=[pl.BlockSpec(memory_space=pl.ANY)] * 2,
+        scratch=[pltpu.SemaphoreType.DMA((6,))],
+        in_specs=[in_hbm] * 2,
     )
     outer = moved(payload, -1, 1)
-    second = moved(payload, 2, -2)
     partner = swap(payload, 1)
-    send, keep, lifted_weights = call(
+    send, keep, lifted_weights, transfer0 = call(
         terms_kernel,
         "terms",
-        [rows(1024), rows(1024, F32), rows(512)],
-        [payload, interp, transfers],
+        [rows(1024), rows(1024, F32), rows(512), rows(512)],
+        [payload, kept_in_hbm(interp), kept_in_hbm(transfers)],
         2 * 512 * 512 * (1024 + 4 * 512),
-        grid=(4,),
-        in_specs=[
-            whole(size + 128, width),
-            whole(size, 512),
-            pl.BlockSpec((1, 1, 512, 512), lambda g: (0, g + 1, 0, 0)),
+        scratch=[
+            pltpu.VMEM((size, 512), BF16),
+            pltpu.VMEM((4, 512, 512), BF16),
+            pltpu.SemaphoreType.DMA((7,)),
         ],
+        in_specs=[in_vmem, in_hbm, in_hbm],
     )
     came = swap(send, 1)
     (term0,) = call(
         leaf_kernel,
         "leaf",
         [rows(576)],
-        [lifted_weights, transfers, payload, skel_index],
+        [lifted_weights, transfer0, payload, skel_index],
         2 * 512 * 512 * 768,
-        grid=(1,),
-        in_specs=[
-            whole(512, 512),
-            pl.BlockSpec((1, 1, 512, 512), lambda g: (0, 0, 0, 0)),
-            whole(size + 128, width),
-            whole(1, 512),
-        ],
     )
     other0 = swap(term0, 1)
-    total, token = near_of([payload, partner], [None, (2, 1)], None, "near_own", (term0,))
-
-    to1, to2, to4, to6, kept, pair = call(
+    total, token = near_of([payload, partner], [None, (2, 1)], None, "near_own", (term0,), cover=20)
+
+    to2, to4, to6, kept, pair = call(
         chip_kernel,
         "chip",
-        [rows(256), rows(192), rows(288), rows(288), rows(128, F32), rows(128)],
+        [rows(448), rows(288), rows(288), rows(128, F32), rows(128)],
         [keep, came, term0, other0],
         1e6,
         after=(token,),
         scratch=[pltpu.VMEM((1024, 512), F32)],
     )
     from2, from4, from6 = swap(to2, 2), swap(to4, 4), swap(to6, 6)
+    late, pair = lax.optimization_barrier((payload, pair))
+    staged = staged_across_rows(late)
     total, token = near_of([outer], [(1, 2)], total, "near_outer", (pair,))
 
-    total, token = near_of([second], [(0, 3)], total, "near_second", (token,))
     to8, to16, ring = call(
         row_kernel,
         "row",
@@ -363,29 +381,28 @@
         1e8,
         after=(token,),
     )
+    staged, outer, ring = lax.optimization_barrier((staged, outer, ring))
+    second = turned(staged)
+    past = swap(outer, 1)
     from8, from16, from24 = swap(to8, 8), swap(to16, 16), swap(to16, 24)
-    to1, outer, ring = lax.optimization_barrier((to1, outer, ring))
-    from1 = swap(to1, 2)
-    past = swap(outer, 1)
-    coupled0, coupled2 = call(
+    coupled0, coupled1, coupled2 = call(
         couple_low_kernel,
         "couple_low",
-        [rows(512), rows(128)],
-        [other0, from4, from6, pair, ring],
-        40 * 512 * 512 * (2 * 256 + 640),
-    )
+        [rows(512), rows(256), rows(128)],
+        [other0, from2, from4, from6, pair, ring],
+        1e6,
+    )
+    total, token = near_of([past], [(3, 0)], total, "near_past", (coupled2,), cover=0.01)
     part2, part4 = call(
         couple_high_kernel,
         "couple_high",
         [rows(256), rows(128)],
         [from8, from16, from24, to8, to16, coupled2],
-        2 * 512 * 512 * (2 * 256 + 128),
+        1e6,
+        after=(token,),
     )
     back2, back4, back6 = swap(part2, 2), swap(part4, 4), swap(part4, 6)
-    (coupled1,) = call(
-        couple_chip_kernel, "couple_chip", [rows(256)], [from1, from2, pair], 2 * 512 * 512 * 512, after=(part4,)
-    )
-    total, token = near_of([past], [(3, 0)], total, "near_past", (coupled1,))
+    total, token = near_of([second], [(0, 3)], total, "near_second", (part4,))
     (mine,) = call(
         half_kernel, "half", [rows(1024)], [coupled1, part2, back2, back4, back6], 1e6, after=(token,)
     )
@@ -397,7 +414,12 @@
         [((size, width), BF16)],
         [total, interp, transfers, far, theirs],
         2 * 512 * 512 * (4 * 256 + 1024),
-        scratch=[pltpu.VMEM((512, 512), F32)],
+        scratch=[
+            pltpu.VMEM((512, 512), F32),
+            pltpu.VMEM((size, width), BF16),
+            pltpu.SemaphoreType.DMA((size // 128,)),
+        ],
+        out_space=pltpu.HBM,
     )[0]
 
 

time: 78.3 us -> 73.8 us (0.943)
  waiting for transfers between devices: 27.8 us -> 17.4 us
  starting transfers between devices: 23.3 us -> 31.2 us
  local copies, waits for them, and re-layouts: 4.13 us -> 0.03 us
  Pallas kernels: 22.6 us -> 24.7 us
    ppermute x2 -> x1, waiting for transfers between devices: 17.4 us -> 0.01 us  [moved(): lax.ppermute(value, AXIS, [(a, b) for a, b in pairs if 0 <= b < leaves])]
    ppermute x15 -> x14, waiting for transfers between devices: 10.4 us -> 17.4 us  [swap(): lax.ppermute(value, AXIS, [(leaf, leaf ^ mask) for leaf in range(leaves)])]
    ppermute x15 -> x14, starting transfers between devices: 17.8 us -> 23.4 us  [swap(): lax.ppermute(value, AXIS, [(leaf, leaf ^ mask) for leaf in range(leaves)])]
    ppermute x0 -> x2, starting transfers between devices: none -> 4.78 us  [the longest x1 2.75 us: turned(): return lax.ppermute(value, AXIS, pairs)]
    unnamed x16 -> x10, local copies, waits for them, and re-layouts: 4.13 us -> 0.03 us
    ppermute x2 -> x1, starting transfers between devices: 5.46 us -> 3.02 us  [moved(): lax.ppermute(value, AXIS, [(a, b) for a, b in pairs if 0 <= b < leaves])]
    pallas_call x15 -> x14, Pallas kernels: 22.6 us -> 24.7 us  [call(): pl.pallas_call(reading, name=name, in_specs=specs, out_specs=[pl.BlockSpe...]
  transfers between devices with their start and end apart: 17 -> 17, of which waited for: 7 -> 5; matrix products, arithmetic and copies ran while one was open for 0% -> 0% of each run, Pallas kernels for 24% -> 27%
where the time goes in v3:
time: 73.8 us; the launch traced here: 73.7 us
  starting transfers between devices  31.2 us (42%)
  Pallas kernels  24.7 us (33%)
  waiting for transfers between devices  17.4 us (24%)
    pallas_call x14, Pallas kernels, call(): pl.pallas_call(reading, name=name, in_specs=specs, out_specs=[pl.BlockSpe...  24.7 us
    ppermute x14, starting transfers between devices, swap(): lax.ppermute(value, AXIS, [(leaf, leaf ^ mask) for leaf in range(leaves)])  23.4 us
    ppermute x14, waiting for transfers between devices, swap(): lax.ppermute(value, AXIS, [(leaf, leaf ^ mask) for leaf in range(leaves)])  17.4 us
    ppermute x1, starting transfers between devices, moved(): lax.ppermute(value, AXIS, [(a, b) for a, b in pairs if 0 <= b < leaves])  3.02 us
    ppermute x1, starting transfers between devices, turned(): return lax.ppermute(value, AXIS, pairs)  2.75 us
    ppermute x1, starting transfers between devices, staged_across_rows(): lax.ppermute(value, AXIS, [(a, b) for a, b in pairs if 0 <= b < leaves])  2.03 us
  transfers between devices with their start and end apart: 17, of which 5 were waited for; matrix products, arithmetic and copies ran while one was open for 0% of the time, Pallas kernels for 27%

profile of v3, /device:TPU:25, one launch (start us, length us, event | category | flops | bytes accessed | tf_op | source)
XLA Modules:
  0.0 73.7 jit_solution(15981851509932366888)
XLA Ops:
  0.0 1.3 %pack.1.refs_0_.refs_2_ = bf16[1152,512]{1,0:T(8,128)(2,1)S(1)} custom-call(bf16[64,1024]{1,0:T(8,128)(2,1)} %refs_1_.12, bf16[1024,512]{1,0:T(8,128)(2,1)} %refs_1_.7), custom_call_target="tpu_custom_call" | custom-call | bytes 2359296 | tf_op jit(solution)/shard_map/pack/pallas_call | solution.py:68
  1.3 0.0 copy-start.3
  1.3 0.8 %collective-permute-start.2 = (bf16[1152,512]{1,0:T(8,128)(2,1)S(1)}, bf16[1152,512]{1,0:T(8,128)(2,1)S(1)}, u32[]{:S(2)}, u32[]{:S(2)}) collective-permute-start(bf16[1152,512]{1,0:T(8,128)(2,1)S(1)} %pack.1.refs_0_.refs_2_), channel_id=1, source_target_pairs={{0,1},{1,0},{2,3},{3,2},{4,5},{5,4},{6,7},{7,6},{8,9},{9,8},{10,11... | collective-permute-start | bytes 3538952 | tf_op jit(solution)/shard_map/ppermute | solution.py:300
  2.0 3.0 %collective-permute-start.4 = (bf16[1152,512]{1,0:T(8,128)(2,1)S(1)}, bf16[1152,512]{1,0:T(8,128)(2,1)S(1)}, u32[]{:S(2)}, u32[]{:S(2)}) collective-permute-start(bf16[1152,512]{1,0:T(8,128)(2,1)S(1)} %pack.1.refs_0_.refs_2_), channel_id=1, source_target_pairs={{1,2},{2,1},{3,4},{4,3},{5,6},{6,5},{7,8},{8,7},{9,10},{10,9},{11,... | collective-permute-start | bytes 3538952 | tf_op jit(solution)/shard_map/ppermute | solution.py:304
  5.1 3.8 %terms.1 = (bf16[1024,512]{1,0:T(8,128)(2,1)S(1)}, f32[1024,512]{1,0:T(8,128)S(1)}, bf16[512,512]{1,0:T(8,128)(2,1)S(1)}, bf16[512,512]{1,0:T(8,128)(2,1)S(1)}) custom-call(bf16[1152,512]{1,0:T(8,128)(2,1)S(1)} %pack.1.refs_0_.refs_2_, bf16[1024,512]{1,0:T(8,128)(2,1)} %refs_1_.13, bf16[1,5,512,512]{3,2,1,0:T(8,128)(2,1)} %refs_2_.3), custom_call_target="tpu_custom_call" | custom-call | flops 1610612736 | bytes 9043968 | tf_op jit(solution)/shard_map/terms/pallas_call | solution.py:68
  8.9 0.0 copy-start.2
  8.9 0.0 copy-start.4
  8.9 0.0 copy-done.3
  8.9 0.6 leaf.1.refs_4_.refs_2_
  9.5 5.5 %collective-permute-start.1 = (bf16[576,512]{1,0:T(8,128)(2,1)S(1)}, bf16[576,512]{1,0:T(8,128)(2,1)S(1)}, u32[]{:S(2)}, u32[]{:S(2)}) collective-permute-start(bf16[576,512]{1,0:T(8,128)(2,1)S(1)} %leaf.1.refs_4_.refs_2_), channel_id=1, source_target_pairs={{0,1},{1,0},{2,3},{3,2},{4,5},{5,4},{6,7},{7,6},{8,9},{9,8},{10,11... | collective-permute-start | bytes 1769480 | tf_op jit(solution)/shard_map/ppermute | solution.py:300
  15.0 0.1 collective-permute-start
  15.1 0.0 collective-permute-done.2.refs_3_
  15.1 0.0 copy-done.2
  15.1 0.0 copy-done.4
  15.1 4.1 %near_own.1 = (f32[1024,512]{1,0:T(8,128)S(1)}, f32[8,128]{1,0:T(8,128)S(1)}) custom-call(s32[1,4]{1,0:T(1,128)S(1)} %copy-done.4, bf16[64,1024]{1,0:T(8,128)(2,1)S(1)} %copy-done.2, bf16[1152,512]{1,0:T(8,128)(2,1)S(1)} %pack.1.refs_0_.refs_2_, bf16[1152,512]{1,0:T(8,128)(2,1)S(1)} %collective-permute-done.2.refs_3_, bf16[576,512]{1,0:T(8,128)(2,1)S(1)} %leaf.1.refs_4_.refs_2_), custom_call_target="tpu_custom_call" | custom-call | flops 64424509440 | bytes 4591632 | tf_op jit(solution)/shard_map/near_own/pallas_call | solution.py:68
  19.2 0.0 collective-permute-done.1.refs_3_.refs_0_
  19.2 0.0 collective-permute-done.refs_1_
  19.2 0.4 chip.1
  19.7 2.0 %collective-permute-start.3 = (bf16[1152,512]{1,0:T(8,128)(2,1)S(1)}, bf16[1152,512]{1,0:T(8,128)(2,1)S(1)}, u32[]{:S(2)}, u32[]{:S(2)}) collective-permute-start(bf16[1152,512]{1,0:T(8,128)(2,1)S(1)} %pack.1.refs_0_.refs_2_), channel_id=1, source_target_pairs={{0,0},{2,2},{3,3},{4,4},{5,5},{6,14},{7,7},{8,8},{9,1},{10,10},{11... | collective-permute-start | bytes 3538952 | tf_op jit(solution)/shard_map/ppermute | solution.py:309
  21.7 0.1 collective-permute-start.5
  21.8 0.1 collective-permute-start.6
  21.9 3.8 %collective-permute-start.7 = (bf16[288,512]{1,0:T(8,128)(2,1)S(1)}, bf16[288,512]{1,0:T(8,128)(2,1)S(1)}, u32[]{:S(2)}, u32[]{:S(2)}) collective-permute-start(bf16[288,512]{1,0:T(8,128)(2,1)S(1)} %get-tuple-element.44), channel_id=1, source_target_pairs={{0,6},{1,7},{2,4},{3,5},{4,2},{5,3},{6,0},{7,1},{8,14},{9,15},{10,... | collective-permute-start | bytes 884744 | tf_op jit(solution)/shard_map/ppermute | solution.py:300
  25.6 0.0 collective-permute-done.4.refs_2_
  25.6 2.4 %near_outer.1 = (f32[1024,512]{1,0:T(8,128)S(1)}, f32[8,128]{1,0:T(8,128)S(1)}) custom-call(s32[1,4]{1,0:T(1,128)S(1)} %copy-done.4, bf16[64,1024]{1,0:T(8,128)(2,1)S(1)} %copy-done.2, bf16[1152,512]{1,0:T(8,128)(2,1)S(1)} %collective-permute-done.4.refs_2_, f32[1024,512]{1,0:T(8,128)S(1)} %get-tuple-element.47.refs_3_, ...), custom_call_target="tpu_custom_call" | custom-call | flops 1610612736 | bytes 5509136 | tf_op jit(solution)/shard_map/near_outer/pallas_call | solution.py:68
  28.0 9.7 %collective-permute-done.6.refs_1_.refs_2_ = bf16[288,512]{1,0:T(8,128)(2,1)S(1)} collective-permute-done((bf16[288,512]{1,0:T(8,128)(2,1)S(1)}, bf16[288,512]{1,0:T(8,128)(2,1)S(1)}, u32[]{:S(2)}, u32[]{:S(2)}) %collective-permute-start.6) | collective-permute-done | bytes 294944 | tf_op jit(solution)/shard_map/ppermute | solution.py:300
  37.7 1.1 %collective-permute-done.7.refs_2_.refs_3_ = bf16[288,512]{1,0:T(8,128)(2,1)S(1)} collective-permute-done((bf16[288,512]{1,0:T(8,128)(2,1)S(1)}, bf16[288,512]{1,0:T(8,128)(2,1)S(1)}, u32[]{:S(2)}, u32[]{:S(2)}) %collective-permute-start.7) | collective-permute-done | bytes 294944 | tf_op jit(solution)/shard_map/ppermute | solution.py:300
  38.8 0.0 collective-permute-done.5.refs_0_.refs_1_
  38.8 0.5 row.1
  39.3 0.0 collective-permute-done.3
  39.3 1.2 %collective-permute-start.9 = (bf16[1152,512]{1,0:T(8,128)(2,1)S(1)}, bf16[1152,512]{1,0:T(8,128)(2,1)S(1)}, u32[]{:S(2)}, u32[]{:S(2)}) collective-permute-start(bf16[1152,512]{1,0:T(8,128)(2,1)S(1)} %collective-permute-done.4.refs_2_), channel_id=1, source_target_pairs={{0,1},{1,0},{2,3},{3,2},{4,5},{5,4},{6,7},{7,6},{8,9},{9,8},{10,11... | collective-permute-start | bytes 3538952 | tf_op jit(solution)/shard_map/ppermute | solution.py:300
  40.5 2.8 %collective-permute-start.8 = (bf16[1152,512]{1,0:T(8,128)(2,1)S(1)}, bf16[1152,512]{1,0:T(8,128)(2,1)S(1)}, u32[]{:S(2)}, u32[]{:S(2)}) collective-permute-start(bf16[1152,512]{1,0:T(8,128)(2,1)S(1)} %collective-permute-done.3), channel_id=1, source_target_pairs={{0,2},{1,7},{2,4},{3,1},{4,6},{5,3},{6,0},{7,5},{8,10},{9,15},{10,... | collective-permute-start | bytes 3538952 | tf_op jit(solution)/shard_map/ppermute | solution.py:313
  43.3 0.0 collective-permute-start.10
  43.3 1.3 %collective-permute-start.11 = (bf16[96,512]{1,0:T(8,128)(2,1)S(1)}, bf16[96,512]{1,0:T(8,128)(2,1)S(1)}, u32[]{:S(2)}, u32[]{:S(2)}) collective-permute-start(bf16[96,512]{1,0:T(8,128)(2,1)S(1)} %get-tuple-element.57.refs_4_), channel_id=1, source_target_pairs={{0,16},{1,17},{2,18},{3,19},{4,20},{5,21},{6,22},{7,23},{8,24},{9,... | collective-permute-start | bytes 294920 | tf_op jit(solution)/shard_map/ppermute | solution.py:300
  44.5 2.6 %collective-permute-start.12 = (bf16[96,512]{1,0:T(8,128)(2,1)S(1)}, bf16[96,512]{1,0:T(8,128)(2,1)S(1)}, u32[]{:S(2)}, u32[]{:S(2)}) collective-permute-start(bf16[96,512]{1,0:T(8,128)(2,1)S(1)} %get-tuple-element.57.refs_4_), channel_id=1, source_target_pairs={{0,24},{1,25},{2,26},{3,27},{4,28},{5,29},{6,30},{7,31},{8,16},{9,... | collective-permute-start | bytes 294920 | tf_op jit(solution)/shard_map/ppermute | solution.py:300
  47.1 1.4 %couple_low.1 = (bf16[512,512]{1,0:T(8,128)(2,1)S(1)}, bf16[256,512]{1,0:T(8,128)(2,1)S(1)}, bf16[128,512]{1,0:T(8,128)(2,1)S(1)}) custom-call(bf16[576,512]{1,0:T(8,128)(2,1)S(1)} %collective-permute-done.1.refs_3_.refs_0_, bf16[448,512]{1,0:T(8,128)(2,1)S(1)} %collective-permute-done.5.refs_0_.refs_1_, ...), custom_call_target="tpu_custom_call" | custom-call | flops 1000000 | bytes 2818048 | tf_op jit(solution)/shard_map/couple_low/pallas_call | solution.py:68
  48.5 0.0 collective-permute-done.9.refs_2_
  48.6 2.5 %near_past.1 = (f32[1024,512]{1,0:T(8,128)S(1)}, f32[8,128]{1,0:T(8,128)S(1)}) custom-call(s32[1,4]{1,0:T(1,128)S(1)} %copy-done.4, bf16[64,1024]{1,0:T(8,128)(2,1)S(1)} %copy-done.2, bf16[1152,512]{1,0:T(8,128)(2,1)S(1)} %collective-permute-done.9.refs_2_, f32[1024,512]{1,0:T(8,128)S(1)} %get-tuple-element.52.refs_3_, ...), custom_call_target="tpu_custom_call" | custom-call | flops 16106127 | bytes 5509136 | tf_op jit(solution)/shard_map/near_past/pallas_call | solution.py:68
  51.0 0.0 collective-permute-done.11.refs_1_
  51.0 1.3 %collective-permute-done.12.refs_2_ = bf16[96,512]{1,0:T(8,128)(2,1)S(1)} collective-permute-done((bf16[96,512]{1,0:T(8,128)(2,1)S(1)}, bf16[96,512]{1,0:T(8,128)(2,1)S(1)}, u32[]{:S(2)}, u32[]{:S(2)}) %collective-permute-start.12) | collective-permute-done | bytes 98336 | tf_op jit(solution)/shard_map/ppermute | solution.py:300
  52.3 0.0 collective-permute-done.10.refs_0_
  52.3 1.0 %couple_high.1 = (bf16[256,512]{1,0:T(8,128)(2,1)S(1)}, bf16[128,512]{1,0:T(8,128)(2,1)S(1)}) custom-call(bf16[128,512]{1,0:T(8,128)(2,1)S(1)} %collective-permute-done.10.refs_0_, bf16[96,512]{1,0:T(8,128)(2,1)S(1)} %collective-permute-done.11.refs_1_, bf16[96,512]{1,0:T(8,128)(2,1)S(1)} %collective-permute-done.12.refs_2_, ...), custom_call_target="tpu_custom_call" | custom-call | flops 1000000 | bytes 1081344 | tf_op jit(solution)/shard_map/couple_high/pallas_call | solution.py:68
  53.3 0.5 collective-permute-start.13
  53.8 0.5 collective-permute-start.14
  54.4 2.9 %collective-permute-start.15 = (bf16[128,512]{1,0:T(8,128)(2,1)S(1)}, bf16[128,512]{1,0:T(8,128)(2,1)S(1)}, u32[]{:S(2)}, u32[]{:S(2)}) collective-permute-start(bf16[128,512]{1,0:T(8,128)(2,1)S(1)} %get-tuple-element.59.refs_4_), channel_id=1, source_target_pairs={{0,6},{1,7},{2,4},{3,5},{4,2},{5,3},{6,0},{7,1},{8,14},{9,15},{10,... | collective-permute-start | bytes 393224 | tf_op jit(solution)/shard_map/ppermute | solution.py:300
  57.3 0.0 collective-permute-done.8.refs_2_
  57.3 0.0 copy-start
  57.3 2.4 %near_second.1 = (f32[1024,512]{1,0:T(8,128)S(1)}, f32[8,128]{1,0:T(8,128)S(1)}) custom-call(s32[1,4]{1,0:T(1,128)S(1)} %copy-done.4, bf16[64,1024]{1,0:T(8,128)(2,1)S(1)} %copy-done.2, bf16[1152,512]{1,0:T(8,128)(2,1)S(1)} %collective-permute-done.8.refs_2_, f32[1024,512]{1,0:T(8,128)S(1)} %get-tuple-element.55.refs_3_, ...), custom_call_target="tpu_custom_call" | custom-call | flops 1610612736 | bytes 5509136 | tf_op jit(solution)/shard_map/near_second/pallas_call | solution.py:68
  59.7 4.1 %collective-permute-done.14.refs_3_ = bf16[128,512]{1,0:T(8,128)(2,1)S(1)} collective-permute-done((bf16[128,512]{1,0:T(8,128)(2,1)S(1)}, bf16[128,512]{1,0:T(8,128)(2,1)S(1)}, u32[]{:S(2)}, u32[]{:S(2)}) %collective-permute-start.14) | collective-permute-done | bytes 131104 | tf_op jit(solution)/shard_map/ppermute | solution.py:300
  63.7 0.0 collective-permute-done.15.refs_4_
  63.7 0.0 collective-permute-done.13.refs_2_
  63.7 0.1 half.1.refs_2_
  63.8 4.1 %collective-permute-start.16 = (bf16[1024,512]{1,0:T(8,128)(2,1)S(1)}, bf16[1024,512]{1,0:T(8,128)(2,1)S(1)}, u32[]{:S(2)}, u32[]{:S(2)}) collective-permute-start(bf16[1024,512]{1,0:T(8,128)(2,1)S(1)} %half.1.refs_2_), channel_id=1, source_target_pairs={{0,1},{1,0},{2,3},{3,2},{4,5},{5,4},{6,7},{7,6},{8,9},{9,8},{10,11... | collective-permute-start | bytes 3145736 | tf_op jit(solution)/shard_map/ppermute | solution.py:300
  67.9 0.0 copy-done
  67.9 0.0 copy-start.1
  67.9 1.0 %far.1.refs_3_ = f32[512,512]{1,0:T(8,128)S(1)} custom-call(bf16[1,5,512,512]{3,2,1,0:T(8,128)(2,1)S(1)} %copy-done, bf16[512,512]{1,0:T(8,128)(2,1)S(1)} %get-tuple-element.61.refs_1_, bf16[1024,512]{1,0:T(8,128)(2,1)S(1)} %half.1.refs_2_), custom_call_target="tpu_custom_call" | custom-call | flops 1048576000 | bytes 5242880 | tf_op jit(solution)/shard_map/far/pallas_call | solution.py:68
  69.0 1.3 %collective-permute-done.16.refs_4_ = bf16[1024,512]{1,0:T(8,128)(2,1)S(1)} collective-permute-done((bf16[1024,512]{1,0:T(8,128)(2,1)S(1)}, bf16[1024,512]{1,0:T(8,128)(2,1)S(1)}, u32[]{:S(2)}, u32[]{:S(2)}) %collective-permute-start.16) | collective-permute-done | bytes 1048608 | tf_op jit(solution)/shard_map/ppermute | solution.py:300
  70.2 0.0 copy-done.1
  70.2 3.3 %product.1 = bf16[1024,512]{1,0:T(8,128)(2,1)} custom-call(f32[1024,512]{1,0:T(8,128)S(1)} %get-tuple-element.60.refs_0_, bf16[1024,512]{1,0:T(8,128)(2,1)S(1)} %copy-done.1, bf16[1,5,512,512]{3,2,1,0:T(8,128)(2,1)S(1)} %copy-done, f32[512,512]{1,0:T(8,128)S(1)} %far.1.refs_3_, bf16[1024,512]{1,0:T(8,128)(2,1)S(1)} %collective-permute-done.16.refs_4_), custom_call_target="tpu_custom_call" | custom-call | flops 1073741824 | bytes 8912896 | tf_op jit(solution)/shard_map/product/pallas_call | solution.py:68
Async XLA Ops:
  1.3 7.6 %copy-start.3 = (s32[1,512]{1,0:T(1,128)S(1)}, s32[1,512]{1,0:T(1,128)}, u32[]{:S(2)}) copy-start(s32[1,512]{1,0:T(1,128)} %refs_3_.1) | copy-start | bytes 6148
  1.3 13.8 %collective-permute-start.2 = (bf16[1152,512]{1,0:T(8,128)(2,1)S(1)}, bf16[1152,512]{1,0:T(8,128)(2,1)S(1)}, u32[]{:S(2)}, u32[]{:S(2)}) collective-permute-start(bf16[1152,512]{1,0:T(8,128)(2,1)S(1)} %pack.1.refs_0_.refs_2_), channel_id=1, source_target_pairs={{0,1},{1,0},{2,3},{3,2},{4,5},{5,4},{6,7},{7,6},{8,9},{9,8},{10,11... | collective-permute-start | bytes 3538952 | tf_op jit(solution)/shard_map/ppermute | solution.py:300
  2.0 23.6 %collective-permute-start.4 = (bf16[1152,512]{1,0:T(8,128)(2,1)S(1)}, bf16[1152,512]{1,0:T(8,128)(2,1)S(1)}, u32[]{:S(2)}, u32[]{:S(2)}) collective-permute-start(bf16[1152,512]{1,0:T(8,128)(2,1)S(1)} %pack.1.refs_0_.refs_2_), channel_id=1, source_target_pairs={{1,2},{2,1},{3,4},{4,3},{5,6},{6,5},{7,8},{8,7},{9,10},{10,9},{11,... | collective-permute-start | bytes 3538952 | tf_op jit(solution)/shard_map/ppermute | solution.py:304
  8.9 6.2 %copy-start.2 = (bf16[64,1024]{1,0:T(8,128)(2,1)S(1)}, bf16[64,1024]{1,0:T(8,128)(2,1)}, u32[]{:S(2)}) copy-start(bf16[64,1024]{1,0:T(8,128)(2,1)} %refs_1_.12) | copy-start | bytes 393220
  8.9 6.2 %copy-start.4 = (s32[1,4]{1,0:T(1,128)S(1)}, s32[1,4]{1,0:T(1,128)}, u32[]{:S(2)}) copy-start(s32[1,4]{1,0:T(1,128)} %refs_0_.10) | copy-start | bytes 52
  9.5 9.7 %collective-permute-start.1 = (bf16[576,512]{1,0:T(8,128)(2,1)S(1)}, bf16[576,512]{1,0:T(8,128)(2,1)S(1)}, u32[]{:S(2)}, u32[]{:S(2)}) collective-permute-start(bf16[576,512]{1,0:T(8,128)(2,1)S(1)} %leaf.1.refs_4_.refs_2_), channel_id=1, source_target_pairs={{0,1},{1,0},{2,3},{3,2},{4,5},{5,4},{6,7},{7,6},{8,9},{9,8},{10,11... | collective-permute-start | bytes 1769480 | tf_op jit(solution)/shard_map/ppermute | solution.py:300
  15.0 4.2 %collective-permute-start = (bf16[1024,512]{1,0:T(8,128)(2,1)S(1)}, bf16[1024,512]{1,0:T(8,128)(2,1)S(1)}, u32[]{:S(2)}, u32[]{:S(2)}) collective-permute-start(bf16[1024,512]{1,0:T(8,128)(2,1)S(1)} %get-tuple-element.36), channel_id=1, source_target_pairs={{0,1},{1,0},{2,3},{3,2},{4,5},{5,4},{6,7},{7,6},{8,9},{9,8},{10,11... | collective-permute-start | bytes 3145736 | tf_op jit(solution)/shard_map/ppermute | solution.py:300
  19.7 19.7 %collective-permute-start.3 = (bf16[1152,512]{1,0:T(8,128)(2,1)S(1)}, bf16[1152,512]{1,0:T(8,128)(2,1)S(1)}, u32[]{:S(2)}, u32[]{:S(2)}) collective-permute-start(bf16[1152,512]{1,0:T(8,128)(2,1)S(1)} %pack.1.refs_0_.refs_2_), channel_id=1, source_target_pairs={{0,0},{2,2},{3,3},{4,4},{5,5},{6,14},{7,7},{8,8},{9,1},{10,10},{11... | collective-permute-start | bytes 3538952 | tf_op jit(solution)/shard_map/ppermute | solution.py:309
  21.7 17.1 %collective-permute-start.5 = (bf16[448,512]{1,0:T(8,128)(2,1)S(1)}, bf16[448,512]{1,0:T(8,128)(2,1)S(1)}, u32[]{:S(2)}, u32[]{:S(2)}) collective-permute-start(bf16[448,512]{1,0:T(8,128)(2,1)S(1)} %get-tuple-element.42), channel_id=1, source_target_pairs={{0,2},{1,3},{2,0},{3,1},{4,6},{5,7},{6,4},{7,5},{8,10},{9,11},{10,... | collective-permute-start | bytes 1376264 | tf_op jit(solution)/shard_map/ppermute | solution.py:300
  21.8 16.0 %collective-permute-start.6 = (bf16[288,512]{1,0:T(8,128)(2,1)S(1)}, bf16[288,512]{1,0:T(8,128)(2,1)S(1)}, u32[]{:S(2)}, u32[]{:S(2)}) collective-permute-start(bf16[288,512]{1,0:T(8,128)(2,1)S(1)} %get-tuple-element.43), channel_id=1, source_target_pairs={{0,4},{1,5},{2,6},{3,7},{4,0},{5,1},{6,2},{7,3},{8,12},{9,13},{10,... | collective-permute-start | bytes 884744 | tf_op jit(solution)/shard_map/ppermute | solution.py:300
  21.9 16.9 %collective-permute-start.7 = (bf16[288,512]{1,0:T(8,128)(2,1)S(1)}, bf16[288,512]{1,0:T(8,128)(2,1)S(1)}, u32[]{:S(2)}, u32[]{:S(2)}) collective-permute-start(bf16[288,512]{1,0:T(8,128)(2,1)S(1)} %get-tuple-element.44), channel_id=1, source_target_pairs={{0,6},{1,7},{2,4},{3,5},{4,2},{5,3},{6,0},{7,1},{8,14},{9,15},{10,... | collective-permute-start | bytes 884744 | tf_op jit(solution)/shard_map/ppermute | solution.py:300
  39.3 9.2 %collective-permute-start.9 = (bf16[1152,512]{1,0:T(8,128)(2,1)S(1)}, bf16[1152,512]{1,0:T(8,128)(2,1)S(1)}, u32[]{:S(2)}, u32[]{:S(2)}) collective-permute-start(bf16[1152,512]{1,0:T(8,128)(2,1)S(1)} %collective-permute-done.4.refs_2_), channel_id=1, source_target_pairs={{0,1},{1,0},{2,3},{3,2},{4,5},{5,4},{6,7},{7,6},{8,9},{9,8},{10,11... | collective-permute-start | bytes 3538952 | tf_op jit(solution)/shard_map/ppermute | solution.py:300
  40.5 16.7 %collective-permute-start.8 = (bf16[1152,512]{1,0:T(8,128)(2,1)S(1)}, bf16[1152,512]{1,0:T(8,128)(2,1)S(1)}, u32[]{:S(2)}, u32[]{:S(2)}) collective-permute-start(bf16[1152,512]{1,0:T(8,128)(2,1)S(1)} %collective-permute-done.3), channel_id=1, source_target_pairs={{0,2},{1,7},{2,4},{3,1},{4,6},{5,3},{6,0},{7,5},{8,10},{9,15},{10,... | collective-permute-start | bytes 3538952 | tf_op jit(solution)/shard_map/ppermute | solution.py:313
  43.3 9.0 %collective-permute-start.10 = (bf16[128,512]{1,0:T(8,128)(2,1)S(1)}, bf16[128,512]{1,0:T(8,128)(2,1)S(1)}, u32[]{:S(2)}, u32[]{:S(2)}) collective-permute-start(bf16[128,512]{1,0:T(8,128)(2,1)S(1)} %get-tuple-element.56.refs_3_), channel_id=1, source_target_pairs={{0,8},{1,9},{2,10},{3,11},{4,12},{5,13},{6,14},{7,15},{8,0},{9,1},... | collective-permute-start | bytes 393224 | tf_op jit(solution)/shard_map/ppermute | solution.py:300
  43.3 7.7 %collective-permute-start.11 = (bf16[96,512]{1,0:T(8,128)(2,1)S(1)}, bf16[96,512]{1,0:T(8,128)(2,1)S(1)}, u32[]{:S(2)}, u32[]{:S(2)}) collective-permute-start(bf16[96,512]{1,0:T(8,128)(2,1)S(1)} %get-tuple-element.57.refs_4_), channel_id=1, source_target_pairs={{0,16},{1,17},{2,18},{3,19},{4,20},{5,21},{6,22},{7,23},{8,24},{9,... | collective-permute-start | bytes 294920 | tf_op jit(solution)/shard_map/ppermute | solution.py:300
  44.5 7.8 %collective-permute-start.12 = (bf16[96,512]{1,0:T(8,128)(2,1)S(1)}, bf16[96,512]{1,0:T(8,128)(2,1)S(1)}, u32[]{:S(2)}, u32[]{:S(2)}) collective-permute-start(bf16[96,512]{1,0:T(8,128)(2,1)S(1)} %get-tuple-element.57.refs_4_), channel_id=1, source_target_pairs={{0,24},{1,25},{2,26},{3,27},{4,28},{5,29},{6,30},{7,31},{8,16},{9,... | collective-permute-start | bytes 294920 | tf_op jit(solution)/shard_map/ppermute | solution.py:300
  53.3 10.4 %collective-permute-start.13 = (bf16[256,512]{1,0:T(8,128)(2,1)S(1)}, bf16[256,512]{1,0:T(8,128)(2,1)S(1)}, u32[]{:S(2)}, u32[]{:S(2)}) collective-permute-start(bf16[256,512]{1,0:T(8,128)(2,1)S(1)} %get-tuple-element.63.refs_1_), channel_id=1, source_target_pairs={{0,2},{1,3},{2,0},{3,1},{4,6},{5,7},{6,4},{7,5},{8,10},{9,11},{10,... | collective-permute-start | bytes 786440 | tf_op jit(solution)/shard_map/ppermute | solution.py:300
  53.8 9.9 %collective-permute-start.14 = (bf16[128,512]{1,0:T(8,128)(2,1)S(1)}, bf16[128,512]{1,0:T(8,128)(2,1)S(1)}, u32[]{:S(2)}, u32[]{:S(2)}) collective-permute-start(bf16[128,512]{1,0:T(8,128)(2,1)S(1)} %get-tuple-element.59.refs_4_), channel_id=1, source_target_pairs={{0,4},{1,5},{2,6},{3,7},{4,0},{5,1},{6,2},{7,3},{8,12},{9,13},{10,... | collective-permute-start | bytes 393224 | tf_op jit(solution)/shard_map/ppermute | solution.py:300
  54.4 9.4 %collective-permute-start.15 = (bf16[128,512]{1,0:T(8,128)(2,1)S(1)}, bf16[128,512]{1,0:T(8,128)(2,1)S(1)}, u32[]{:S(2)}, u32[]{:S(2)}) collective-permute-start(bf16[128,512]{1,0:T(8,128)(2,1)S(1)} %get-tuple-element.59.refs_4_), channel_id=1, source_target_pairs={{0,6},{1,7},{2,4},{3,5},{4,2},{5,3},{6,0},{7,1},{8,14},{9,15},{10,... | collective-permute-start | bytes 393224 | tf_op jit(solution)/shard_map/ppermute | solution.py:300
  57.3 10.7 %copy-start = (bf16[1,5,512,512]{3,2,1,0:T(8,128)(2,1)S(1)}, bf16[1,5,512,512]{3,2,1,0:T(8,128)(2,1)}, u32[]{:S(2)}) copy-start(bf16[1,5,512,512]{3,2,1,0:T(8,128)(2,1)} %refs_2_.3) | copy-start | bytes 7864324
  63.8 6.4 %collective-permute-start.16 = (bf16[1024,512]{1,0:T(8,128)(2,1)S(1)}, bf16[1024,512]{1,0:T(8,128)(2,1)S(1)}, u32[]{:S(2)}, u32[]{:S(2)}) collective-permute-start(bf16[1024,512]{1,0:T(8,128)(2,1)S(1)} %half.1.refs_2_), channel_id=1, source_target_pairs={{0,1},{1,0},{2,3},{3,2},{4,5},{5,4},{6,7},{7,6},{8,9},{9,8},{10,11... | collective-permute-start | bytes 3145736 | tf_op jit(solution)/shard_map/ppermute | solution.py:300
  67.9 2.3 %copy-start.1 = (bf16[1024,512]{1,0:T(8,128)(2,1)S(1)}, bf16[1024,512]{1,0:T(8,128)(2,1)}, u32[]{:S(2)}) copy-start(bf16[1024,512]{1,0:T(8,128)(2,1)} %refs_1_.13) | copy-start | bytes 3145732

commit v4 on v3

--- a/solution.py
+++ b/solution.py
@@ -112,19 +112,11 @@
     wait_all(start_all([pltpu.make_async_copy(a, b, done.at[k]) for k, (a, b) in enumerate(parts)]))
 
 
-def terms_kernel(w, interp, transfers, send, keep, lifted_weights, transfer0, p, t, done):
+def terms_kernel(w, p, transfers, send, keep, lifted_weights, transfer0, t, done):
     core, _, _ = place()
-    half = p.shape[0] // 2
-    first = start_all(
-        [
-            pltpu.make_async_copy(interp.at[k * half : (k + 1) * half, :], p.at[k * half : (k + 1) * half, :], done.at[k])
-            for k in range(2)
-        ]
-    )
-    levels = start_all([pltpu.make_async_copy(transfers.at[0, k + 1], t.at[k], done.at[2 + k]) for k in range(4)])
-    last = start_all([pltpu.make_async_copy(transfers.at[0, 0], transfer0, done.at[6])])
-    wait_all(first)
-    lifted_weights[...] = dot(w[0 : 2 * half, :], p[...], ((0,), (0,))).astype(BF16)
+    levels = start_all([pltpu.make_async_copy(transfers.at[0, k + 1], t.at[k], done.at[k]) for k in range(4)])
+    last = start_all([pltpu.make_async_copy(transfers.at[0, 0], transfer0, done.at[4])])
+    lifted_weights[...] = dot(w[0 : p.shape[0], :], p[...], ((0,), (0,))).astype(BF16)
     theirs = pl.multiple_of((1 - core) * 256, 256)
     mine = pl.multiple_of(core * 256, 256)
     for k in range(4):
@@ -265,30 +257,43 @@
     return call(body, name, [((size, width), F32), ((8, 128), F32)], args, flops, smem=(0,), after=after)
 
 
-def add_levels(far, transfers, half, part):
-    columns = pl.ds(pl.multiple_of(part * 256, 256), 256)
-    value = far[:, columns]
+def columns_of(core):
+    return pl.ds(pl.multiple_of(core * 256, 256), 256)
+
+
+def with_levels(value, transfers, half):
     for level in range(1, 5):
         value = value + dot(transfers[0, level], half[(level - 1) * 256 : level * 256, :], ((1,), (1,)))
-    far[:, columns] = value
-
-
-def far_kernel(transfers, coupled0, mine, far):
+    return value
+
+
+def far_kernel(transfers, coupled0, mine, total, interp, begun, out):
     core, _, _ = place()
-    far[...] = dot(transfers[0, 0], coupled0[...], ((1,), (1,)))
-    add_levels(far, transfers, mine, core)
-
-
-def product_kernel(total, interp, transfers, begun, theirs, product, far, out, done):
+    begun[...] = dot(transfers[0, 0], coupled0[...], ((1,), (1,)))
+    columns = columns_of(core)
+    skeleton = with_levels(begun[:, columns], transfers, mine).astype(BF16)
+    block = total.shape[0] // 2
+    for k in range(2):
+        rows = slice(k * block, (k + 1) * block)
+        out[rows, :] = (total[rows, columns] + dot(interp[rows, :], skeleton)).astype(BF16)
+
+
+def product_kernel(total, interp, transfers, begun, theirs, ready, product, out, done):
     core, _, _ = place()
-    far[...] = begun[...]
-    add_levels(far, transfers, theirs, 1 - core)
-    skeleton = far[...].astype(BF16)
+    columns = columns_of(1 - core)
+    out[:, columns_of(core)] = ready[...]
+    skeleton = with_levels(begun[:, columns], transfers, theirs).astype(BF16)
     copies = []
-    for k in range(total.shape[0] // 128):
-        rows = slice(k * 128, (k + 1) * 128)
-        out[rows, :] = (total[rows, :] + dot(interp[rows, :], skeleton)).astype(BF16)
-        copies += start_all([pltpu.make_async_copy(out.at[rows, :], product.at[rows, :], done.at[k])])
+    block = total.shape[0] // 2
+    for k in range(2):
+        rows = slice(k * block, (k + 1) * block)
+        out[rows, columns] = (total[rows, columns] + dot(interp[rows, :], skeleton)).astype(BF16)
+        copies += start_all(
+            [
+                pltpu.make_async_copy(out.at[pl.ds(at, 128), :], product.at[pl.ds(at, 128), :], done.at[at // 128])
+                for at in range(k * block, (k + 1) * block, 128)
+            ]
+        )
     wait_all(copies)
 
 
@@ -339,14 +344,13 @@
         terms_kernel,
         "terms",
         [rows(1024), rows(1024, F32), rows(512), rows(512)],
-        [payload, kept_in_hbm(interp), kept_in_hbm(transfers)],
+        [payload, interp, kept_in_hbm(transfers)],
         2 * 512 * 512 * (1024 + 4 * 512),
         scratch=[
-            pltpu.VMEM((size, 512), BF16),
             pltpu.VMEM((4, 512, 512), BF16),
-            pltpu.SemaphoreType.DMA((7,)),
+            pltpu.SemaphoreType.DMA((5,)),
         ],
-        in_specs=[in_vmem, in_hbm, in_hbm],
+        in_specs=[in_vmem, in_vmem, in_hbm],
     )
     came = swap(send, 1)
     (term0,) = call(
@@ -357,7 +361,7 @@
         2 * 512 * 512 * 768,
     )
     other0 = swap(term0, 1)
-    total, token = near_of([payload, partner], [None, (2, 1)], None, "near_own", (term0,), cover=20)
+    total, token = near_of([payload], [None], None, "near_self", (term0,), cover=20)
 
     to2, to4, to6, kept, pair = call(
         chip_kernel,
@@ -365,13 +369,13 @@
         [rows(448), rows(288), rows(288), rows(128, F32), rows(128)],
         [keep, came, term0, other0],
         1e6,
-        after=(token,),
+        after=(token, partner),
         scratch=[pltpu.VMEM((1024, 512), F32)],
     )
     from2, from4, from6 = swap(to2, 2), swap(to4, 4), swap(to6, 6)
     late, pair = lax.optimization_barrier((payload, pair))
     staged = staged_across_rows(late)
-    total, token = near_of([outer], [(1, 2)], total, "near_outer", (pair,))
+    total, token = near_of([partner, outer], [(2, 1), (1, 2)], total, "near_one", (pair,))
 
     to8, to16, ring = call(
         row_kernel,
@@ -407,18 +411,20 @@
         half_kernel, "half", [rows(1024)], [coupled1, part2, back2, back4, back6], 1e6, after=(token,)
     )
     theirs = swap(mine, 1)
-    (far,) = call(far_kernel, "far", [rows(512, F32)], [transfers, coupled0, mine], 2 * 512 * 512 * 5 * 400)
+    far, ready = call(
+        far_kernel,
+        "far",
+        [rows(512, F32), ((size, 256), BF16)],
+        [transfers, coupled0, mine, total, interp],
+        2 * 512 * 512 * (512 + 4 * 256 + 512),
+    )
     return call(
         product_kernel,
         "product",
         [((size, width), BF16)],
-        [total, interp, transfers, far, theirs],
-        2 * 512 * 512 * (4 * 256 + 1024),
-        scratch=[
-            pltpu.VMEM((512, 512), F32),
-            pltpu.VMEM((size, width), BF16),
-            pltpu.SemaphoreType.DMA((size // 128,)),
-        ],
+        [total, interp, transfers, far, theirs, ready],
+        2 * 512 * 512 * (4 * 256 + 512),
+        scratch=[pltpu.VMEM((size, width), BF16), pltpu.SemaphoreType.DMA((size // 128,))],
         out_space=pltpu.HBM,
     )[0]
 

time: 73.8 us -> 71.4 us (0.967)
  starting transfers between devices: 31.2 us -> 29.8 us
    ppermute x14, starting transfers between devices: 23.4 us -> 22.1 us  [swap(): lax.ppermute(value, AXIS, [(leaf, leaf ^ mask) for leaf in range(leaves)])]
  transfers between devices with their start and end apart: 17 -> 17, of which waited for: 5 -> 6; matrix products, arithmetic and copies ran while one was open for 0% -> 0% of each run, Pallas kernels for 27% -> 29%
where the time goes in v4:
time: 71.4 us; the launch traced here: 71.2 us
  starting transfers between devices  29.8 us (42%)
  Pallas kernels  24.3 us (34%)
  waiting for transfers between devices  16.7 us (23%)
    pallas_call x14, Pallas kernels, call(): pl.pallas_call(reading, name=name, in_specs=specs, out_specs=[pl.BlockSpe...  24.3 us
    ppermute x14, starting transfers between devices, swap(): lax.ppermute(value, AXIS, [(leaf, leaf ^ mask) for leaf in range(leaves)])  22.1 us
    ppermute x14, waiting for transfers between devices, swap(): lax.ppermute(value, AXIS, [(leaf, leaf ^ mask) for leaf in range(leaves)])  16.7 us
    ppermute x1, starting transfers between devices, moved(): lax.ppermute(value, AXIS, [(a, b) for a, b in pairs if 0 <= b < leaves])  3.02 us
    ppermute x1, starting transfers between devices, turned(): return lax.ppermute(value, AXIS, pairs)  2.67 us
    ppermute x1, starting transfers between devices, staged_across_rows(): lax.ppermute(value, AXIS, [(a, b) for a, b in pairs if 0 <= b < leaves])  2.03 us
  transfers between devices with their start and end apart: 17, of which 6 were waited for; matrix products, arithmetic and copies ran while one was open for 0% of the time, Pallas kernels for 29%

profile of v4, /device:TPU:25, one launch (start us, length us, event | category | flops | bytes accessed | tf_op | source)
XLA Modules:
  0.0 71.2 jit_solution(5993181822452773965)
XLA Ops:
  0.0 0.0 copy-start.1
  0.0 1.3 %pack.1.refs_0_.refs_2_ = bf16[1152,512]{1,0:T(8,128)(2,1)S(1)} custom-call(bf16[64,1024]{1,0:T(8,128)(2,1)} %refs_1_.12, bf16[1024,512]{1,0:T(8,128)(2,1)} %refs_1_.7), custom_call_target="tpu_custom_call" | custom-call | bytes 2359296 | tf_op jit(solution)/shard_map/pack/pallas_call | solution.py:68
  1.3 0.0 copy-start.3
  1.4 0.8 %collective-permute-start.2 = (bf16[1152,512]{1,0:T(8,128)(2,1)S(1)}, bf16[1152,512]{1,0:T(8,128)(2,1)S(1)}, u32[]{:S(2)}, u32[]{:S(2)}) collective-permute-start(bf16[1152,512]{1,0:T(8,128)(2,1)S(1)} %pack.1.refs_0_.refs_2_), channel_id=1, source_target_pairs={{0,1},{1,0},{2,3},{3,2},{4,5},{5,4},{6,7},{7,6},{8,9},{9,8},{10,11... | collective-permute-start | bytes 3538952 | tf_op jit(solution)/shard_map/ppermute | solution.py:305
  2.1 3.0 %collective-permute-start.4 = (bf16[1152,512]{1,0:T(8,128)(2,1)S(1)}, bf16[1152,512]{1,0:T(8,128)(2,1)S(1)}, u32[]{:S(2)}, u32[]{:S(2)}) collective-permute-start(bf16[1152,512]{1,0:T(8,128)(2,1)S(1)} %pack.1.refs_0_.refs_2_), channel_id=1, source_target_pairs={{1,2},{2,1},{3,4},{4,3},{5,6},{6,5},{7,8},{8,7},{9,10},{10,9},{11,... | collective-permute-start | bytes 3538952 | tf_op jit(solution)/shard_map/ppermute | solution.py:309
  5.1 0.0 copy-done.1
  5.1 3.3 %terms.1 = (bf16[1024,512]{1,0:T(8,128)(2,1)S(1)}, f32[1024,512]{1,0:T(8,128)S(1)}, bf16[512,512]{1,0:T(8,128)(2,1)S(1)}, bf16[512,512]{1,0:T(8,128)(2,1)S(1)}) custom-call(bf16[1152,512]{1,0:T(8,128)(2,1)S(1)} %pack.1.refs_0_.refs_2_, bf16[1024,512]{1,0:T(8,128)(2,1)S(1)} %copy-done.1, bf16[1,5,512,512]{3,2,1,0:T(8,128)(2,1)} %refs_2_.3), custom_call_target="tpu_custom_call" | custom-call | flops 1610612736 | bytes 9043968 | tf_op jit(solution)/shard_map/terms/pallas_call | solution.py:68
  8.4 0.0 copy-start.2
  8.4 0.0 copy-start.4
  8.4 0.0 copy-done.3
  8.4 0.6 leaf.1.refs_3_.refs_2_
  9.1 5.5 %collective-permute-start.1 = (bf16[576,512]{1,0:T(8,128)(2,1)S(1)}, bf16[576,512]{1,0:T(8,128)(2,1)S(1)}, u32[]{:S(2)}, u32[]{:S(2)}) collective-permute-start(bf16[576,512]{1,0:T(8,128)(2,1)S(1)} %leaf.1.refs_3_.refs_2_), channel_id=1, source_target_pairs={{0,1},{1,0},{2,3},{3,2},{4,5},{5,4},{6,7},{7,6},{8,9},{9,8},{10,11... | collective-permute-start | bytes 1769480 | tf_op jit(solution)/shard_map/ppermute | solution.py:305
  14.5 0.1 collective-permute-start
  14.6 0.0 copy-done.2
  14.6 0.0 copy-done.4
  14.6 2.4 %near_self.1 = (f32[1024,512]{1,0:T(8,128)S(1)}, f32[8,128]{1,0:T(8,128)S(1)}) custom-call(s32[1,4]{1,0:T(1,128)S(1)} %copy-done.4, bf16[64,1024]{1,0:T(8,128)(2,1)S(1)} %copy-done.2, bf16[1152,512]{1,0:T(8,128)(2,1)S(1)} %pack.1.refs_0_.refs_2_, bf16[576,512]{1,0:T(8,128)(2,1)S(1)} %leaf.1.refs_3_.refs_2_), custom_call_target="tpu_custom_call" | custom-call | flops 32212254720 | bytes 3411984 | tf_op jit(solution)/shard_map/near_self/pallas_call | solution.py:68
  17.1 0.0 collective-permute-done.1.refs_3_.refs_0_
  17.1 0.6 collective-permute-done.refs_1_
  17.7 0.0 collective-permute-done.2.refs_5_.refs_2_
  17.7 0.4 chip.1
  18.1 2.0 %collective-permute-start.3 = (bf16[1152,512]{1,0:T(8,128)(2,1)S(1)}, bf16[1152,512]{1,0:T(8,128)(2,1)S(1)}, u32[]{:S(2)}, u32[]{:S(2)}) collective-permute-start(bf16[1152,512]{1,0:T(8,128)(2,1)S(1)} %pack.1.refs_0_.refs_2_), channel_id=1, source_target_pairs={{0,0},{2,2},{3,3},{4,4},{5,5},{6,14},{7,7},{8,8},{9,1},{10,10},{11... | collective-permute-start | bytes 3538952 | tf_op jit(solution)/shard_map/ppermute | solution.py:314
  20.1 0.1 collective-permute-start.5
  20.2 0.1 collective-permute-start.6
  20.3 3.8 %collective-permute-start.7 = (bf16[288,512]{1,0:T(8,128)(2,1)S(1)}, bf16[288,512]{1,0:T(8,128)(2,1)S(1)}, u32[]{:S(2)}, u32[]{:S(2)}) collective-permute-start(bf16[288,512]{1,0:T(8,128)(2,1)S(1)} %get-tuple-element.46), channel_id=1, source_target_pairs={{0,6},{1,7},{2,4},{3,5},{4,2},{5,3},{6,0},{7,1},{8,14},{9,15},{10,... | collective-permute-start | bytes 884744 | tf_op jit(solution)/shard_map/ppermute | solution.py:305
  24.1 0.0 collective-permute-done.4.refs_3_
  24.1 4.2 %near_one.1 = (f32[1024,512]{1,0:T(8,128)S(1)}, f32[8,128]{1,0:T(8,128)S(1)}) custom-call(s32[1,4]{1,0:T(1,128)S(1)} %copy-done.4, bf16[64,1024]{1,0:T(8,128)(2,1)S(1)} %copy-done.2, bf16[1152,512]{1,0:T(8,128)(2,1)S(1)} %collective-permute-done.2.refs_5_.refs_2_, bf16[1152,512]{1,0:T(8,128)(2,1)S(1)} %collective-permute-done.4.refs_3_, ...), custom_call_target="tpu_custom_call" | custom-call | flops 3221225472 | bytes 6688784 | tf_op jit(solution)/shard_map/near_one/pallas_call | solution.py:68
  28.2 8.0 %collective-permute-done.6.refs_1_.refs_2_ = bf16[288,512]{1,0:T(8,128)(2,1)S(1)} collective-permute-done((bf16[288,512]{1,0:T(8,128)(2,1)S(1)}, bf16[288,512]{1,0:T(8,128)(2,1)S(1)}, u32[]{:S(2)}, u32[]{:S(2)}) %collective-permute-start.6) | collective-permute-done | bytes 294944 | tf_op jit(solution)/shard_map/ppermute | solution.py:305
  36.2 0.0 collective-permute-done.7.refs_2_.refs_3_
  36.2 0.0 collective-permute-done.5.refs_0_.refs_1_
  36.2 0.5 row.1
  36.7 0.0 collective-permute-done.3
  36.7 2.2 %collective-permute-start.9 = (bf16[1152,512]{1,0:T(8,128)(2,1)S(1)}, bf16[1152,512]{1,0:T(8,128)(2,1)S(1)}, u32[]{:S(2)}, u32[]{:S(2)}) collective-permute-start(bf16[1152,512]{1,0:T(8,128)(2,1)S(1)} %collective-permute-done.4.refs_3_), channel_id=1, source_target_pairs={{0,1},{1,0},{2,3},{3,2},{4,5},{5,4},{6,7},{7,6},{8,9},{9,8},{10,11... | collective-permute-start | bytes 3538952 | tf_op jit(solution)/shard_map/ppermute | solution.py:305
  38.9 2.7 %collective-permute-start.8 = (bf16[1152,512]{1,0:T(8,128)(2,1)S(1)}, bf16[1152,512]{1,0:T(8,128)(2,1)S(1)}, u32[]{:S(2)}, u32[]{:S(2)}) collective-permute-start(bf16[1152,512]{1,0:T(8,128)(2,1)S(1)} %collective-permute-done.3), channel_id=1, source_target_pairs={{0,2},{1,7},{2,4},{3,1},{4,6},{5,3},{6,0},{7,5},{8,10},{9,15},{10,... | collective-permute-start | bytes 3538952 | tf_op jit(solution)/shard_map/ppermute | solution.py:318
  41.6 0.0 collective-permute-start.10
  41.6 2.8 %collective-permute-start.11 = (bf16[96,512]{1,0:T(8,128)(2,1)S(1)}, bf16[96,512]{1,0:T(8,128)(2,1)S(1)}, u32[]{:S(2)}, u32[]{:S(2)}) collective-permute-start(bf16[96,512]{1,0:T(8,128)(2,1)S(1)} %get-tuple-element.59.refs_4_), channel_id=1, source_target_pairs={{0,16},{1,17},{2,18},{3,19},{4,20},{5,21},{6,22},{7,23},{8,24},{9,... | collective-permute-start | bytes 294920 | tf_op jit(solution)/shard_map/ppermute | solution.py:305
  44.4 1.1 %collective-permute-start.12 = (bf16[96,512]{1,0:T(8,128)(2,1)S(1)}, bf16[96,512]{1,0:T(8,128)(2,1)S(1)}, u32[]{:S(2)}, u32[]{:S(2)}) collective-permute-start(bf16[96,512]{1,0:T(8,128)(2,1)S(1)} %get-tuple-element.59.refs_4_), channel_id=1, source_target_pairs={{0,24},{1,25},{2,26},{3,27},{4,28},{5,29},{6,30},{7,31},{8,16},{9,... | collective-permute-start | bytes 294920 | tf_op jit(solution)/shard_map/ppermute | solution.py:305
  45.5 1.4 %couple_low.1 = (bf16[512,512]{1,0:T(8,128)(2,1)S(1)}, bf16[256,512]{1,0:T(8,128)(2,1)S(1)}, bf16[128,512]{1,0:T(8,128)(2,1)S(1)}) custom-call(bf16[576,512]{1,0:T(8,128)(2,1)S(1)} %collective-permute-done.1.refs_3_.refs_0_, bf16[448,512]{1,0:T(8,128)(2,1)S(1)} %collective-permute-done.5.refs_0_.refs_1_, ...), custom_call_target="tpu_custom_call" | custom-call | flops 1000000 | bytes 2818048 | tf_op jit(solution)/shard_map/couple_low/pallas_call | solution.py:68
  46.9 0.0 collective-permute-done.9.refs_2_
  46.9 2.5 %near_past.1 = (f32[1024,512]{1,0:T(8,128)S(1)}, f32[8,128]{1,0:T(8,128)S(1)}) custom-call(s32[1,4]{1,0:T(1,128)S(1)} %copy-done.4, bf16[64,1024]{1,0:T(8,128)(2,1)S(1)} %copy-done.2, bf16[1152,512]{1,0:T(8,128)(2,1)S(1)} %collective-permute-done.9.refs_2_, f32[1024,512]{1,0:T(8,128)S(1)} %get-tuple-element.54.refs_3_, ...), custom_call_target="tpu_custom_call" | custom-call | flops 16106127 | bytes 5509136 | tf_op jit(solution)/shard_map/near_past/pallas_call | solution.py:68
  49.4 0.8 %collective-permute-done.11.refs_1_ = bf16[96,512]{1,0:T(8,128)(2,1)S(1)} collective-permute-done((bf16[96,512]{1,0:T(8,128)(2,1)S(1)}, bf16[96,512]{1,0:T(8,128)(2,1)S(1)}, u32[]{:S(2)}, u32[]{:S(2)}) %collective-permute-start.11) | collective-permute-done | bytes 98336 | tf_op jit(solution)/shard_map/ppermute | solution.py:305
  50.1 1.8 %collective-permute-done.12.refs_2_ = bf16[96,512]{1,0:T(8,128)(2,1)S(1)} collective-permute-done((bf16[96,512]{1,0:T(8,128)(2,1)S(1)}, bf16[96,512]{1,0:T(8,128)(2,1)S(1)}, u32[]{:S(2)}, u32[]{:S(2)}) %collective-permute-start.12) | collective-permute-done | bytes 98336 | tf_op jit(solution)/shard_map/ppermute | solution.py:305
  52.0 0.0 collective-permute-done.10.refs_0_
  52.0 1.0 %couple_high.1 = (bf16[256,512]{1,0:T(8,128)(2,1)S(1)}, bf16[128,512]{1,0:T(8,128)(2,1)S(1)}) custom-call(bf16[128,512]{1,0:T(8,128)(2,1)S(1)} %collective-permute-done.10.refs_0_, bf16[96,512]{1,0:T(8,128)(2,1)S(1)} %collective-permute-done.11.refs_1_, bf16[96,512]{1,0:T(8,128)(2,1)S(1)} %collective-permute-done.12.refs_2_, ...), custom_call_target="tpu_custom_call" | custom-call | flops 1000000 | bytes 1081344 | tf_op jit(solution)/shard_map/couple_high/pallas_call | solution.py:68
  53.0 0.2 collective-permute-start.13
  53.2 1.5 %collective-permute-start.14 = (bf16[128,512]{1,0:T(8,128)(2,1)S(1)}, bf16[128,512]{1,0:T(8,128)(2,1)S(1)}, u32[]{:S(2)}, u32[]{:S(2)}) collective-permute-start(bf16[128,512]{1,0:T(8,128)(2,1)S(1)} %get-tuple-element.61.refs_4_), channel_id=1, source_target_pairs={{0,4},{1,5},{2,6},{3,7},{4,0},{5,1},{6,2},{7,3},{8,12},{9,13},{10,... | collective-permute-start | bytes 393224 | tf_op jit(solution)/shard_map/ppermute | solution.py:305
  54.7 2.2 %collective-permute-start.15 = (bf16[128,512]{1,0:T(8,128)(2,1)S(1)}, bf16[128,512]{1,0:T(8,128)(2,1)S(1)}, u32[]{:S(2)}, u32[]{:S(2)}) collective-permute-start(bf16[128,512]{1,0:T(8,128)(2,1)S(1)} %get-tuple-element.61.refs_4_), channel_id=1, source_target_pairs={{0,6},{1,7},{2,4},{3,5},{4,2},{5,3},{6,0},{7,1},{8,14},{9,15},{10,... | collective-permute-start | bytes 393224 | tf_op jit(solution)/shard_map/ppermute | solution.py:305
  56.9 0.0 collective-permute-done.8.refs_2_
  56.9 0.0 copy-start
  56.9 2.4 %near_second.1 = (f32[1024,512]{1,0:T(8,128)S(1)}, f32[8,128]{1,0:T(8,128)S(1)}) custom-call(s32[1,4]{1,0:T(1,128)S(1)} %copy-done.4, bf16[64,1024]{1,0:T(8,128)(2,1)S(1)} %copy-done.2, bf16[1152,512]{1,0:T(8,128)(2,1)S(1)} %collective-permute-done.8.refs_2_, f32[1024,512]{1,0:T(8,128)S(1)} %get-tuple-element.57.refs_3_, ...), custom_call_target="tpu_custom_call" | custom-call | flops 1610612736 | bytes 5509136 | tf_op jit(solution)/shard_map/near_second/pallas_call | solution.py:68
  59.3 5.1 %collective-permute-done.14.refs_3_ = bf16[128,512]{1,0:T(8,128)(2,1)S(1)} collective-permute-done((bf16[128,512]{1,0:T(8,128)(2,1)S(1)}, bf16[128,512]{1,0:T(8,128)(2,1)S(1)}, u32[]{:S(2)}, u32[]{:S(2)}) %collective-permute-start.14) | collective-permute-done | bytes 131104 | tf_op jit(solution)/shard_map/ppermute | solution.py:305
  64.4 0.0 collective-permute-done.15.refs_4_
  64.4 0.0 collective-permute-done.13.refs_2_
  64.4 0.1 half.1.refs_2_
  64.5 1.9 %collective-permute-start.16 = (bf16[1024,512]{1,0:T(8,128)(2,1)S(1)}, bf16[1024,512]{1,0:T(8,128)(2,1)S(1)}, u32[]{:S(2)}, u32[]{:S(2)}) collective-permute-start(bf16[1024,512]{1,0:T(8,128)(2,1)S(1)} %half.1.refs_2_), channel_id=1, source_target_pairs={{0,1},{1,0},{2,3},{3,2},{4,5},{5,4},{6,7},{7,6},{8,9},{9,8},{10,11... | collective-permute-start | bytes 3145736 | tf_op jit(solution)/shard_map/ppermute | solution.py:305
  66.3 0.0 copy-done
  66.3 1.9 %far.1 = (f32[512,512]{1,0:T(8,128)S(1)}, bf16[1024,256]{1,0:T(8,128)(2,1)S(1)}) custom-call(bf16[1,5,512,512]{3,2,1,0:T(8,128)(2,1)S(1)} %copy-done, bf16[512,512]{1,0:T(8,128)(2,1)S(1)} %get-tuple-element.63.refs_1_, bf16[1024,512]{1,0:T(8,128)(2,1)S(1)} %half.1.refs_2_, f32[1024,512]{1,0:T(8,128)S(1)} %get-tuple-element.62.refs_3_.refs_0_, ...), custom_call_target="tpu_custom_call" | custom-call | flops 1073741824 | bytes 8912896 | tf_op jit(solution)/shard_map/far/pallas_call | solution.py:68
  68.2 0.4 collective-permute-done.16.refs_4_
  68.6 2.4 %product.1 = bf16[1024,512]{1,0:T(8,128)(2,1)} custom-call(f32[1024,512]{1,0:T(8,128)S(1)} %get-tuple-element.62.refs_3_.refs_0_, bf16[1024,512]{1,0:T(8,128)(2,1)S(1)} %copy-done.1, bf16[1,5,512,512]{3,2,1,0:T(8,128)(2,1)S(1)} %copy-done, f32[512,512]{1,0:T(8,128)S(1)} %get-tuple-element.67.refs_3_, bf16[1024,512]{1,0:T(8,128)(2,1)S(1)} %collective-permute-done.16.refs_4_, ...), custom_call_target="tpu_custom_call" | custom-call | flops 805306368 | bytes 9437184 | tf_op jit(solution)/shard_map/product/pallas_call | solution.py:68
Async XLA Ops:
  0.0 5.1 %copy-start.1 = (bf16[1024,512]{1,0:T(8,128)(2,1)S(1)}, bf16[1024,512]{1,0:T(8,128)(2,1)}, u32[]{:S(2)}) copy-start(bf16[1024,512]{1,0:T(8,128)(2,1)} %refs_1_.13) | copy-start | bytes 3145732
  1.3 7.1 %copy-start.3 = (s32[1,512]{1,0:T(1,128)S(1)}, s32[1,512]{1,0:T(1,128)}, u32[]{:S(2)}) copy-start(s32[1,512]{1,0:T(1,128)} %refs_3_.1) | copy-start | bytes 6148
  1.4 16.3 %collective-permute-start.2 = (bf16[1152,512]{1,0:T(8,128)(2,1)S(1)}, bf16[1152,512]{1,0:T(8,128)(2,1)S(1)}, u32[]{:S(2)}, u32[]{:S(2)}) collective-permute-start(bf16[1152,512]{1,0:T(8,128)(2,1)S(1)} %pack.1.refs_0_.refs_2_), channel_id=1, source_target_pairs={{0,1},{1,0},{2,3},{3,2},{4,5},{5,4},{6,7},{7,6},{8,9},{9,8},{10,11... | collective-permute-start | bytes 3538952 | tf_op jit(solution)/shard_map/ppermute | solution.py:305
  2.1 22.0 %collective-permute-start.4 = (bf16[1152,512]{1,0:T(8,128)(2,1)S(1)}, bf16[1152,512]{1,0:T(8,128)(2,1)S(1)}, u32[]{:S(2)}, u32[]{:S(2)}) collective-permute-start(bf16[1152,512]{1,0:T(8,128)(2,1)S(1)} %pack.1.refs_0_.refs_2_), channel_id=1, source_target_pairs={{1,2},{2,1},{3,4},{4,3},{5,6},{6,5},{7,8},{8,7},{9,10},{10,9},{11,... | collective-permute-start | bytes 3538952 | tf_op jit(solution)/shard_map/ppermute | solution.py:309
  8.4 6.2 %copy-start.2 = (bf16[64,1024]{1,0:T(8,128)(2,1)S(1)}, bf16[64,1024]{1,0:T(8,128)(2,1)}, u32[]{:S(2)}) copy-start(bf16[64,1024]{1,0:T(8,128)(2,1)} %refs_1_.12) | copy-start | bytes 393220
  8.4 6.2 %copy-start.4 = (s32[1,4]{1,0:T(1,128)S(1)}, s32[1,4]{1,0:T(1,128)}, u32[]{:S(2)}) copy-start(s32[1,4]{1,0:T(1,128)} %refs_0_.10) | copy-start | bytes 52
  9.1 8.0 %collective-permute-start.1 = (bf16[576,512]{1,0:T(8,128)(2,1)S(1)}, bf16[576,512]{1,0:T(8,128)(2,1)S(1)}, u32[]{:S(2)}, u32[]{:S(2)}) collective-permute-start(bf16[576,512]{1,0:T(8,128)(2,1)S(1)} %leaf.1.refs_3_.refs_2_), channel_id=1, source_target_pairs={{0,1},{1,0},{2,3},{3,2},{4,5},{5,4},{6,7},{7,6},{8,9},{9,8},{10,11... | collective-permute-start | bytes 1769480 | tf_op jit(solution)/shard_map/ppermute | solution.py:305
  14.5 3.1 %collective-permute-start = (bf16[1024,512]{1,0:T(8,128)(2,1)S(1)}, bf16[1024,512]{1,0:T(8,128)(2,1)S(1)}, u32[]{:S(2)}, u32[]{:S(2)}) collective-permute-start(bf16[1024,512]{1,0:T(8,128)(2,1)S(1)} %get-tuple-element.38), channel_id=1, source_target_pairs={{0,1},{1,0},{2,3},{3,2},{4,5},{5,4},{6,7},{7,6},{8,9},{9,8},{10,11... | collective-permute-start | bytes 3145736 | tf_op jit(solution)/shard_map/ppermute | solution.py:305
  18.1 18.6 %collective-permute-start.3 = (bf16[1152,512]{1,0:T(8,128)(2,1)S(1)}, bf16[1152,512]{1,0:T(8,128)(2,1)S(1)}, u32[]{:S(2)}, u32[]{:S(2)}) collective-permute-start(bf16[1152,512]{1,0:T(8,128)(2,1)S(1)} %pack.1.refs_0_.refs_2_), channel_id=1, source_target_pairs={{0,0},{2,2},{3,3},{4,4},{5,5},{6,14},{7,7},{8,8},{9,1},{10,10},{11... | collective-permute-start | bytes 3538952 | tf_op jit(solution)/shard_map/ppermute | solution.py:314
  20.1 16.1 %collective-permute-start.5 = (bf16[448,512]{1,0:T(8,128)(2,1)S(1)}, bf16[448,512]{1,0:T(8,128)(2,1)S(1)}, u32[]{:S(2)}, u32[]{:S(2)}) collective-permute-start(bf16[448,512]{1,0:T(8,128)(2,1)S(1)} %get-tuple-element.44), channel_id=1, source_target_pairs={{0,2},{1,3},{2,0},{3,1},{4,6},{5,7},{6,4},{7,5},{8,10},{9,11},{10,... | collective-permute-start | bytes 1376264 | tf_op jit(solution)/shard_map/ppermute | solution.py:305
  20.2 16.0 %collective-permute-start.6 = (bf16[288,512]{1,0:T(8,128)(2,1)S(1)}, bf16[288,512]{1,0:T(8,128)(2,1)S(1)}, u32[]{:S(2)}, u32[]{:S(2)}) collective-permute-start(bf16[288,512]{1,0:T(8,128)(2,1)S(1)} %get-tuple-element.45), channel_id=1, source_target_pairs={{0,4},{1,5},{2,6},{3,7},{4,0},{5,1},{6,2},{7,3},{8,12},{9,13},{10,... | collective-permute-start | bytes 884744 | tf_op jit(solution)/shard_map/ppermute | solution.py:305
  20.3 15.9 %collective-permute-start.7 = (bf16[288,512]{1,0:T(8,128)(2,1)S(1)}, bf16[288,512]{1,0:T(8,128)(2,1)S(1)}, u32[]{:S(2)}, u32[]{:S(2)}) collective-permute-start(bf16[288,512]{1,0:T(8,128)(2,1)S(1)} %get-tuple-element.46), channel_id=1, source_target_pairs={{0,6},{1,7},{2,4},{3,5},{4,2},{5,3},{6,0},{7,1},{8,14},{9,15},{10,... | collective-permute-start | bytes 884744 | tf_op jit(solution)/shard_map/ppermute | solution.py:305
  36.7 10.2 %collective-permute-start.9 = (bf16[1152,512]{1,0:T(8,128)(2,1)S(1)}, bf16[1152,512]{1,0:T(8,128)(2,1)S(1)}, u32[]{:S(2)}, u32[]{:S(2)}) collective-permute-start(bf16[1152,512]{1,0:T(8,128)(2,1)S(1)} %collective-permute-done.4.refs_3_), channel_id=1, source_target_pairs={{0,1},{1,0},{2,3},{3,2},{4,5},{5,4},{6,7},{7,6},{8,9},{9,8},{10,11... | collective-permute-start | bytes 3538952 | tf_op jit(solution)/shard_map/ppermute | solution.py:305
  38.9 18.0 %collective-permute-start.8 = (bf16[1152,512]{1,0:T(8,128)(2,1)S(1)}, bf16[1152,512]{1,0:T(8,128)(2,1)S(1)}, u32[]{:S(2)}, u32[]{:S(2)}) collective-permute-start(bf16[1152,512]{1,0:T(8,128)(2,1)S(1)} %collective-permute-done.3), channel_id=1, source_target_pairs={{0,2},{1,7},{2,4},{3,1},{4,6},{5,3},{6,0},{7,5},{8,10},{9,15},{10,... | collective-permute-start | bytes 3538952 | tf_op jit(solution)/shard_map/ppermute | solution.py:318
  41.6 10.4 %collective-permute-start.10 = (bf16[128,512]{1,0:T(8,128)(2,1)S(1)}, bf16[128,512]{1,0:T(8,128)(2,1)S(1)}, u32[]{:S(2)}, u32[]{:S(2)}) collective-permute-start(bf16[128,512]{1,0:T(8,128)(2,1)S(1)} %get-tuple-element.58.refs_3_), channel_id=1, source_target_pairs={{0,8},{1,9},{2,10},{3,11},{4,12},{5,13},{6,14},{7,15},{8,0},{9,1},... | collective-permute-start | bytes 393224 | tf_op jit(solution)/shard_map/ppermute | solution.py:305
  41.6 8.5 %collective-permute-start.11 = (bf16[96,512]{1,0:T(8,128)(2,1)S(1)}, bf16[96,512]{1,0:T(8,128)(2,1)S(1)}, u32[]{:S(2)}, u32[]{:S(2)}) collective-permute-start(bf16[96,512]{1,0:T(8,128)(2,1)S(1)} %get-tuple-element.59.refs_4_), channel_id=1, source_target_pairs={{0,16},{1,17},{2,18},{3,19},{4,20},{5,21},{6,22},{7,23},{8,24},{9,... | collective-permute-start | bytes 294920 | tf_op jit(solution)/shard_map/ppermute | solution.py:305
  44.4 7.6 %collective-permute-start.12 = (bf16[96,512]{1,0:T(8,128)(2,1)S(1)}, bf16[96,512]{1,0:T(8,128)(2,1)S(1)}, u32[]{:S(2)}, u32[]{:S(2)}) collective-permute-start(bf16[96,512]{1,0:T(8,128)(2,1)S(1)} %get-tuple-element.59.refs_4_), channel_id=1, source_target_pairs={{0,24},{1,25},{2,26},{3,27},{4,28},{5,29},{6,30},{7,31},{8,16},{9,... | collective-permute-start | bytes 294920 | tf_op jit(solution)/shard_map/ppermute | solution.py:305
  53.0 11.4 %collective-permute-start.13 = (bf16[256,512]{1,0:T(8,128)(2,1)S(1)}, bf16[256,512]{1,0:T(8,128)(2,1)S(1)}, u32[]{:S(2)}, u32[]{:S(2)}) collective-permute-start(bf16[256,512]{1,0:T(8,128)(2,1)S(1)} %get-tuple-element.65.refs_1_), channel_id=1, source_target_pairs={{0,2},{1,3},{2,0},{3,1},{4,6},{5,7},{6,4},{7,5},{8,10},{9,11},{10,... | collective-permute-start | bytes 786440 | tf_op jit(solution)/shard_map/ppermute | solution.py:305
  53.2 11.2 %collective-permute-start.14 = (bf16[128,512]{1,0:T(8,128)(2,1)S(1)}, bf16[128,512]{1,0:T(8,128)(2,1)S(1)}, u32[]{:S(2)}, u32[]{:S(2)}) collective-permute-start(bf16[128,512]{1,0:T(8,128)(2,1)S(1)} %get-tuple-element.61.refs_4_), channel_id=1, source_target_pairs={{0,4},{1,5},{2,6},{3,7},{4,0},{5,1},{6,2},{7,3},{8,12},{9,13},{10,... | collective-permute-start | bytes 393224 | tf_op jit(solution)/shard_map/ppermute | solution.py:305
  54.7 9.7 %collective-permute-start.15 = (bf16[128,512]{1,0:T(8,128)(2,1)S(1)}, bf16[128,512]{1,0:T(8,128)(2,1)S(1)}, u32[]{:S(2)}, u32[]{:S(2)}) collective-permute-start(bf16[128,512]{1,0:T(8,128)(2,1)S(1)} %get-tuple-element.61.refs_4_), channel_id=1, source_target_pairs={{0,6},{1,7},{2,4},{3,5},{4,2},{5,3},{6,0},{7,1},{8,14},{9,15},{10,... | collective-permute-start | bytes 393224 | tf_op jit(solution)/shard_map/ppermute | solution.py:305
  56.9 9.4 %copy-start = (bf16[1,5,512,512]{3,2,1,0:T(8,128)(2,1)S(1)}, bf16[1,5,512,512]{3,2,1,0:T(8,128)(2,1)}, u32[]{:S(2)}) copy-start(bf16[1,5,512,512]{3,2,1,0:T(8,128)(2,1)} %refs_2_.3) | copy-start | bytes 7864324
  64.5 4.1 %collective-permute-start.16 = (bf16[1024,512]{1,0:T(8,128)(2,1)S(1)}, bf16[1024,512]{1,0:T(8,128)(2,1)S(1)}, u32[]{:S(2)}, u32[]{:S(2)}) collective-permute-start(bf16[1024,512]{1,0:T(8,128)(2,1)S(1)} %half.1.refs_2_), channel_id=1, source_target_pairs={{0,1},{1,0},{2,3},{3,2},{4,5},{5,4},{6,7},{7,6},{8,9},{9,8},{10,11... | collective-permute-start | bytes 3145736 | tf_op jit(solution)/shard_map/ppermute | solution.py:305

commit v5 on v4

--- a/solution.py
+++ b/solution.py
@@ -112,37 +112,33 @@
     wait_all(start_all([pltpu.make_async_copy(a, b, done.at[k]) for k, (a, b) in enumerate(parts)]))
 
 
-def terms_kernel(w, p, transfers, send, keep, lifted_weights, transfer0, t, done):
+def terms_kernel(w, p, index, transfers, send, keep, lifted_weights, t, done):
     core, _, _ = place()
-    levels = start_all([pltpu.make_async_copy(transfers.at[0, k + 1], t.at[k], done.at[k]) for k in range(4)])
-    last = start_all([pltpu.make_async_copy(transfers.at[0, 0], transfer0, done.at[4])])
-    lifted_weights[...] = dot(w[0 : p.shape[0], :], p[...], ((0,), (0,))).astype(BF16)
+    copies = start_all([pltpu.make_async_copy(transfers.at[0, (k + 1) % 5], t.at[k], done.at[k]) for k in range(5)])
+    size = p.shape[0]
+    lifted_weights[...] = dot(w[0:size, :], p[...], ((0,), (0,))).astype(BF16)
+    rank = lax.broadcasted_iota(jnp.int32, (size // 2, index.shape[1]), 0)
+    chosen = dot(w[size : size + 64, :], (rank == index[...]).astype(F32).astype(BF16))
+    chosen = chosen + dot(w[size + 64 : size + 128, :], (rank + size // 2 == index[...]).astype(F32).astype(BF16))
+    send[1536:1600, :] = chosen.astype(BF16)
     theirs = pl.multiple_of((1 - core) * 256, 256)
     mine = pl.multiple_of(core * 256, 256)
     for k in range(4):
-        levels[k].wait()
+        copies[k].wait()
         send[k * 256 : (k + 1) * 256, :] = dot(lifted_weights[pl.ds(theirs, 256), :], t[k]).astype(BF16)
         keep[k * 256 : (k + 1) * 256, :] = dot(lifted_weights[pl.ds(mine, 256), :], t[k])
-    wait_all(last)
-
-
-def leaf_kernel(lifted_weights, t, payload, index, out):
-    size = payload.shape[0] - 128
-    out[0:512, :] = dot(lifted_weights[...], t[...]).astype(BF16)
-    rank = lax.broadcasted_iota(jnp.int32, (size // 2, index.shape[1]), 0)
-    chosen = dot(payload[size : size + 64, :], (rank == index[...]).astype(F32).astype(BF16))
-    chosen = chosen + dot(payload[size + 64 : size + 128, :], (rank + size // 2 == index[...]).astype(F32).astype(BF16))
-    out[512:576, :] = chosen.astype(BF16)
-
-
-def chip_kernel(keep, came, mine, theirs, to2, to4, to6, kept, pair, total):
+    copies[4].wait()
+    send[1024:1536, :] = dot(lifted_weights[...], t[4]).astype(BF16)
+
+
+def chip_kernel(keep, came, sent, to2, to4, to6, kept, pair, total):
     core, x, _ = place()
-    mine, theirs = mine[512:576, :], theirs[512:576, :]
+    mine, theirs = sent[1536:1600, :], came[1536:1600, :]
     first = jnp.where(core == 0, mine, theirs)
     second = jnp.where(core == 0, theirs, mine)
     pair[0:64, :] = first
     pair[64:128, :] = second
-    total[...] = keep[...] + came[...].astype(F32)
+    total[...] = keep[...] + came[0:1024, :].astype(F32)
     to2[192:448, :] = total[0:256, :].astype(BF16)
     to2[128:192, :] = jnp.concatenate([first[:, :256], second[:, :256]], axis=1)
     for level, at in ((3, 0), (4, 64)):
@@ -176,10 +172,10 @@
     return dot(sums, gaussian(lifted(sibling, True), lifted(own, False))).astype(BF16)
 
 
-def couple_low_kernel(term0, from2, from4, from6, pair, ring, out0, out1, out2):
+def couple_low_kernel(came, from2, from4, from6, pair, ring, out0, out1, out2):
     core, x, _ = place()
     first, second = pair[0:64, :], pair[64:128, :]
-    out0[...] = couple(term0[0:512, :], jnp.where(core == 0, first, second), jnp.where(core == 0, second, first))
+    out0[...] = couple(came[1024:1536, :], jnp.where(core == 0, first, second), jnp.where(core == 0, second, first))
     own = jnp.concatenate([first[:, 0:256], second[:, 0:256]], axis=1)
     out1[...] = couple(from2[192:448, :], own, from2[128:192, :])
     low = x & 2
@@ -340,34 +336,27 @@
     )
     outer = moved(payload, -1, 1)
     partner = swap(payload, 1)
-    send, keep, lifted_weights, transfer0 = call(
+    send, keep = call(
         terms_kernel,
         "terms",
-        [rows(1024), rows(1024, F32), rows(512), rows(512)],
-        [payload, interp, kept_in_hbm(transfers)],
-        2 * 512 * 512 * (1024 + 4 * 512),
+        [rows(1600), rows(1024, F32)],
+        [payload, interp, skel_index, kept_in_hbm(transfers)],
+        2 * 512 * 512 * (1024 + 5 * 512),
         scratch=[
-            pltpu.VMEM((4, 512, 512), BF16),
+            pltpu.VMEM((512, 512), BF16),
+            pltpu.VMEM((5, 512, 512), BF16),
             pltpu.SemaphoreType.DMA((5,)),
         ],
-        in_specs=[in_vmem, in_vmem, in_hbm],
+        in_specs=[in_vmem, in_vmem, in_vmem, in_hbm],
     )
     came = swap(send, 1)
-    (term0,) = call(
-        leaf_kernel,
-        "leaf",
-        [rows(576)],
-        [lifted_weights, transfer0, payload, skel_index],
-        2 * 512 * 512 * 768,
-    )
-    other0 = swap(term0, 1)
-    total, token = near_of([payload], [None], None, "near_self", (term0,), cover=20)
+    total, token = near_of([payload], [None], None, "near_self", (send,), cover=20)
 
     to2, to4, to6, kept, pair = call(
         chip_kernel,
         "chip",
         [rows(448), rows(288), rows(288), rows(128, F32), rows(128)],
-        [keep, came, term0, other0],
+        [keep, came, send],
         1e6,
         after=(token, partner),
         scratch=[pltpu.VMEM((1024, 512), F32)],
@@ -393,7 +382,7 @@
         couple_low_kernel,
         "couple_low",
         [rows(512), rows(256), rows(128)],
-        [other0, from2, from4, from6, pair, ring],
+        [came, from2, from4, from6, pair, ring],
         1e6,
     )
     total, token = near_of([past], [(3, 0)], total, "near_past", (coupled2,), cover=0.01)

time: 71.4 us -> 70.8 us (level)
  waiting for transfers between devices: 16.7 us -> 18.7 us
  starting transfers between devices: 29.8 us -> 28 us
    ppermute x14 -> x13, waiting for transfers between devices: 16.7 us -> 18.7 us  [swap(): lax.ppermute(value, AXIS, [(leaf, leaf ^ mask) for leaf in range(leaves)])]
    ppermute x14 -> x13, starting transfers between devices: 22.1 us -> 20.5 us  [swap(): lax.ppermute(value, AXIS, [(leaf, leaf ^ mask) for leaf in range(leaves)])]
    pallas_call x14 -> x13, Pallas kernels: 24.3 us -> 23.6 us  [call(): pl.pallas_call(reading, name=name, in_specs=specs, out_specs=[pl.BlockSpe...]
  transfers between devices with their start and end apart: 17 -> 16, of which waited for: 6 -> 6; matrix products, arithmetic and copies ran while one was open for 0% -> 0% of each run, Pallas kernels for 29% -> 28%
where the time goes in v5:
time: 70.8 us; the launch traced here: 70.6 us
  starting transfers between devices  28 us (40%)
  Pallas kernels  23.6 us (33%)
  waiting for transfers between devices  18.7 us (26%)
    pallas_call x13, Pallas kernels, call(): pl.pallas_call(reading, name=name, in_specs=specs, out_specs=[pl.BlockSpe...  23.6 us
    ppermute x13, starting transfers between devices, swap(): lax.ppermute(value, AXIS, [(leaf, leaf ^ mask) for leaf in range(leaves)])  20.5 us
    ppermute x13, waiting for transfers between devices, swap(): lax.ppermute(value, AXIS, [(leaf, leaf ^ mask) for leaf in range(leaves)])  18.7 us
    ppermute x1, starting transfers between devices, moved(): lax.ppermute(value, AXIS, [(a, b) for a, b in pairs if 0 <= b < leaves])  3.02 us
    ppermute x1, starting transfers between devices, turned(): return lax.ppermute(value, AXIS, pairs)  2.41 us
    ppermute x1, starting transfers between devices, staged_across_rows(): lax.ppermute(value, AXIS, [(a, b) for a, b in pairs if 0 <= b < leaves])  2.03 us
  transfers between devices with their start and end apart: 16, of which 6 were waited for; matrix products, arithmetic and copies ran while one was open for 0% of the time, Pallas kernels for 28%

profile of v5, /device:TPU:25, one launch (start us, length us, event | category | flops | bytes accessed | tf_op | source)
XLA Modules:
  0.0 70.6 jit_solution(17627506312531826491)
XLA Ops:
  0.0 0.0 copy-start.4
  0.0 0.0 copy-start.1
  0.0 1.3 %pack.1.refs_0_.refs_2_ = bf16[1152,512]{1,0:T(8,128)(2,1)S(1)} custom-call(bf16[64,1024]{1,0:T(8,128)(2,1)} %refs_1_.12, bf16[1024,512]{1,0:T(8,128)(2,1)} %refs_1_.7), custom_call_target="tpu_custom_call" | custom-call | bytes 2359296 | tf_op jit(solution)/shard_map/pack/pallas_call | solution.py:68
  1.3 0.0 copy-start.2
  1.4 0.0 copy-start.3
  1.4 0.8 %collective-permute-start.1 = (bf16[1152,512]{1,0:T(8,128)(2,1)S(1)}, bf16[1152,512]{1,0:T(8,128)(2,1)S(1)}, u32[]{:S(2)}, u32[]{:S(2)}) collective-permute-start(bf16[1152,512]{1,0:T(8,128)(2,1)S(1)} %pack.1.refs_0_.refs_2_), channel_id=1, source_target_pairs={{0,1},{1,0},{2,3},{3,2},{4,5},{5,4},{6,7},{7,6},{8,9},{9,8},{10,11... | collective-permute-start | bytes 3538952 | tf_op jit(solution)/shard_map/ppermute | solution.py:301
  2.1 3.0 %collective-permute-start.3 = (bf16[1152,512]{1,0:T(8,128)(2,1)S(1)}, bf16[1152,512]{1,0:T(8,128)(2,1)S(1)}, u32[]{:S(2)}, u32[]{:S(2)}) collective-permute-start(bf16[1152,512]{1,0:T(8,128)(2,1)S(1)} %pack.1.refs_0_.refs_2_), channel_id=1, source_target_pairs={{1,2},{2,1},{3,4},{4,3},{5,6},{6,5},{7,8},{8,7},{9,10},{10,9},{11,... | collective-permute-start | bytes 3538952 | tf_op jit(solution)/shard_map/ppermute | solution.py:305
  5.1 0.0 copy-done.4
  5.2 0.0 copy-done.1
  5.2 3.3 %terms.1 = (bf16[1600,512]{1,0:T(8,128)(2,1)S(1)}, f32[1024,512]{1,0:T(8,128)S(1)}) custom-call(bf16[1152,512]{1,0:T(8,128)(2,1)S(1)} %pack.1.refs_0_.refs_2_, bf16[1024,512]{1,0:T(8,128)(2,1)S(1)} %copy-done.1, s32[1,512]{1,0:T(1,128)S(1)} %copy-done.4, bf16[1,5,512,512]{3,2,1,0:T(8,128)(2,1)} %refs_2_.3), custom_call_target="tpu_custom_call" | custom-call | flops 1879048192 | bytes 8587264 | tf_op jit(solution)/shard_map/terms/pallas_call | solution.py:68
  8.5 5.5 %collective-permute-start = (bf16[1600,512]{1,0:T(8,128)(2,1)S(1)}, bf16[1600,512]{1,0:T(8,128)(2,1)S(1)}, u32[]{:S(2)}, u32[]{:S(2)}) collective-permute-start(bf16[1600,512]{1,0:T(8,128)(2,1)S(1)} %get-tuple-element.36.refs_3_.refs_2_), channel_id=1, source_target_pairs={{0,1},{1,0},{2,3},{3,2},{4,5},{5,4},{6,7},{7,6},{8,9},{9,8},{10,11... | collective-permute-start | bytes 4915208 | tf_op jit(solution)/shard_map/ppermute | solution.py:301
  14.0 0.0 copy-done.2
  14.0 0.0 copy-done.3
  14.0 2.4 %near_self.1 = (f32[1024,512]{1,0:T(8,128)S(1)}, f32[8,128]{1,0:T(8,128)S(1)}) custom-call(s32[1,4]{1,0:T(1,128)S(1)} %copy-done.3, bf16[64,1024]{1,0:T(8,128)(2,1)S(1)} %copy-done.2, bf16[1152,512]{1,0:T(8,128)(2,1)S(1)} %pack.1.refs_0_.refs_2_, bf16[1600,512]{1,0:T(8,128)(2,1)S(1)} %get-tuple-element.36.refs_3_.refs_2_), custom_call_target="tpu_custom_call" | custom-call | flops 32212254720 | bytes 3411984 | tf_op jit(solution)/shard_map/near_self/pallas_call | solution.py:68
  16.4 0.0 collective-permute-done.1.refs_4_.refs_2_
  16.4 0.7 %collective-permute-done.refs_1_.refs_0_ = bf16[1600,512]{1,0:T(8,128)(2,1)S(1)} collective-permute-done((bf16[1600,512]{1,0:T(8,128)(2,1)S(1)}, bf16[1600,512]{1,0:T(8,128)(2,1)S(1)}, u32[]{:S(2)}, u32[]{:S(2)}) %collective-permute-start) | collective-permute-done | bytes 1638432 | tf_op jit(solution)/shard_map/ppermute | solution.py:301
  17.1 0.4 chip.1
  17.5 2.0 %collective-permute-start.2 = (bf16[1152,512]{1,0:T(8,128)(2,1)S(1)}, bf16[1152,512]{1,0:T(8,128)(2,1)S(1)}, u32[]{:S(2)}, u32[]{:S(2)}) collective-permute-start(bf16[1152,512]{1,0:T(8,128)(2,1)S(1)} %pack.1.refs_0_.refs_2_), channel_id=1, source_target_pairs={{0,0},{2,2},{3,3},{4,4},{5,5},{6,14},{7,7},{8,8},{9,1},{10,10},{11... | collective-permute-start | bytes 3538952 | tf_op jit(solution)/shard_map/ppermute | solution.py:310
  19.5 0.1 collective-permute-start.4
  19.6 0.1 collective-permute-start.5
  19.7 3.8 %collective-permute-start.6 = (bf16[288,512]{1,0:T(8,128)(2,1)S(1)}, bf16[288,512]{1,0:T(8,128)(2,1)S(1)}, u32[]{:S(2)}, u32[]{:S(2)}) collective-permute-start(bf16[288,512]{1,0:T(8,128)(2,1)S(1)} %get-tuple-element.42), channel_id=1, source_target_pairs={{0,6},{1,7},{2,4},{3,5},{4,2},{5,3},{6,0},{7,1},{8,14},{9,15},{10,... | collective-permute-start | bytes 884744 | tf_op jit(solution)/shard_map/ppermute | solution.py:301
  23.5 0.0 collective-permute-done.3.refs_3_
  23.5 4.1 %near_one.1 = (f32[1024,512]{1,0:T(8,128)S(1)}, f32[8,128]{1,0:T(8,128)S(1)}) custom-call(s32[1,4]{1,0:T(1,128)S(1)} %copy-done.3, bf16[64,1024]{1,0:T(8,128)(2,1)S(1)} %copy-done.2, bf16[1152,512]{1,0:T(8,128)(2,1)S(1)} %collective-permute-done.1.refs_4_.refs_2_, bf16[1152,512]{1,0:T(8,128)(2,1)S(1)} %collective-permute-done.3.refs_3_, ...), custom_call_target="tpu_custom_call" | custom-call | flops 3221225472 | bytes 6688784 | tf_op jit(solution)/shard_map/near_one/pallas_call | solution.py:68
  27.5 9.2 %collective-permute-done.5.refs_1_.refs_2_ = bf16[288,512]{1,0:T(8,128)(2,1)S(1)} collective-permute-done((bf16[288,512]{1,0:T(8,128)(2,1)S(1)}, bf16[288,512]{1,0:T(8,128)(2,1)S(1)}, u32[]{:S(2)}, u32[]{:S(2)}) %collective-permute-start.5) | collective-permute-done | bytes 294944 | tf_op jit(solution)/shard_map/ppermute | solution.py:301
  36.8 0.0 collective-permute-done.6.refs_2_.refs_3_
  36.8 0.0 collective-permute-done.4.refs_0_.refs_1_
  36.8 0.5 row.1
  37.3 0.0 collective-permute-done.2
  37.3 1.3 %collective-permute-start.8 = (bf16[1152,512]{1,0:T(8,128)(2,1)S(1)}, bf16[1152,512]{1,0:T(8,128)(2,1)S(1)}, u32[]{:S(2)}, u32[]{:S(2)}) collective-permute-start(bf16[1152,512]{1,0:T(8,128)(2,1)S(1)} %collective-permute-done.3.refs_3_), channel_id=1, source_target_pairs={{0,1},{1,0},{2,3},{3,2},{4,5},{5,4},{6,7},{7,6},{8,9},{9,8},{10,11... | collective-permute-start | bytes 3538952 | tf_op jit(solution)/shard_map/ppermute | solution.py:301
  38.6 2.4 %collective-permute-start.7 = (bf16[1152,512]{1,0:T(8,128)(2,1)S(1)}, bf16[1152,512]{1,0:T(8,128)(2,1)S(1)}, u32[]{:S(2)}, u32[]{:S(2)}) collective-permute-start(bf16[1152,512]{1,0:T(8,128)(2,1)S(1)} %collective-permute-done.2), channel_id=1, source_target_pairs={{0,2},{1,7},{2,4},{3,1},{4,6},{5,3},{6,0},{7,5},{8,10},{9,15},{10,... | collective-permute-start | bytes 3538952 | tf_op jit(solution)/shard_map/ppermute | solution.py:314
  41.0 0.0 collective-permute-start.9
  41.0 3.4 %collective-permute-start.10 = (bf16[96,512]{1,0:T(8,128)(2,1)S(1)}, bf16[96,512]{1,0:T(8,128)(2,1)S(1)}, u32[]{:S(2)}, u32[]{:S(2)}) collective-permute-start(bf16[96,512]{1,0:T(8,128)(2,1)S(1)} %get-tuple-element.55.refs_4_), channel_id=1, source_target_pairs={{0,16},{1,17},{2,18},{3,19},{4,20},{5,21},{6,22},{7,23},{8,24},{9,... | collective-permute-start | bytes 294920 | tf_op jit(solution)/shard_map/ppermute | solution.py:301
  44.4 0.4 collective-permute-start.11
  44.9 1.4 %couple_low.1 = (bf16[512,512]{1,0:T(8,128)(2,1)S(1)}, bf16[256,512]{1,0:T(8,128)(2,1)S(1)}, bf16[128,512]{1,0:T(8,128)(2,1)S(1)}) custom-call(bf16[1600,512]{1,0:T(8,128)(2,1)S(1)} %collective-permute-done.refs_1_.refs_0_, bf16[448,512]{1,0:T(8,128)(2,1)S(1)} %collective-permute-done.4.refs_0_.refs_1_, ...), custom_call_target="tpu_custom_call" | custom-call | flops 1000000 | bytes 3866624 | tf_op jit(solution)/shard_map/couple_low/pallas_call | solution.py:68
  46.3 0.0 collective-permute-done.8.refs_2_
  46.3 2.5 %near_past.1 = (f32[1024,512]{1,0:T(8,128)S(1)}, f32[8,128]{1,0:T(8,128)S(1)}) custom-call(s32[1,4]{1,0:T(1,128)S(1)} %copy-done.3, bf16[64,1024]{1,0:T(8,128)(2,1)S(1)} %copy-done.2, bf16[1152,512]{1,0:T(8,128)(2,1)S(1)} %collective-permute-done.8.refs_2_, f32[1024,512]{1,0:T(8,128)S(1)} %get-tuple-element.50.refs_3_, ...), custom_call_target="tpu_custom_call" | custom-call | flops 16106127 | bytes 5509136 | tf_op jit(solution)/shard_map/near_past/pallas_call | solution.py:68
  48.8 1.4 %collective-permute-done.10.refs_1_ = bf16[96,512]{1,0:T(8,128)(2,1)S(1)} collective-permute-done((bf16[96,512]{1,0:T(8,128)(2,1)S(1)}, bf16[96,512]{1,0:T(8,128)(2,1)S(1)}, u32[]{:S(2)}, u32[]{:S(2)}) %collective-permute-start.10) | collective-permute-done | bytes 98336 | tf_op jit(solution)/shard_map/ppermute | solution.py:301
  50.2 1.8 %collective-permute-done.11.refs_2_ = bf16[96,512]{1,0:T(8,128)(2,1)S(1)} collective-permute-done((bf16[96,512]{1,0:T(8,128)(2,1)S(1)}, bf16[96,512]{1,0:T(8,128)(2,1)S(1)}, u32[]{:S(2)}, u32[]{:S(2)}) %collective-permute-start.11) | collective-permute-done | bytes 98336 | tf_op jit(solution)/shard_map/ppermute | solution.py:301
  52.0 0.0 collective-permute-done.9.refs_0_
  52.0 1.0 %couple_high.1 = (bf16[256,512]{1,0:T(8,128)(2,1)S(1)}, bf16[128,512]{1,0:T(8,128)(2,1)S(1)}) custom-call(bf16[128,512]{1,0:T(8,128)(2,1)S(1)} %collective-permute-done.9.refs_0_, bf16[96,512]{1,0:T(8,128)(2,1)S(1)} %collective-permute-done.10.refs_1_, bf16[96,512]{1,0:T(8,128)(2,1)S(1)} %collective-permute-done.11.refs_2_, ...), custom_call_target="tpu_custom_call" | custom-call | flops 1000000 | bytes 1081344 | tf_op jit(solution)/shard_map/couple_high/pallas_call | solution.py:68
  53.0 0.2 collective-permute-start.12
  53.2 1.5 %collective-permute-start.13 = (bf16[128,512]{1,0:T(8,128)(2,1)S(1)}, bf16[128,512]{1,0:T(8,128)(2,1)S(1)}, u32[]{:S(2)}, u32[]{:S(2)}) collective-permute-start(bf16[128,512]{1,0:T(8,128)(2,1)S(1)} %get-tuple-element.57.refs_4_), channel_id=1, source_target_pairs={{0,4},{1,5},{2,6},{3,7},{4,0},{5,1},{6,2},{7,3},{8,12},{9,13},{10,... | collective-permute-start | bytes 393224 | tf_op jit(solution)/shard_map/ppermute | solution.py:301
  54.8 2.2 %collective-permute-start.14 = (bf16[128,512]{1,0:T(8,128)(2,1)S(1)}, bf16[128,512]{1,0:T(8,128)(2,1)S(1)}, u32[]{:S(2)}, u32[]{:S(2)}) collective-permute-start(bf16[128,512]{1,0:T(8,128)(2,1)S(1)} %get-tuple-element.57.refs_4_), channel_id=1, source_target_pairs={{0,6},{1,7},{2,4},{3,5},{4,2},{5,3},{6,0},{7,1},{8,14},{9,15},{10,... | collective-permute-start | bytes 393224 | tf_op jit(solution)/shard_map/ppermute | solution.py:301
  56.9 0.0 collective-permute-done.7.refs_2_
  56.9 0.0 copy-start
  56.9 2.4 %near_second.1 = (f32[1024,512]{1,0:T(8,128)S(1)}, f32[8,128]{1,0:T(8,128)S(1)}) custom-call(s32[1,4]{1,0:T(1,128)S(1)} %copy-done.3, bf16[64,1024]{1,0:T(8,128)(2,1)S(1)} %copy-done.2, bf16[1152,512]{1,0:T(8,128)(2,1)S(1)} %collective-permute-done.7.refs_2_, f32[1024,512]{1,0:T(8,128)S(1)} %get-tuple-element.53.refs_3_, ...), custom_call_target="tpu_custom_call" | custom-call | flops 1610612736 | bytes 5509136 | tf_op jit(solution)/shard_map/near_second/pallas_call | solution.py:68
  59.3 5.1 %collective-permute-done.13.refs_3_ = bf16[128,512]{1,0:T(8,128)(2,1)S(1)} collective-permute-done((bf16[128,512]{1,0:T(8,128)(2,1)S(1)}, bf16[128,512]{1,0:T(8,128)(2,1)S(1)}, u32[]{:S(2)}, u32[]{:S(2)}) %collective-permute-start.13) | collective-permute-done | bytes 131104 | tf_op jit(solution)/shard_map/ppermute | solution.py:301
  64.4 0.0 collective-permute-done.14.refs_4_
  64.4 0.0 collective-permute-done.12.refs_2_
  64.4 0.1 half.1.refs_2_
  64.5 1.3 %collective-permute-start.15 = (bf16[1024,512]{1,0:T(8,128)(2,1)S(1)}, bf16[1024,512]{1,0:T(8,128)(2,1)S(1)}, u32[]{:S(2)}, u32[]{:S(2)}) collective-permute-start(bf16[1024,512]{1,0:T(8,128)(2,1)S(1)} %half.1.refs_2_), channel_id=1, source_target_pairs={{0,1},{1,0},{2,3},{3,2},{4,5},{5,4},{6,7},{7,6},{8,9},{9,8},{10,11... | collective-permute-start | bytes 3145736 | tf_op jit(solution)/shard_map/ppermute | solution.py:301
  65.7 0.0 copy-done
  65.7 1.9 %far.1 = (f32[512,512]{1,0:T(8,128)S(1)}, bf16[1024,256]{1,0:T(8,128)(2,1)S(1)}) custom-call(bf16[1,5,512,512]{3,2,1,0:T(8,128)(2,1)S(1)} %copy-done, bf16[512,512]{1,0:T(8,128)(2,1)S(1)} %get-tuple-element.59.refs_1_, bf16[1024,512]{1,0:T(8,128)(2,1)S(1)} %half.1.refs_2_, f32[1024,512]{1,0:T(8,128)S(1)} %get-tuple-element.58.refs_3_.refs_0_, ...), custom_call_target="tpu_custom_call" | custom-call | flops 1073741824 | bytes 8912896 | tf_op jit(solution)/shard_map/far/pallas_call | solution.py:68
  67.6 0.4 collective-permute-done.15.refs_4_
  68.0 2.4 %product.1 = bf16[1024,512]{1,0:T(8,128)(2,1)} custom-call(f32[1024,512]{1,0:T(8,128)S(1)} %get-tuple-element.58.refs_3_.refs_0_, bf16[1024,512]{1,0:T(8,128)(2,1)S(1)} %copy-done.1, bf16[1,5,512,512]{3,2,1,0:T(8,128)(2,1)S(1)} %copy-done, f32[512,512]{1,0:T(8,128)S(1)} %get-tuple-element.63.refs_3_, bf16[1024,512]{1,0:T(8,128)(2,1)S(1)} %collective-permute-done.15.refs_4_, ...), custom_call_target="tpu_custom_call" | custom-call | flops 805306368 | bytes 9437184 | tf_op jit(solution)/shard_map/product/pallas_call | solution.py:68
Async XLA Ops:
  0.0 5.1 %copy-start.4 = (s32[1,512]{1,0:T(1,128)S(1)}, s32[1,512]{1,0:T(1,128)}, u32[]{:S(2)}) copy-start(s32[1,512]{1,0:T(1,128)} %refs_2_.2) | copy-start | bytes 6148
  0.0 5.2 %copy-start.1 = (bf16[1024,512]{1,0:T(8,128)(2,1)S(1)}, bf16[1024,512]{1,0:T(8,128)(2,1)}, u32[]{:S(2)}) copy-start(bf16[1024,512]{1,0:T(8,128)(2,1)} %refs_1_.13) | copy-start | bytes 3145732
  1.3 12.6 %copy-start.2 = (bf16[64,1024]{1,0:T(8,128)(2,1)S(1)}, bf16[64,1024]{1,0:T(8,128)(2,1)}, u32[]{:S(2)}) copy-start(bf16[64,1024]{1,0:T(8,128)(2,1)} %refs_1_.12) | copy-start | bytes 393220
  1.4 12.6 %copy-start.3 = (s32[1,4]{1,0:T(1,128)S(1)}, s32[1,4]{1,0:T(1,128)}, u32[]{:S(2)}) copy-start(s32[1,4]{1,0:T(1,128)} %refs_0_.10) | copy-start | bytes 52
  1.4 15.0 %collective-permute-start.1 = (bf16[1152,512]{1,0:T(8,128)(2,1)S(1)}, bf16[1152,512]{1,0:T(8,128)(2,1)S(1)}, u32[]{:S(2)}, u32[]{:S(2)}) collective-permute-start(bf16[1152,512]{1,0:T(8,128)(2,1)S(1)} %pack.1.refs_0_.refs_2_), channel_id=1, source_target_pairs={{0,1},{1,0},{2,3},{3,2},{4,5},{5,4},{6,7},{7,6},{8,9},{9,8},{10,11... | collective-permute-start | bytes 3538952 | tf_op jit(solution)/shard_map/ppermute | solution.py:301
  2.1 21.4 %collective-permute-start.3 = (bf16[1152,512]{1,0:T(8,128)(2,1)S(1)}, bf16[1152,512]{1,0:T(8,128)(2,1)S(1)}, u32[]{:S(2)}, u32[]{:S(2)}) collective-permute-start(bf16[1152,512]{1,0:T(8,128)(2,1)S(1)} %pack.1.refs_0_.refs_2_), channel_id=1, source_target_pairs={{1,2},{2,1},{3,4},{4,3},{5,6},{6,5},{7,8},{8,7},{9,10},{10,9},{11,... | collective-permute-start | bytes 3538952 | tf_op jit(solution)/shard_map/ppermute | solution.py:305
  8.5 8.6 %collective-permute-start = (bf16[1600,512]{1,0:T(8,128)(2,1)S(1)}, bf16[1600,512]{1,0:T(8,128)(2,1)S(1)}, u32[]{:S(2)}, u32[]{:S(2)}) collective-permute-start(bf16[1600,512]{1,0:T(8,128)(2,1)S(1)} %get-tuple-element.36.refs_3_.refs_2_), channel_id=1, source_target_pairs={{0,1},{1,0},{2,3},{3,2},{4,5},{5,4},{6,7},{7,6},{8,9},{9,8},{10,11... | collective-permute-start | bytes 4915208 | tf_op jit(solution)/shard_map/ppermute | solution.py:301
  17.5 19.8 %collective-permute-start.2 = (bf16[1152,512]{1,0:T(8,128)(2,1)S(1)}, bf16[1152,512]{1,0:T(8,128)(2,1)S(1)}, u32[]{:S(2)}, u32[]{:S(2)}) collective-permute-start(bf16[1152,512]{1,0:T(8,128)(2,1)S(1)} %pack.1.refs_0_.refs_2_), channel_id=1, source_target_pairs={{0,0},{2,2},{3,3},{4,4},{5,5},{6,14},{7,7},{8,8},{9,1},{10,10},{11... | collective-permute-start | bytes 3538952 | tf_op jit(solution)/shard_map/ppermute | solution.py:310
  19.5 17.2 %collective-permute-start.4 = (bf16[448,512]{1,0:T(8,128)(2,1)S(1)}, bf16[448,512]{1,0:T(8,128)(2,1)S(1)}, u32[]{:S(2)}, u32[]{:S(2)}) collective-permute-start(bf16[448,512]{1,0:T(8,128)(2,1)S(1)} %get-tuple-element.40), channel_id=1, source_target_pairs={{0,2},{1,3},{2,0},{3,1},{4,6},{5,7},{6,4},{7,5},{8,10},{9,11},{10,... | collective-permute-start | bytes 1376264 | tf_op jit(solution)/shard_map/ppermute | solution.py:301
  19.6 17.1 %collective-permute-start.5 = (bf16[288,512]{1,0:T(8,128)(2,1)S(1)}, bf16[288,512]{1,0:T(8,128)(2,1)S(1)}, u32[]{:S(2)}, u32[]{:S(2)}) collective-permute-start(bf16[288,512]{1,0:T(8,128)(2,1)S(1)} %get-tuple-element.41), channel_id=1, source_target_pairs={{0,4},{1,5},{2,6},{3,7},{4,0},{5,1},{6,2},{7,3},{8,12},{9,13},{10,... | collective-permute-start | bytes 884744 | tf_op jit(solution)/shard_map/ppermute | solution.py:301
  19.7 17.1 %collective-permute-start.6 = (bf16[288,512]{1,0:T(8,128)(2,1)S(1)}, bf16[288,512]{1,0:T(8,128)(2,1)S(1)}, u32[]{:S(2)}, u32[]{:S(2)}) collective-permute-start(bf16[288,512]{1,0:T(8,128)(2,1)S(1)} %get-tuple-element.42), channel_id=1, source_target_pairs={{0,6},{1,7},{2,4},{3,5},{4,2},{5,3},{6,0},{7,1},{8,14},{9,15},{10,... | collective-permute-start | bytes 884744 | tf_op jit(solution)/shard_map/ppermute | solution.py:301
  37.3 9.0 %collective-permute-start.8 = (bf16[1152,512]{1,0:T(8,128)(2,1)S(1)}, bf16[1152,512]{1,0:T(8,128)(2,1)S(1)}, u32[]{:S(2)}, u32[]{:S(2)}) collective-permute-start(bf16[1152,512]{1,0:T(8,128)(2,1)S(1)} %collective-permute-done.3.refs_3_), channel_id=1, source_target_pairs={{0,1},{1,0},{2,3},{3,2},{4,5},{5,4},{6,7},{7,6},{8,9},{9,8},{10,11... | collective-permute-start | bytes 3538952 | tf_op jit(solution)/shard_map/ppermute | solution.py:301
  38.6 18.3 %collective-permute-start.7 = (bf16[1152,512]{1,0:T(8,128)(2,1)S(1)}, bf16[1152,512]{1,0:T(8,128)(2,1)S(1)}, u32[]{:S(2)}, u32[]{:S(2)}) collective-permute-start(bf16[1152,512]{1,0:T(8,128)(2,1)S(1)} %collective-permute-done.2), channel_id=1, source_target_pairs={{0,2},{1,7},{2,4},{3,1},{4,6},{5,3},{6,0},{7,5},{8,10},{9,15},{10,... | collective-permute-start | bytes 3538952 | tf_op jit(solution)/shard_map/ppermute | solution.py:314
  41.0 11.0 %collective-permute-start.9 = (bf16[128,512]{1,0:T(8,128)(2,1)S(1)}, bf16[128,512]{1,0:T(8,128)(2,1)S(1)}, u32[]{:S(2)}, u32[]{:S(2)}) collective-permute-start(bf16[128,512]{1,0:T(8,128)(2,1)S(1)} %get-tuple-element.54.refs_3_), channel_id=1, source_target_pairs={{0,8},{1,9},{2,10},{3,11},{4,12},{5,13},{6,14},{7,15},{8,0},{9,1},... | collective-permute-start | bytes 393224 | tf_op jit(solution)/shard_map/ppermute | solution.py:301
  41.0 9.1 %collective-permute-start.10 = (bf16[96,512]{1,0:T(8,128)(2,1)S(1)}, bf16[96,512]{1,0:T(8,128)(2,1)S(1)}, u32[]{:S(2)}, u32[]{:S(2)}) collective-permute-start(bf16[96,512]{1,0:T(8,128)(2,1)S(1)} %get-tuple-element.55.refs_4_), channel_id=1, source_target_pairs={{0,16},{1,17},{2,18},{3,19},{4,20},{5,21},{6,22},{7,23},{8,24},{9,... | collective-permute-start | bytes 294920 | tf_op jit(solution)/shard_map/ppermute | solution.py:301
  44.4 7.6 %collective-permute-start.11 = (bf16[96,512]{1,0:T(8,128)(2,1)S(1)}, bf16[96,512]{1,0:T(8,128)(2,1)S(1)}, u32[]{:S(2)}, u32[]{:S(2)}) collective-permute-start(bf16[96,512]{1,0:T(8,128)(2,1)S(1)} %get-tuple-element.55.refs_4_), channel_id=1, source_target_pairs={{0,24},{1,25},{2,26},{3,27},{4,28},{5,29},{6,30},{7,31},{8,16},{9,... | collective-permute-start | bytes 294920 | tf_op jit(solution)/shard_map/ppermute | solution.py:301
  53.0 11.4 %collective-permute-start.12 = (bf16[256,512]{1,0:T(8,128)(2,1)S(1)}, bf16[256,512]{1,0:T(8,128)(2,1)S(1)}, u32[]{:S(2)}, u32[]{:S(2)}) collective-permute-start(bf16[256,512]{1,0:T(8,128)(2,1)S(1)} %get-tuple-element.61.refs_1_), channel_id=1, source_target_pairs={{0,2},{1,3},{2,0},{3,1},{4,6},{5,7},{6,4},{7,5},{8,10},{9,11},{10,... | collective-permute-start | bytes 786440 | tf_op jit(solution)/shard_map/ppermute | solution.py:301
  53.2 11.2 %collective-permute-start.13 = (bf16[128,512]{1,0:T(8,128)(2,1)S(1)}, bf16[128,512]{1,0:T(8,128)(2,1)S(1)}, u32[]{:S(2)}, u32[]{:S(2)}) collective-permute-start(bf16[128,512]{1,0:T(8,128)(2,1)S(1)} %get-tuple-element.57.refs_4_), channel_id=1, source_target_pairs={{0,4},{1,5},{2,6},{3,7},{4,0},{5,1},{6,2},{7,3},{8,12},{9,13},{10,... | collective-permute-start | bytes 393224 | tf_op jit(solution)/shard_map/ppermute | solution.py:301
  54.8 9.6 %collective-permute-start.14 = (bf16[128,512]{1,0:T(8,128)(2,1)S(1)}, bf16[128,512]{1,0:T(8,128)(2,1)S(1)}, u32[]{:S(2)}, u32[]{:S(2)}) collective-permute-start(bf16[128,512]{1,0:T(8,128)(2,1)S(1)} %get-tuple-element.57.refs_4_), channel_id=1, source_target_pairs={{0,6},{1,7},{2,4},{3,5},{4,2},{5,3},{6,0},{7,1},{8,14},{9,15},{10,... | collective-permute-start | bytes 393224 | tf_op jit(solution)/shard_map/ppermute | solution.py:301
  56.9 8.8 %copy-start = (bf16[1,5,512,512]{3,2,1,0:T(8,128)(2,1)S(1)}, bf16[1,5,512,512]{3,2,1,0:T(8,128)(2,1)}, u32[]{:S(2)}) copy-start(bf16[1,5,512,512]{3,2,1,0:T(8,128)(2,1)} %refs_2_.3) | copy-start | bytes 7864324
  64.5 3.5 %collective-permute-start.15 = (bf16[1024,512]{1,0:T(8,128)(2,1)S(1)}, bf16[1024,512]{1,0:T(8,128)(2,1)S(1)}, u32[]{:S(2)}, u32[]{:S(2)}) collective-permute-start(bf16[1024,512]{1,0:T(8,128)(2,1)S(1)} %half.1.refs_2_), channel_id=1, source_target_pairs={{0,1},{1,0},{2,3},{3,2},{4,5},{5,4},{6,7},{7,6},{8,9},{9,8},{10,11... | collective-permute-start | bytes 3145736 | tf_op jit(solution)/shard_map/ppermute | solution.py:301

commit v6 on v5

--- a/solution.py
+++ b/solution.py
@@ -277,19 +277,18 @@
 def product_kernel(total, interp, transfers, begun, theirs, ready, product, out, done):
     core, _, _ = place()
     columns = columns_of(1 - core)
-    out[:, columns_of(core)] = ready[...]
+    block = total.shape[0] // 4
+    blocks = [slice(k * block, (k + 1) * block) for k in range(4)]
+    copies = start_all(
+        [
+            pltpu.make_async_copy(ready.at[rows, :], product.at[rows, columns_of(core)], done.at[k])
+            for k, rows in enumerate(blocks)
+        ]
+    )
     skeleton = with_levels(begun[:, columns], transfers, theirs).astype(BF16)
-    copies = []
-    block = total.shape[0] // 2
-    for k in range(2):
-        rows = slice(k * block, (k + 1) * block)
-        out[rows, columns] = (total[rows, columns] + dot(interp[rows, :], skeleton)).astype(BF16)
-        copies += start_all(
-            [
-                pltpu.make_async_copy(out.at[pl.ds(at, 128), :], product.at[pl.ds(at, 128), :], done.at[at // 128])
-                for at in range(k * block, (k + 1) * block, 128)
-            ]
-        )
+    for k, rows in enumerate(blocks):
+        out[rows, :] = (total[rows, columns] + dot(interp[rows, :], skeleton)).astype(BF16)
+        copies += start_all([pltpu.make_async_copy(out.at[rows, :], product.at[rows, columns], done.at[4 + k])])
     wait_all(copies)
 
 
@@ -413,7 +412,7 @@
         [((size, width), BF16)],
         [total, interp, transfers, far, theirs, ready],
         2 * 512 * 512 * (4 * 256 + 512),
-        scratch=[pltpu.VMEM((size, width), BF16), pltpu.SemaphoreType.DMA((size // 128,))],
+        scratch=[pltpu.VMEM((size, 256), BF16), pltpu.SemaphoreType.DMA((8,))],
         out_space=pltpu.HBM,
     )[0]
 

time: 70.8 us -> 70.7 us (level)
  no operation moved by 1% of the time
where the time goes in v6:
time: 70.7 us; the launch traced here: 70.5 us
  starting transfers between devices  28 us (40%)
  Pallas kernels  23.5 us (33%)
  waiting for transfers between devices  18.7 us (26%)
    pallas_call x13, Pallas kernels, call(): pl.pallas_call(reading, name=name, in_specs=specs, out_specs=[pl.BlockSpe...  23.5 us
    ppermute x13, starting transfers between devices, swap(): lax.ppermute(value, AXIS, [(leaf, leaf ^ mask) for leaf in range(leaves)])  20.5 us
    ppermute x13, waiting for transfers between devices, swap(): lax.ppermute(value, AXIS, [(leaf, leaf ^ mask) for leaf in range(leaves)])  18.7 us
    ppermute x1, starting transfers between devices, moved(): lax.ppermute(value, AXIS, [(a, b) for a, b in pairs if 0 <= b < leaves])  3.02 us
    ppermute x1, starting transfers between devices, turned(): return lax.ppermute(value, AXIS, pairs)  2.41 us
    ppermute x1, starting transfers between devices, staged_across_rows(): lax.ppermute(value, AXIS, [(a, b) for a, b in pairs if 0 <= b < leaves])  2.03 us
  transfers between devices with their start and end apart: 16, of which 6 were waited for; matrix products, arithmetic and copies ran while one was open for 0% of the time, Pallas kernels for 28%

profile of v6, /device:TPU:25, one launch (start us, length us, event | category | flops | bytes accessed | tf_op | source)
XLA Modules:
  0.0 70.5 jit_solution(15961565608437784265)
XLA Ops:
  0.0 0.0 copy-start.4
  0.0 0.0 copy-start.1
  0.0 1.3 %pack.1.refs_0_.refs_2_ = bf16[1152,512]{1,0:T(8,128)(2,1)S(1)} custom-call(bf16[64,1024]{1,0:T(8,128)(2,1)} %refs_1_.12, bf16[1024,512]{1,0:T(8,128)(2,1)} %refs_1_.7), custom_call_target="tpu_custom_call" | custom-call | bytes 2359296 | tf_op jit(solution)/shard_map/pack/pallas_call | solution.py:68
  1.3 0.0 copy-start.2
  1.4 0.0 copy-start.3
  1.4 0.8 %collective-permute-start.1 = (bf16[1152,512]{1,0:T(8,128)(2,1)S(1)}, bf16[1152,512]{1,0:T(8,128)(2,1)S(1)}, u32[]{:S(2)}, u32[]{:S(2)}) collective-permute-start(bf16[1152,512]{1,0:T(8,128)(2,1)S(1)} %pack.1.refs_0_.refs_2_), channel_id=1, source_target_pairs={{0,1},{1,0},{2,3},{3,2},{4,5},{5,4},{6,7},{7,6},{8,9},{9,8},{10,11... | collective-permute-start | bytes 3538952 | tf_op jit(solution)/shard_map/ppermute | solution.py:300
  2.1 3.0 %collective-permute-start.3 = (bf16[1152,512]{1,0:T(8,128)(2,1)S(1)}, bf16[1152,512]{1,0:T(8,128)(2,1)S(1)}, u32[]{:S(2)}, u32[]{:S(2)}) collective-permute-start(bf16[1152,512]{1,0:T(8,128)(2,1)S(1)} %pack.1.refs_0_.refs_2_), channel_id=1, source_target_pairs={{1,2},{2,1},{3,4},{4,3},{5,6},{6,5},{7,8},{8,7},{9,10},{10,9},{11,... | collective-permute-start | bytes 3538952 | tf_op jit(solution)/shard_map/ppermute | solution.py:304
  5.1 0.0 copy-done.4
  5.2 0.0 copy-done.1
  5.2 3.3 %terms.1 = (bf16[1600,512]{1,0:T(8,128)(2,1)S(1)}, f32[1024,512]{1,0:T(8,128)S(1)}) custom-call(bf16[1152,512]{1,0:T(8,128)(2,1)S(1)} %pack.1.refs_0_.refs_2_, bf16[1024,512]{1,0:T(8,128)(2,1)S(1)} %copy-done.1, s32[1,512]{1,0:T(1,128)S(1)} %copy-done.4, bf16[1,5,512,512]{3,2,1,0:T(8,128)(2,1)} %refs_2_.3), custom_call_target="tpu_custom_call" | custom-call | flops 1879048192 | bytes 8587264 | tf_op jit(solution)/shard_map/terms/pallas_call | solution.py:68
  8.5 5.5 %collective-permute-start = (bf16[1600,512]{1,0:T(8,128)(2,1)S(1)}, bf16[1600,512]{1,0:T(8,128)(2,1)S(1)}, u32[]{:S(2)}, u32[]{:S(2)}) collective-permute-start(bf16[1600,512]{1,0:T(8,128)(2,1)S(1)} %get-tuple-element.36.refs_3_.refs_2_), channel_id=1, source_target_pairs={{0,1},{1,0},{2,3},{3,2},{4,5},{5,4},{6,7},{7,6},{8,9},{9,8},{10,11... | collective-permute-start | bytes 4915208 | tf_op jit(solution)/shard_map/ppermute | solution.py:300
  14.0 0.0 copy-done.2
  14.0 0.0 copy-done.3
  14.0 2.4 %near_self.1 = (f32[1024,512]{1,0:T(8,128)S(1)}, f32[8,128]{1,0:T(8,128)S(1)}) custom-call(s32[1,4]{1,0:T(1,128)S(1)} %copy-done.3, bf16[64,1024]{1,0:T(8,128)(2,1)S(1)} %copy-done.2, bf16[1152,512]{1,0:T(8,128)(2,1)S(1)} %pack.1.refs_0_.refs_2_, bf16[1600,512]{1,0:T(8,128)(2,1)S(1)} %get-tuple-element.36.refs_3_.refs_2_), custom_call_target="tpu_custom_call" | custom-call | flops 32212254720 | bytes 3411984 | tf_op jit(solution)/shard_map/near_self/pallas_call | solution.py:68
  16.4 0.0 collective-permute-done.1.refs_4_.refs_2_
  16.4 0.7 %collective-permute-done.refs_1_.refs_0_ = bf16[1600,512]{1,0:T(8,128)(2,1)S(1)} collective-permute-done((bf16[1600,512]{1,0:T(8,128)(2,1)S(1)}, bf16[1600,512]{1,0:T(8,128)(2,1)S(1)}, u32[]{:S(2)}, u32[]{:S(2)}) %collective-permute-start) | collective-permute-done | bytes 1638432 | tf_op jit(solution)/shard_map/ppermute | solution.py:300
  17.1 0.4 chip.1
  17.5 2.0 %collective-permute-start.2 = (bf16[1152,512]{1,0:T(8,128)(2,1)S(1)}, bf16[1152,512]{1,0:T(8,128)(2,1)S(1)}, u32[]{:S(2)}, u32[]{:S(2)}) collective-permute-start(bf16[1152,512]{1,0:T(8,128)(2,1)S(1)} %pack.1.refs_0_.refs_2_), channel_id=1, source_target_pairs={{0,0},{2,2},{3,3},{4,4},{5,5},{6,14},{7,7},{8,8},{9,1},{10,10},{11... | collective-permute-start | bytes 3538952 | tf_op jit(solution)/shard_map/ppermute | solution.py:309
  19.5 0.1 collective-permute-start.4
  19.6 0.1 collective-permute-start.5
  19.7 3.8 %collective-permute-start.6 = (bf16[288,512]{1,0:T(8,128)(2,1)S(1)}, bf16[288,512]{1,0:T(8,128)(2,1)S(1)}, u32[]{:S(2)}, u32[]{:S(2)}) collective-permute-start(bf16[288,512]{1,0:T(8,128)(2,1)S(1)} %get-tuple-element.42), channel_id=1, source_target_pairs={{0,6},{1,7},{2,4},{3,5},{4,2},{5,3},{6,0},{7,1},{8,14},{9,15},{10,... | collective-permute-start | bytes 884744 | tf_op jit(solution)/shard_map/ppermute | solution.py:300
  23.5 0.0 collective-permute-done.3.refs_3_
  23.5 4.1 %near_one.1 = (f32[1024,512]{1,0:T(8,128)S(1)}, f32[8,128]{1,0:T(8,128)S(1)}) custom-call(s32[1,4]{1,0:T(1,128)S(1)} %copy-done.3, bf16[64,1024]{1,0:T(8,128)(2,1)S(1)} %copy-done.2, bf16[1152,512]{1,0:T(8,128)(2,1)S(1)} %collective-permute-done.1.refs_4_.refs_2_, bf16[1152,512]{1,0:T(8,128)(2,1)S(1)} %collective-permute-done.3.refs_3_, ...), custom_call_target="tpu_custom_call" | custom-call | flops 3221225472 | bytes 6688784 | tf_op jit(solution)/shard_map/near_one/pallas_call | solution.py:68
  27.5 9.2 %collective-permute-done.5.refs_1_.refs_2_ = bf16[288,512]{1,0:T(8,128)(2,1)S(1)} collective-permute-done((bf16[288,512]{1,0:T(8,128)(2,1)S(1)}, bf16[288,512]{1,0:T(8,128)(2,1)S(1)}, u32[]{:S(2)}, u32[]{:S(2)}) %collective-permute-start.5) | collective-permute-done | bytes 294944 | tf_op jit(solution)/shard_map/ppermute | solution.py:300
  36.8 0.0 collective-permute-done.6.refs_2_.refs_3_
  36.8 0.0 collective-permute-done.4.refs_0_.refs_1_
  36.8 0.5 row.1
  37.3 0.0 collective-permute-done.2
  37.3 1.3 %collective-permute-start.8 = (bf16[1152,512]{1,0:T(8,128)(2,1)S(1)}, bf16[1152,512]{1,0:T(8,128)(2,1)S(1)}, u32[]{:S(2)}, u32[]{:S(2)}) collective-permute-start(bf16[1152,512]{1,0:T(8,128)(2,1)S(1)} %collective-permute-done.3.refs_3_), channel_id=1, source_target_pairs={{0,1},{1,0},{2,3},{3,2},{4,5},{5,4},{6,7},{7,6},{8,9},{9,8},{10,11... | collective-permute-start | bytes 3538952 | tf_op jit(solution)/shard_map/ppermute | solution.py:300
  38.6 2.4 %collective-permute-start.7 = (bf16[1152,512]{1,0:T(8,128)(2,1)S(1)}, bf16[1152,512]{1,0:T(8,128)(2,1)S(1)}, u32[]{:S(2)}, u32[]{:S(2)}) collective-permute-start(bf16[1152,512]{1,0:T(8,128)(2,1)S(1)} %collective-permute-done.2), channel_id=1, source_target_pairs={{0,2},{1,7},{2,4},{3,1},{4,6},{5,3},{6,0},{7,5},{8,10},{9,15},{10,... | collective-permute-start | bytes 3538952 | tf_op jit(solution)/shard_map/ppermute | solution.py:313
  41.0 0.0 collective-permute-start.9
  41.0 3.4 %collective-permute-start.10 = (bf16[96,512]{1,0:T(8,128)(2,1)S(1)}, bf16[96,512]{1,0:T(8,128)(2,1)S(1)}, u32[]{:S(2)}, u32[]{:S(2)}) collective-permute-start(bf16[96,512]{1,0:T(8,128)(2,1)S(1)} %get-tuple-element.55.refs_4_), channel_id=1, source_target_pairs={{0,16},{1,17},{2,18},{3,19},{4,20},{5,21},{6,22},{7,23},{8,24},{9,... | collective-permute-start | bytes 294920 | tf_op jit(solution)/shard_map/ppermute | solution.py:300
  44.4 0.4 collective-permute-start.11
  44.9 1.4 %couple_low.1 = (bf16[512,512]{1,0:T(8,128)(2,1)S(1)}, bf16[256,512]{1,0:T(8,128)(2,1)S(1)}, bf16[128,512]{1,0:T(8,128)(2,1)S(1)}) custom-call(bf16[1600,512]{1,0:T(8,128)(2,1)S(1)} %collective-permute-done.refs_1_.refs_0_, bf16[448,512]{1,0:T(8,128)(2,1)S(1)} %collective-permute-done.4.refs_0_.refs_1_, ...), custom_call_target="tpu_custom_call" | custom-call | flops 1000000 | bytes 3866624 | tf_op jit(solution)/shard_map/couple_low/pallas_call | solution.py:68
  46.3 0.0 collective-permute-done.8.refs_2_
  46.3 2.5 %near_past.1 = (f32[1024,512]{1,0:T(8,128)S(1)}, f32[8,128]{1,0:T(8,128)S(1)}) custom-call(s32[1,4]{1,0:T(1,128)S(1)} %copy-done.3, bf16[64,1024]{1,0:T(8,128)(2,1)S(1)} %copy-done.2, bf16[1152,512]{1,0:T(8,128)(2,1)S(1)} %collective-permute-done.8.refs_2_, f32[1024,512]{1,0:T(8,128)S(1)} %get-tuple-element.50.refs_3_, ...), custom_call_target="tpu_custom_call" | custom-call | flops 16106127 | bytes 5509136 | tf_op jit(solution)/shard_map/near_past/pallas_call | solution.py:68
  48.8 1.4 %collective-permute-done.10.refs_1_ = bf16[96,512]{1,0:T(8,128)(2,1)S(1)} collective-permute-done((bf16[96,512]{1,0:T(8,128)(2,1)S(1)}, bf16[96,512]{1,0:T(8,128)(2,1)S(1)}, u32[]{:S(2)}, u32[]{:S(2)}) %collective-permute-start.10) | collective-permute-done | bytes 98336 | tf_op jit(solution)/shard_map/ppermute | solution.py:300
  50.2 1.8 %collective-permute-done.11.refs_2_ = bf16[96,512]{1,0:T(8,128)(2,1)S(1)} collective-permute-done((bf16[96,512]{1,0:T(8,128)(2,1)S(1)}, bf16[96,512]{1,0:T(8,128)(2,1)S(1)}, u32[]{:S(2)}, u32[]{:S(2)}) %collective-permute-start.11) | collective-permute-done | bytes 98336 | tf_op jit(solution)/shard_map/ppermute | solution.py:300
  52.0 0.0 collective-permute-done.9.refs_0_
  52.0 1.0 %couple_high.1 = (bf16[256,512]{1,0:T(8,128)(2,1)S(1)}, bf16[128,512]{1,0:T(8,128)(2,1)S(1)}) custom-call(bf16[128,512]{1,0:T(8,128)(2,1)S(1)} %collective-permute-done.9.refs_0_, bf16[96,512]{1,0:T(8,128)(2,1)S(1)} %collective-permute-done.10.refs_1_, bf16[96,512]{1,0:T(8,128)(2,1)S(1)} %collective-permute-done.11.refs_2_, ...), custom_call_target="tpu_custom_call" | custom-call | flops 1000000 | bytes 1081344 | tf_op jit(solution)/shard_map/couple_high/pallas_call | solution.py:68
  53.0 0.2 collective-permute-start.12
  53.2 1.5 %collective-permute-start.13 = (bf16[128,512]{1,0:T(8,128)(2,1)S(1)}, bf16[128,512]{1,0:T(8,128)(2,1)S(1)}, u32[]{:S(2)}, u32[]{:S(2)}) collective-permute-start(bf16[128,512]{1,0:T(8,128)(2,1)S(1)} %get-tuple-element.57.refs_4_), channel_id=1, source_target_pairs={{0,4},{1,5},{2,6},{3,7},{4,0},{5,1},{6,2},{7,3},{8,12},{9,13},{10,... | collective-permute-start | bytes 393224 | tf_op jit(solution)/shard_map/ppermute | solution.py:300
  54.8 2.2 %collective-permute-start.14 = (bf16[128,512]{1,0:T(8,128)(2,1)S(1)}, bf16[128,512]{1,0:T(8,128)(2,1)S(1)}, u32[]{:S(2)}, u32[]{:S(2)}) collective-permute-start(bf16[128,512]{1,0:T(8,128)(2,1)S(1)} %get-tuple-element.57.refs_4_), channel_id=1, source_target_pairs={{0,6},{1,7},{2,4},{3,5},{4,2},{5,3},{6,0},{7,1},{8,14},{9,15},{10,... | collective-permute-start | bytes 393224 | tf_op jit(solution)/shard_map/ppermute | solution.py:300
  56.9 0.0 collective-permute-done.7.refs_2_
  56.9 0.0 copy-start
  56.9 2.4 %near_second.1 = (f32[1024,512]{1,0:T(8,128)S(1)}, f32[8,128]{1,0:T(8,128)S(1)}) custom-call(s32[1,4]{1,0:T(1,128)S(1)} %copy-done.3, bf16[64,1024]{1,0:T(8,128)(2,1)S(1)} %copy-done.2, bf16[1152,512]{1,0:T(8,128)(2,1)S(1)} %collective-permute-done.7.refs_2_, f32[1024,512]{1,0:T(8,128)S(1)} %get-tuple-element.53.refs_3_, ...), custom_call_target="tpu_custom_call" | custom-call | flops 1610612736 | bytes 5509136 | tf_op jit(solution)/shard_map/near_second/pallas_call | solution.py:68
  59.3 5.1 %collective-permute-done.13.refs_3_ = bf16[128,512]{1,0:T(8,128)(2,1)S(1)} collective-permute-done((bf16[128,512]{1,0:T(8,128)(2,1)S(1)}, bf16[128,512]{1,0:T(8,128)(2,1)S(1)}, u32[]{:S(2)}, u32[]{:S(2)}) %collective-permute-start.13) | collective-permute-done | bytes 131104 | tf_op jit(solution)/shard_map/ppermute | solution.py:300
  64.4 0.0 collective-permute-done.14.refs_4_
  64.4 0.0 collective-permute-done.12.refs_2_
  64.4 0.1 half.1.refs_2_
  64.5 1.3 %collective-permute-start.15 = (bf16[1024,512]{1,0:T(8,128)(2,1)S(1)}, bf16[1024,512]{1,0:T(8,128)(2,1)S(1)}, u32[]{:S(2)}, u32[]{:S(2)}) collective-permute-start(bf16[1024,512]{1,0:T(8,128)(2,1)S(1)} %half.1.refs_2_), channel_id=1, source_target_pairs={{0,1},{1,0},{2,3},{3,2},{4,5},{5,4},{6,7},{7,6},{8,9},{9,8},{10,11... | collective-permute-start | bytes 3145736 | tf_op jit(solution)/shard_map/ppermute | solution.py:300
  65.7 0.0 copy-done
  65.7 1.9 %far.1 = (f32[512,512]{1,0:T(8,128)S(1)}, bf16[1024,256]{1,0:T(8,128)(2,1)S(1)}) custom-call(bf16[1,5,512,512]{3,2,1,0:T(8,128)(2,1)S(1)} %copy-done, bf16[512,512]{1,0:T(8,128)(2,1)S(1)} %get-tuple-element.59.refs_1_, bf16[1024,512]{1,0:T(8,128)(2,1)S(1)} %half.1.refs_2_, f32[1024,512]{1,0:T(8,128)S(1)} %get-tuple-element.58.refs_3_.refs_0_, ...), custom_call_target="tpu_custom_call" | custom-call | flops 1073741824 | bytes 8912896 | tf_op jit(solution)/shard_map/far/pallas_call | solution.py:68
  67.6 0.4 collective-permute-done.15.refs_4_
  68.0 2.3 %product.1 = bf16[1024,512]{1,0:T(8,128)(2,1)} custom-call(f32[1024,512]{1,0:T(8,128)S(1)} %get-tuple-element.58.refs_3_.refs_0_, bf16[1024,512]{1,0:T(8,128)(2,1)S(1)} %copy-done.1, bf16[1,5,512,512]{3,2,1,0:T(8,128)(2,1)S(1)} %copy-done, f32[512,512]{1,0:T(8,128)S(1)} %get-tuple-element.63.refs_3_, bf16[1024,512]{1,0:T(8,128)(2,1)S(1)} %collective-permute-done.15.refs_4_, ...), custom_call_target="tpu_custom_call" | custom-call | flops 805306368 | bytes 9437184 | tf_op jit(solution)/shard_map/product/pallas_call | solution.py:68
Async XLA Ops:
  0.0 5.1 %copy-start.4 = (s32[1,512]{1,0:T(1,128)S(1)}, s32[1,512]{1,0:T(1,128)}, u32[]{:S(2)}) copy-start(s32[1,512]{1,0:T(1,128)} %refs_2_.2) | copy-start | bytes 6148
  0.0 5.2 %copy-start.1 = (bf16[1024,512]{1,0:T(8,128)(2,1)S(1)}, bf16[1024,512]{1,0:T(8,128)(2,1)}, u32[]{:S(2)}) copy-start(bf16[1024,512]{1,0:T(8,128)(2,1)} %refs_1_.13) | copy-start | bytes 3145732
  1.3 12.6 %copy-start.2 = (bf16[64,1024]{1,0:T(8,128)(2,1)S(1)}, bf16[64,1024]{1,0:T(8,128)(2,1)}, u32[]{:S(2)}) copy-start(bf16[64,1024]{1,0:T(8,128)(2,1)} %refs_1_.12) | copy-start | bytes 393220
  1.4 12.6 %copy-start.3 = (s32[1,4]{1,0:T(1,128)S(1)}, s32[1,4]{1,0:T(1,128)}, u32[]{:S(2)}) copy-start(s32[1,4]{1,0:T(1,128)} %refs_0_.10) | copy-start | bytes 52
  1.4 15.0 %collective-permute-start.1 = (bf16[1152,512]{1,0:T(8,128)(2,1)S(1)}, bf16[1152,512]{1,0:T(8,128)(2,1)S(1)}, u32[]{:S(2)}, u32[]{:S(2)}) collective-permute-start(bf16[1152,512]{1,0:T(8,128)(2,1)S(1)} %pack.1.refs_0_.refs_2_), channel_id=1, source_target_pairs={{0,1},{1,0},{2,3},{3,2},{4,5},{5,4},{6,7},{7,6},{8,9},{9,8},{10,11... | collective-permute-start | bytes 3538952 | tf_op jit(solution)/shard_map/ppermute | solution.py:300
  2.1 21.4 %collective-permute-start.3 = (bf16[1152,512]{1,0:T(8,128)(2,1)S(1)}, bf16[1152,512]{1,0:T(8,128)(2,1)S(1)}, u32[]{:S(2)}, u32[]{:S(2)}) collective-permute-start(bf16[1152,512]{1,0:T(8,128)(2,1)S(1)} %pack.1.refs_0_.refs_2_), channel_id=1, source_target_pairs={{1,2},{2,1},{3,4},{4,3},{5,6},{6,5},{7,8},{8,7},{9,10},{10,9},{11,... | collective-permute-start | bytes 3538952 | tf_op jit(solution)/shard_map/ppermute | solution.py:304
  8.5 8.6 %collective-permute-start = (bf16[1600,512]{1,0:T(8,128)(2,1)S(1)}, bf16[1600,512]{1,0:T(8,128)(2,1)S(1)}, u32[]{:S(2)}, u32[]{:S(2)}) collective-permute-start(bf16[1600,512]{1,0:T(8,128)(2,1)S(1)} %get-tuple-element.36.refs_3_.refs_2_), channel_id=1, source_target_pairs={{0,1},{1,0},{2,3},{3,2},{4,5},{5,4},{6,7},{7,6},{8,9},{9,8},{10,11... | collective-permute-start | bytes 4915208 | tf_op jit(solution)/shard_map/ppermute | solution.py:300
  17.5 19.8 %collective-permute-start.2 = (bf16[1152,512]{1,0:T(8,128)(2,1)S(1)}, bf16[1152,512]{1,0:T(8,128)(2,1)S(1)}, u32[]{:S(2)}, u32[]{:S(2)}) collective-permute-start(bf16[1152,512]{1,0:T(8,128)(2,1)S(1)} %pack.1.refs_0_.refs_2_), channel_id=1, source_target_pairs={{0,0},{2,2},{3,3},{4,4},{5,5},{6,14},{7,7},{8,8},{9,1},{10,10},{11... | collective-permute-start | bytes 3538952 | tf_op jit(solution)/shard_map/ppermute | solution.py:309
  19.5 17.2 %collective-permute-start.4 = (bf16[448,512]{1,0:T(8,128)(2,1)S(1)}, bf16[448,512]{1,0:T(8,128)(2,1)S(1)}, u32[]{:S(2)}, u32[]{:S(2)}) collective-permute-start(bf16[448,512]{1,0:T(8,128)(2,1)S(1)} %get-tuple-element.40), channel_id=1, source_target_pairs={{0,2},{1,3},{2,0},{3,1},{4,6},{5,7},{6,4},{7,5},{8,10},{9,11},{10,... | collective-permute-start | bytes 1376264 | tf_op jit(solution)/shard_map/ppermute | solution.py:300
  19.6 17.1 %collective-permute-start.5 = (bf16[288,512]{1,0:T(8,128)(2,1)S(1)}, bf16[288,512]{1,0:T(8,128)(2,1)S(1)}, u32[]{:S(2)}, u32[]{:S(2)}) collective-permute-start(bf16[288,512]{1,0:T(8,128)(2,1)S(1)} %get-tuple-element.41), channel_id=1, source_target_pairs={{0,4},{1,5},{2,6},{3,7},{4,0},{5,1},{6,2},{7,3},{8,12},{9,13},{10,... | collective-permute-start | bytes 884744 | tf_op jit(solution)/shard_map/ppermute | solution.py:300
  19.7 17.1 %collective-permute-start.6 = (bf16[288,512]{1,0:T(8,128)(2,1)S(1)}, bf16[288,512]{1,0:T(8,128)(2,1)S(1)}, u32[]{:S(2)}, u32[]{:S(2)}) collective-permute-start(bf16[288,512]{1,0:T(8,128)(2,1)S(1)} %get-tuple-element.42), channel_id=1, source_target_pairs={{0,6},{1,7},{2,4},{3,5},{4,2},{5,3},{6,0},{7,1},{8,14},{9,15},{10,... | collective-permute-start | bytes 884744 | tf_op jit(solution)/shard_map/ppermute | solution.py:300
  37.3 9.0 %collective-permute-start.8 = (bf16[1152,512]{1,0:T(8,128)(2,1)S(1)}, bf16[1152,512]{1,0:T(8,128)(2,1)S(1)}, u32[]{:S(2)}, u32[]{:S(2)}) collective-permute-start(bf16[1152,512]{1,0:T(8,128)(2,1)S(1)} %collective-permute-done.3.refs_3_), channel_id=1, source_target_pairs={{0,1},{1,0},{2,3},{3,2},{4,5},{5,4},{6,7},{7,6},{8,9},{9,8},{10,11... | collective-permute-start | bytes 3538952 | tf_op jit(solution)/shard_map/ppermute | solution.py:300
  38.6 18.3 %collective-permute-start.7 = (bf16[1152,512]{1,0:T(8,128)(2,1)S(1)}, bf16[1152,512]{1,0:T(8,128)(2,1)S(1)}, u32[]{:S(2)}, u32[]{:S(2)}) collective-permute-start(bf16[1152,512]{1,0:T(8,128)(2,1)S(1)} %collective-permute-done.2), channel_id=1, source_target_pairs={{0,2},{1,7},{2,4},{3,1},{4,6},{5,3},{6,0},{7,5},{8,10},{9,15},{10,... | collective-permute-start | bytes 3538952 | tf_op jit(solution)/shard_map/ppermute | solution.py:313
  41.0 11.0 %collective-permute-start.9 = (bf16[128,512]{1,0:T(8,128)(2,1)S(1)}, bf16[128,512]{1,0:T(8,128)(2,1)S(1)}, u32[]{:S(2)}, u32[]{:S(2)}) collective-permute-start(bf16[128,512]{1,0:T(8,128)(2,1)S(1)} %get-tuple-element.54.refs_3_), channel_id=1, source_target_pairs={{0,8},{1,9},{2,10},{3,11},{4,12},{5,13},{6,14},{7,15},{8,0},{9,1},... | collective-permute-start | bytes 393224 | tf_op jit(solution)/shard_map/ppermute | solution.py:300
  41.0 9.1 %collective-permute-start.10 = (bf16[96,512]{1,0:T(8,128)(2,1)S(1)}, bf16[96,512]{1,0:T(8,128)(2,1)S(1)}, u32[]{:S(2)}, u32[]{:S(2)}) collective-permute-start(bf16[96,512]{1,0:T(8,128)(2,1)S(1)} %get-tuple-element.55.refs_4_), channel_id=1, source_target_pairs={{0,16},{1,17},{2,18},{3,19},{4,20},{5,21},{6,22},{7,23},{8,24},{9,... | collective-permute-start | bytes 294920 | tf_op jit(solution)/shard_map/ppermute | solution.py:300
  44.4 7.6 %collective-permute-start.11 = (bf16[96,512]{1,0:T(8,128)(2,1)S(1)}, bf16[96,512]{1,0:T(8,128)(2,1)S(1)}, u32[]{:S(2)}, u32[]{:S(2)}) collective-permute-start(bf16[96,512]{1,0:T(8,128)(2,1)S(1)} %get-tuple-element.55.refs_4_), channel_id=1, source_target_pairs={{0,24},{1,25},{2,26},{3,27},{4,28},{5,29},{6,30},{7,31},{8,16},{9,... | collective-permute-start | bytes 294920 | tf_op jit(solution)/shard_map/ppermute | solution.py:300
  53.0 11.4 %collective-permute-start.12 = (bf16[256,512]{1,0:T(8,128)(2,1)S(1)}, bf16[256,512]{1,0:T(8,128)(2,1)S(1)}, u32[]{:S(2)}, u32[]{:S(2)}) collective-permute-start(bf16[256,512]{1,0:T(8,128)(2,1)S(1)} %get-tuple-element.61.refs_1_), channel_id=1, source_target_pairs={{0,2},{1,3},{2,0},{3,1},{4,6},{5,7},{6,4},{7,5},{8,10},{9,11},{10,... | collective-permute-start | bytes 786440 | tf_op jit(solution)/shard_map/ppermute | solution.py:300
  53.2 11.2 %collective-permute-start.13 = (bf16[128,512]{1,0:T(8,128)(2,1)S(1)}, bf16[128,512]{1,0:T(8,128)(2,1)S(1)}, u32[]{:S(2)}, u32[]{:S(2)}) collective-permute-start(bf16[128,512]{1,0:T(8,128)(2,1)S(1)} %get-tuple-element.57.refs_4_), channel_id=1, source_target_pairs={{0,4},{1,5},{2,6},{3,7},{4,0},{5,1},{6,2},{7,3},{8,12},{9,13},{10,... | collective-permute-start | bytes 393224 | tf_op jit(solution)/shard_map/ppermute | solution.py:300
  54.8 9.6 %collective-permute-start.14 = (bf16[128,512]{1,0:T(8,128)(2,1)S(1)}, bf16[128,512]{1,0:T(8,128)(2,1)S(1)}, u32[]{:S(2)}, u32[]{:S(2)}) collective-permute-start(bf16[128,512]{1,0:T(8,128)(2,1)S(1)} %get-tuple-element.57.refs_4_), channel_id=1, source_target_pairs={{0,6},{1,7},{2,4},{3,5},{4,2},{5,3},{6,0},{7,1},{8,14},{9,15},{10,... | collective-permute-start | bytes 393224 | tf_op jit(solution)/shard_map/ppermute | solution.py:300
  56.9 8.8 %copy-start = (bf16[1,5,512,512]{3,2,1,0:T(8,128)(2,1)S(1)}, bf16[1,5,512,512]{3,2,1,0:T(8,128)(2,1)}, u32[]{:S(2)}) copy-start(bf16[1,5,512,512]{3,2,1,0:T(8,128)(2,1)} %refs_2_.3) | copy-start | bytes 7864324
  64.5 3.5 %collective-permute-start.15 = (bf16[1024,512]{1,0:T(8,128)(2,1)S(1)}, bf16[1024,512]{1,0:T(8,128)(2,1)S(1)}, u32[]{:S(2)}, u32[]{:S(2)}) collective-permute-start(bf16[1024,512]{1,0:T(8,128)(2,1)S(1)} %half.1.refs_2_), channel_id=1, source_target_pairs={{0,1},{1,0},{2,3},{3,2},{4,5},{5,4},{6,7},{7,6},{8,9},{9,8},{10,11... | collective-permute-start | bytes 3145736 | tf_op jit(solution)/shard_map/ppermute | solution.py:300
